TPU v7x, 32 devices: a whole 2x2x4 slice. The times are simulated.
32 devices in a mesh: groups: 2 (over x), wide: 16 (over z, y, core).
Axes of the slice: x: 2, y: 2, z: 4, core: 2. Of those that a mesh axis runs over, the one named last changes fastest.
Arguments:
- features: bfloat16 [4096, 512], P(('groups', 'wide')), parts along dimension 0, may hold values from -3.5 to 3.5
- centres: bfloat16 [8192, 512], P(('groups', 'wide')), parts along dimension 0, may hold values from -3.5 to 3.5
- targets: bfloat16 [4096, 128], P(('groups', 'wide')), parts along dimension 0, may hold values from -8 to 8
- coefficients: float32 [8192, 128], P(('groups', 'wide')), parts along dimension 0, may hold values from -1.6 to 1.6
- momentum: float32 [8192, 128], P(('groups', 'wide')), parts along dimension 0, may hold values from -0.8 to 0.8
- block_inverse: float32 [32, 256, 256], P(('groups', 'wide')), parts along dimension 0, may hold values from -3 to 3
Outputs:
- residual: float32 [4096, 128], P(('groups', 'wide')), parts along dimension 0
- new_momentum: float32 [8192, 128], P(('groups', 'wide')), parts along dimension 0
- new_coefficients: float32 [8192, 128], P(('groups', 'wide')), parts along dimension 0
There are 2 independent parts, one for each index of `groups`. A program takes and returns all parts, laid end to end along the dimension named above; each array names one. Nothing has to cross between parts.
All inputs are finite; a program needn't handle non-finite values.
Results may differ from a plain program's by a relative error of at most 0.0033.
Values may be sent and summed in bfloat16 or wider, within the bound.
No kernel may reach another device: no remote copies, remote signals or barrier semaphores. Data moves between devices by JAX's collectives and lax.ppermute only.
A program may use at most 128 MiB of HBM per device.

v0:
```python
import jax
import jax.numpy as jnp
from jax import lax
from jax.sharding import PartitionSpec as P


def shards(features, centres, targets, coefficients, momentum, block_inverse):
    width = features.shape[1]
    centre_norms = jnp.sum(centres.astype(jnp.float32) ** 2, axis=1)
    shard_rows = lax.all_gather(features, "wide", axis=0, tiled=True)
    row_norms = jnp.sum(shard_rows.astype(jnp.float32) ** 2, axis=1)
    products = jnp.dot(shard_rows, centres.T, preferred_element_type=jnp.float32)
    kernel = jnp.exp(
        (2.0 * products - row_norms[:, None] - centre_norms[None, :]) * (2.0 / width)
    ).astype(jnp.bfloat16)
    batch_size = kernel.shape[0]
    coef_half = coefficients.astype(jnp.bfloat16)
    prediction = lax.psum_scatter(
        jnp.dot(kernel, coef_half, preferred_element_type=jnp.float32),
        "wide",
        scatter_dimension=0,
        tiled=True,
    )
    residual = prediction - targets.astype(jnp.float32)
    residual_half = lax.all_gather(residual.astype(jnp.bfloat16), "wide", axis=0, tiled=True)
    gradient = lax.dot_general(
        kernel, residual_half, (((0,), (0,)), ((), ())), preferred_element_type=jnp.float32
    )
    nblocks = block_inverse.shape[0]
    order = block_inverse.shape[1]
    grad_blocks = gradient.reshape(nblocks, order, gradient.shape[1])
    conditioned = jnp.einsum(
        "bij,bjk->bik", block_inverse, grad_blocks, precision=lax.Precision.HIGHEST
    )
    new_momentum = 0.9 * momentum + conditioned.reshape(gradient.shape) / batch_size
    new_coefficients = coefficients - 0.5 * new_momentum
    return (residual, new_momentum, new_coefficients)


def solution(mesh):
    in_specs = (
        P(("groups", "wide"), None),
        P(("groups", "wide"), None),
        P(("groups", "wide"), None),
        P(("groups", "wide"), None),
        P(("groups", "wide"), None),
        P(("groups", "wide"), None, None),
    )
    out_specs = (
        P(("groups", "wide"), None),
        P(("groups", "wide"), None),
        P(("groups", "wide"), None),
    )
    return jax.shard_map(shards, mesh=mesh, in_specs=in_specs, out_specs=out_specs, check_vma=False)
```

profile of v0, /device:TPU:0, one launch (start us, length us, event | category | flops | bytes accessed | tf_op | source)
XLA Modules:
  0.0 146.8 jit_solution(18435210653149370365)
XLA Ops:
  7.2 0.0 copy-start
  7.2 0.0 copy-start.3
  7.2 0.0 all-gather.2.cloned.1.call-start
  7.2 0.7 all-gather.2.cloned.1.call-update
  7.9 0.0 reduce-scatter.2.cloned.1.call-start
  8.0 1.1 multiply_reduce_fusion.1
  9.1 45.3 %all-gather.2.cloned.1.call-done = bf16[2048,512]{1,0:T(8,128)(2,1)} async-done(((bf16[128,512]{1,0:T(8,128)(2,1)}), bf16[2048,512]{1,0:T(8,128)(2,1)}) %all-gather.2.cloned.1.call-update) | async-done | bytes 2097168 | tf_op jit(solution)/shard_map/all_gather | solution.py:10
  54.3 0.0 copy-start.1
  54.3 2.2 %multiply_reduce_fusion = f32[2048]{0:T(1024)S(1)} fusion(bf16[2048,512]{1,0:T(8,128)(2,1)} %all-gather.2.cloned.1.call-done), kind=kLoop, calls=%fused_computation | loop fusion | flops 3143680 | bytes 2105344 | tf_op jit(solution)/shard_map/reduce_sum | solution.py:11
  56.5 0.0 copy-done.3
  56.6 0.0 copy-done.1
  56.6 0.0 copy-start.2
  56.6 0.7 fusion.4
  57.3 0.1 copy-done.2
  57.5 0.0 copy-start.4
  57.5 0.0 copy-start.5
  57.5 1.4 fusion.8
  58.9 0.0 reduce-scatter.2.cloned.1.call-update
  58.9 0.1 copy.10
  59.0 0.0 copy-done.4
  59.0 0.1 copy.9
  59.1 56.1 %reduce-scatter.2.cloned.1.call-done = f32[128,128]{1,0:T(8,128)} async-done(((f32[2048,128]{1,0:T(8,128)}), f32[128,128]{1,0:T(8,128)}) %reduce-scatter.2.cloned.1.call-update) | async-done | bytes 65552 | tf_op jit(solution)/shard_map/reduce_scatter | solution.py:18
  115.2 0.0 copy-done.5
  115.2 1.5 %fusion.10 = (bf16[128,128]{1,0:T(8,128)(2,1)S(1)}, f32[128,128]{1,0:T(8,128)}) fusion(f32[128,128]{1,0:T(8,128)} %reduce-scatter.2.cloned.1.call-done, bf16[128,128]{1,0:T(8,128)(2,1)S(1)} %copy-done.5), kind=kLoop, calls=%fused_computation.16 | loop fusion | flops 49152 | bytes 196608 | tf_op jit(solution)/shard_map/convert_element_type | solution.py:25
  116.7 20.8 %all_gather.7 = bf16[2048,128]{1,0:T(8,128)(2,1)S(1)} all-gather(bf16[128,128]{1,0:T(8,128)(2,1)S(1)} %get-tuple-element.6), channel_id=1, replica_groups=mesh['groups'=2,'wide'=16] {'wide'}, dimensions={0}, use_global_device_ids=true | all-gather | bytes 557056 | tf_op jit(solution)/shard_map/all_gather | solution.py:25
  137.5 0.5 fusion.11
  138.0 0.0 copy-done
  138.0 0.4 multiply_subtract_fusion
  138.4 0.8 copy.12
  139.2 0.8 copy.11
Async XLA Ops:
  7.2 130.9 %copy-start = (f32[1,256,256]{2,1,0:T(8,128)S(1)}, f32[1,256,256]{2,1,0:T(8,128)}, u32[]{:S(2)}) copy-start(f32[1,256,256]{2,1,0:T(8,128)} %param.11) | copy-start | bytes 786436
  7.2 49.4 %copy-start.3 = (bf16[256,512]{1,0:T(8,128)(2,1)S(1)}, bf16[256,512]{1,0:T(8,128)(2,1)}, u32[]{:S(2)}) copy-start(bf16[256,512]{1,0:T(8,128)(2,1)} %param.7) | copy-start | bytes 786436
  7.2 47.1 %all-gather.2.cloned.1.call-start = ((), (), s32[]{:S(2)}) async-start(), calls=%async_computation.1 | async-start | bytes 2228224 | tf_op jit(solution)/shard_map/all_gather | solution.py:10
  7.9 107.3 %reduce-scatter.2.cloned.1.call-start = ((), (), s32[]{:S(2)}) async-start(), calls=%async_computation.2 | async-start | bytes 1114112 | tf_op jit(solution)/shard_map/reduce_scatter | solution.py:18
  54.3 2.2 %copy-start.1 = (bf16[2048,512]{1,0:T(8,128)(2,1)S(1)}, bf16[2048,512]{1,0:T(8,128)(2,1)}, u32[]{:S(2)}) copy-start(bf16[2048,512]{1,0:T(8,128)(2,1)} %all-gather.2.cloned.1.call-done) | copy-start | bytes 6291460
  56.6 0.9 copy-start.2
  57.5 1.5 %copy-start.4 = (f32[256,128]{1,0:T(8,128)S(1)}, f32[256,128]{1,0:T(8,128)}, u32[]{:S(2)}) copy-start(f32[256,128]{1,0:T(8,128)} %param.10) | copy-start | bytes 393220
  57.5 57.8 %copy-start.5 = (bf16[128,128]{1,0:T(8,128)(2,1)S(1)}, bf16[128,128]{1,0:T(8,128)(2,1)}, u32[]{:S(2)}) copy-start(bf16[128,128]{1,0:T(8,128)(2,1)} %param.8) | copy-start | bytes 98308
Sparse Core Ops, SparseCore 0:
  10.2 44.0 all-gather.1
  59.0 56.1 reduce-scatter.1
where the time goes:
time: 147 us
  waiting for transfers between devices  102 us (69%)
  blocking collectives  20.8 us (14%)
  between operations  14.1 us (10%)
  other arithmetic  4.78 us (3%)
  matrix products  3.03 us (2%)
  local copies, waits for them, and re-layouts  1.87 us (1%)
    reduce_scatter x1, waiting for transfers between devices, shards(): lax.psum_scatter(jnp.dot(kernel, coef_half, preferred_element_type=jnp.fl...  56.1 us
    all_gather x1, waiting for transfers between devices, shards(): shard_rows = lax.all_gather(features, 'wide', axis=0, tiled=True)  45.3 us
    all_gather x1, blocking collectives, shards(): lax.all_gather(residual.astype(jnp.bfloat16), 'wide', axis=0, tiled=True)  20.8 us
  transfers between devices with their start and end apart: 2, of which 2 were waited for; matrix products, arithmetic and copies ran while one was open for 1% of the time, Pallas kernels for 0%

commit v1 on v0

v1 whole, which is shorter than its diff:
```python
import functools

import jax
import jax.numpy as jnp
from jax import lax
from jax.experimental import pallas as pl
from jax.experimental.pallas import tpu as pltpu
from jax.sharding import PartitionSpec as P


F32, BF16 = jnp.float32, jnp.bfloat16
MIB = 1 << 20


def swap(x, mask, size):
    return lax.ppermute(x, "wide", [(i, i ^ mask) for i in range(size)])


def masks_of(bits):
    masks = [0]
    for bit in bits:
        masks += [m ^ bit for m in masks]
    return masks


def digits_of(bits):
    return [bits[i : i + 2] for i in range(0, len(bits), 2)]


def gather_pieces(x, digits, size):
    pieces = [x]
    for digit in digits:
        whole = pieces[0] if len(pieces) == 1 else jnp.concatenate(pieces)
        pieces = [whole] + [swap(whole, m, size) for m in masks_of(digit)[1:]]
    return pieces


def nbytes(*arrays):
    return sum(a.size * a.dtype.itemsize for a in arrays)


def whole_call(body, outs, args, scratch=(), flops=0):
    moved = nbytes(*args, *outs)
    return pl.pallas_call(
        body,
        out_shape=outs,
        in_specs=[pl.BlockSpec(memory_space=pltpu.VMEM)] * len(args),
        out_specs=[pl.BlockSpec(memory_space=pltpu.VMEM)] * len(outs),
        scratch_shapes=scratch,
        compiler_params=pltpu.CompilerParams(vmem_limit_bytes=moved + 12 * MIB),
        cost_estimate=pl.CostEstimate(flops=flops, bytes_accessed=moved, transcendentals=0),
    )(*args)


def predict_body(nrow, ncen, first, *refs):
    rows, refs = refs[:nrow], refs[nrow:]
    centres, refs = refs[:ncen], refs[ncen:]
    coefs, refs = refs[:ncen], refs[ncen:]
    given, refs = (refs[:1], refs[1:]) if first else (refs[:nrow], refs[nrow:])
    kernel_ref, sums = refs[0], refs[1:]
    width = rows[0].shape[1]
    order = centres[0].shape[0]
    chunk = 128
    norms = []
    ones = jnp.ones((8, width), BF16)
    for c in centres:
        square = c[...].astype(F32) ** 2
        high = square.astype(BF16)
        low = (square - high.astype(F32)).astype(BF16)
        dims = (((1,), (1,)), ((), ()))
        norm = lax.dot_general(ones, high, dims, preferred_element_type=F32)
        norm += lax.dot_general(ones, low, dims, preferred_element_type=F32)
        norms.append(norm[:1])
    base = 0
    for piece in range(nrow):
        count = rows[piece].shape[0] // chunk

        def step(i, base=base, piece=piece):
            at = pl.ds(i * chunk, chunk)
            x = rows[piece][at, :]
            row_norms = jnp.sum(x.astype(F32) ** 2, axis=1, keepdims=True)
            if not first:
                total = given[piece][at, :]
            elif piece == 0:
                total = jnp.where(i == 0, -1.0, 0.0) * given[0][...].astype(F32)
            else:
                total = jnp.zeros((chunk, sums[0].shape[1]), F32)
            for j in range(ncen):
                products = lax.dot_general(x, centres[j][...], (((1,), (1,)), ((), ())), preferred_element_type=F32)
                k = jnp.exp((2.0 * products - row_norms - norms[j]) * (2.0 / width)).astype(BF16)
                kernel_ref[pl.ds(base + i * chunk, chunk), j * order : (j + 1) * order] = k
                total += jnp.dot(k, coefs[j][...], preferred_element_type=F32)
            sums[piece][at, :] = total

        if count == 1:
            step(0)
        else:
            pl.loop(0, count)(step)
        base += count * chunk


def predict(rows, centres, coefs, given, first):
    total = sum(x.shape[0] for x in rows)
    depth = sum(c.shape[0] for c in centres)
    outs = [jax.ShapeDtypeStruct((total, depth), BF16)]
    outs += [jax.ShapeDtypeStruct((x.shape[0], coefs[0].shape[1]), F32) for x in rows]
    body = functools.partial(predict_body, len(rows), len(centres), first)
    flops = 2 * total * depth * (rows[0].shape[1] + coefs[0].shape[1])
    kernel, *sums = whole_call(body, outs, [*rows, *centres, *coefs, *given], flops=flops)
    return kernel, sums


def gradient_body(nker, npiece, *refs):
    kernels, refs = refs[:nker], refs[nker:]
    pieces, refs = refs[:npiece], refs[npiece:]
    keep, give, residual = refs
    base = 0
    for piece in pieces:
        residual[base : base + piece.shape[0], :] = piece[...]
        base += piece.shape[0]
    chunk = min(512, base)
    for n, kernel in enumerate(kernels):
        half = kernel.shape[1] // 2
        for side, out in ((0, keep), (1, give)):
            at = pl.ds(n * half, half)
            columns = slice(side * half, (side + 1) * half)

            def term(i, columns=columns, kernel=kernel):
                return lax.dot_general(
                    kernel[pl.ds(i * chunk, chunk), columns],
                    residual[pl.ds(i * chunk, chunk), :],
                    (((0,), (0,)), ((), ())),
                    preferred_element_type=F32,
                )

            out[at, :] = term(0)
            if base > chunk:

                @pl.loop(1, base // chunk)
                def _(i, out=out, at=at, term=term):
                    out[at, :] += term(i)


def gradients(kernels, pieces):
    total = kernels[0].shape[0]
    columns = pieces[0].shape[1]
    depth = sum(k.shape[1] for k in kernels)
    out = jax.ShapeDtypeStruct((depth // 2, columns), F32)
    body = functools.partial(gradient_body, len(kernels), len(pieces))
    return whole_call(
        body,
        [out, out],
        [*kernels, *pieces],
        scratch=[pltpu.VMEM((total, columns), BF16)],
        flops=2 * total * depth * columns,
    )


def update_body(batch, keep, arrived, inverse, momentum, coefficients, new_momentum, new_coefficients):
    gradient = keep[...] + arrived[...]
    nblocks, order = inverse.shape[0], inverse.shape[1]
    for b in range(nblocks):
        at = slice(b * order, (b + 1) * order)
        conditioned = jnp.dot(
            inverse[b], gradient[at], precision=lax.Precision.HIGHEST, preferred_element_type=F32
        )
        moved = 0.9 * momentum[at, :] + conditioned / batch
        new_momentum[at, :] = moved
        new_coefficients[at, :] = coefficients[at, :] - 0.5 * moved


def shards(size, features, centres, targets, coefficients, momentum, block_inverse):
    batch = features.shape[0] * size
    count = centres.shape[0]
    core, far = 1, size // 2
    digits = digits_of([1 << b for b in range(1, size.bit_length() - 2)])
    send = functools.partial(swap, size=size)

    coef_half = coefficients.astype(BF16)
    far_centres, far_coef = send(centres, far), send(coef_half, far)
    rows = gather_pieces(features, digits, size)
    near = [centres, send(centres, core)]
    near_coef = [coef_half, send(coef_half, core)]
    kernel_near, sums = predict(rows, near, near_coef, [targets], True)
    far_centres, far_coef, sums = lax.optimization_barrier((far_centres, far_coef, sums))
    distant = [far_centres, send(far_centres, core)]
    distant_coef = [far_coef, send(far_coef, core)]
    kernel_far, sums = predict(rows, distant, distant_coef, sums, False)

    for digit in reversed(digits):
        masks = masks_of(digit)
        if len(sums) == 1:
            sums = jnp.split(sums[0], len(masks))
        total = sums[0]
        for m, part in zip(masks[1:], sums[1:]):
            total = total + send(part, m)
        sums = [total]
    residual = sums[0]
    residuals = gather_pieces(residual.astype(BF16), digits, size)

    keep, give = gradients([kernel_near, kernel_far], residuals)
    both = keep + send(give, core)
    arrived = send(both[count:], far)
    out = jax.ShapeDtypeStruct(momentum.shape, F32)
    new_momentum, new_coefficients = whole_call(
        functools.partial(update_body, batch),
        [out, out],
        [both[:count], arrived, block_inverse, momentum, coefficients],
    )
    return residual, new_momentum, new_coefficients


def solution(mesh):
    one = P(("groups", "wide"), None)
    in_specs = (one, one, one, one, one, P(("groups", "wide"), None, None))
    return jax.shard_map(
        functools.partial(shards, mesh.shape["wide"]),
        mesh=mesh,
        in_specs=in_specs,
        out_specs=(one, one, one),
        check_vma=False,
    )
```

time: 147 us -> 54.7 us (0.37)
  waiting for transfers between devices: 102 us -> 23.5 us
  starting transfers between devices: 0.08 us -> 21.8 us
  blocking collectives: 20.8 us -> 0 us
  between operations: 14.1 us -> 0.77 us
  Pallas kernels: 0 us -> 5.83 us
  other arithmetic: 4.78 us -> 1.59 us
  matrix products: 3.03 us -> 0 us
    reduce_scatter x1 -> x0, waiting for transfers between devices: 56.1 us -> none  [shards(): lax.psum_scatter(jnp.dot(kernel, coef_half, preferred_element_type=jnp.fl...]
    all_gather x1 -> x0, waiting for transfers between devices: 45.3 us -> none  [shards(): shard_rows = lax.all_gather(features, 'wide', axis=0, tiled=True)]
    ppermute x0 -> x17, waiting for transfers between devices: none -> 23.5 us  [swap(): return lax.ppermute(x, 'wide', [(i, i ^ mask) for i in range(size)])]
    ppermute x0 -> x17, starting transfers between devices: none -> 21.8 us  [swap(): return lax.ppermute(x, 'wide', [(i, i ^ mask) for i in range(size)])]
    all_gather x1 -> x0, blocking collectives: 20.8 us -> none  [shards(): lax.all_gather(residual.astype(jnp.bfloat16), 'wide', axis=0, tiled=True)]
    pallas_call x0 -> x4, Pallas kernels: none -> 5.83 us  [whole_call(): pl.pallas_call(body, out_shape=outs, in_specs=[pl.BlockSpec(memory_space=...]
    reduce_sum x2 -> x0, other arithmetic: 3.3 us -> none  [the longest x1 2.22 us: shards(): row_norms = jnp.sum(shard_rows.astype(jnp.float32) ** 2, axis=1)]
    dot_general x4 -> x0, matrix products: 3.03 us -> none  [the longest x1 1.41 us: shards(): jnp.dot(kernel, coef_half, preferred_element_type=jnp.float32)]
  transfers between devices with their start and end apart: 2 -> 17, of which waited for: 2 -> 10; matrix products, arithmetic and copies ran while one was open for 1% -> 2% of each run, Pallas kernels for 0% -> 3%
where the time goes in v1:
time: 54.7 us; the launch traced here: 54.5 us
  waiting for transfers between devices  23.5 us (43%)
  starting transfers between devices  21.8 us (40%)
  Pallas kernels  5.83 us (11%)
  other arithmetic  1.59 us (3%)
  local copies, waits for them, and re-layouts  0.99 us (2%)
  between operations  0.77 us (1%)
    ppermute x17, waiting for transfers between devices, swap(): return lax.ppermute(x, 'wide', [(i, i ^ mask) for i in range(size)])  23.5 us
    ppermute x17, starting transfers between devices, swap(): return lax.ppermute(x, 'wide', [(i, i ^ mask) for i in range(size)])  21.8 us
    pallas_call x4, Pallas kernels, whole_call(): pl.pallas_call(body, out_shape=outs, in_specs=[pl.BlockSpec(memory_space=...  5.83 us
  transfers between devices with their start and end apart: 17, of which 10 were waited for; matrix products, arithmetic and copies ran while one was open for 2% of the time, Pallas kernels for 3%

profile of v1, /device:TPU:0, one launch (start us, length us, event | category | flops | bytes accessed | tf_op | source)
XLA Modules:
  0.0 54.5 jit_solution(5344276139903098317)
XLA Ops:
  0.6 0.5 collective-permute-start.5
  1.2 3.7 %collective-permute-start.3 = (bf16[256,512]{1,0:T(8,128)(2,1)}, bf16[256,512]{1,0:T(8,128)(2,1)S(1)}, u32[]{:S(2)}, u32[]{:S(2)}) collective-permute-start(bf16[256,512]{1,0:T(8,128)(2,1)} %refs_4_.1), channel_id=1, source_target_pairs={{0,8},{1,9},{2,10},{3,11},{4,12},{5,13},{6,14},{7,15},{8,0},{9,1},... | collective-permute-start | bytes 786440 | tf_op jit(solution)/shard_map/ppermute | solution.py:16
  4.8 0.9 %convert_element_type.6.refs_6_ = bf16[256,128]{1,0:T(8,128)(2,1)S(1)} convert(f32[256,128]{1,0:T(8,128)} %coefficients.1) | non-fusion elementwise | flops 32768 | bytes 196608 | tf_op jit(solution)/shard_map/convert_element_type | solution.py:179
  5.7 0.2 collective-permute-start.6
  5.9 2.5 %collective-permute-start.2 = (bf16[128,512]{1,0:T(8,128)(2,1)S(1)}, bf16[128,512]{1,0:T(8,128)(2,1)S(1)}, u32[]{:S(2)}, u32[]{:S(2)}) collective-permute-start(bf16[128,512]{1,0:T(8,128)(2,1)S(1)} %copy-done.3), channel_id=1, source_target_pairs={{0,6},{1,7},{2,4},{3,5},{4,2},{5,3},{6,0},{7,1},{8,14},{9,15},{10,... | collective-permute-start | bytes 393224 | tf_op jit(solution)/shard_map/ppermute | solution.py:16
  8.4 0.4 collective-permute-start.1
  8.9 0.5 collective-permute-start
  9.4 5.2 %collective-permute-done.2.refs_3_ = bf16[128,512]{1,0:T(8,128)(2,1)S(1)} collective-permute-done((bf16[128,512]{1,0:T(8,128)(2,1)S(1)}, bf16[128,512]{1,0:T(8,128)(2,1)S(1)}, u32[]{:S(2)}, u32[]{:S(2)}) %collective-permute-start.2) | collective-permute-done | bytes 131104 | tf_op jit(solution)/shard_map/ppermute | solution.py:16
  14.6 3.3 %collective-permute-start.4 = (bf16[256,128]{1,0:T(8,128)(2,1)S(1)}, bf16[256,128]{1,0:T(8,128)(2,1)S(1)}, u32[]{:S(2)}, u32[]{:S(2)}) collective-permute-start(bf16[256,128]{1,0:T(8,128)(2,1)S(1)} %convert_element_type.6.refs_6_), channel_id=1, source_target_pairs={{0,8},{1,9},{2,10},{3,11},{4,12},{5,13},{6,14},{7,15},{8,0},{9,1},... | collective-permute-start | bytes 196616 | tf_op jit(solution)/shard_map/ppermute | solution.py:16
  17.8 3.4 %collective-permute-done.1.refs_2_ = bf16[128,512]{1,0:T(8,128)(2,1)S(1)} collective-permute-done((bf16[128,512]{1,0:T(8,128)(2,1)S(1)}, bf16[128,512]{1,0:T(8,128)(2,1)S(1)}, u32[]{:S(2)}, u32[]{:S(2)}) %collective-permute-start.1) | collective-permute-done | bytes 131104 | tf_op jit(solution)/shard_map/ppermute | solution.py:16
  21.3 0.9 %copy-done.4 = bf16[256,512]{1,0:T(8,128)(2,1)S(1)} copy-done((bf16[256,512]{1,0:T(8,128)(2,1)S(1)}, bf16[256,512]{1,0:T(8,128)(2,1)}, u32[]{:S(2)}) %copy-start.4) | copy-done | bytes 262168
  22.3 1.8 %shard_map.85 = (bf16[512,512]{1,0:T(8,128)(2,1)S(1)}, f32[128,128]{1,0:T(8,128)S(1)}, f32[128,128]{1,0:T(8,128)S(1)}, f32[128,128]{1,0:T(8,128)S(1)}, f32[128,128]{1,0:T(8,128)S(1)}) custom-call(bf16[128,512]{1,0:T(8,128)(2,1)S(1)} %copy-done.3, bf16[128,512]{1,0:T(8,128)(2,1)S(1)} %collective-permute-done.refs_1_, ...), custom_call_target="tpu_custom_call" | custom-call | flops 335544320 | bytes 1998848 | tf_op jit(solution)/shard_map/pallas_call | solution.py:44
  24.1 0.1 collective-permute-start.7
  24.2 0.5 collective-permute-start.8
  24.7 1.1 %collective-permute-done.8.refs_7_ = bf16[256,128]{1,0:T(8,128)(2,1)S(1)} collective-permute-done((bf16[256,128]{1,0:T(8,128)(2,1)S(1)}, bf16[256,128]{1,0:T(8,128)(2,1)S(1)}, u32[]{:S(2)}, u32[]{:S(2)}) %collective-permute-start.8) | collective-permute-done | bytes 65568 | tf_op jit(solution)/shard_map/ppermute | solution.py:16
  25.8 2.5 %shard_map.86 = (bf16[512,512]{1,0:T(8,128)(2,1)S(1)}, f32[128,128]{1,0:T(8,128)S(1)}, f32[128,128]{1,0:T(8,128)S(1)}, f32[128,128]{1,0:T(8,128)S(1)}, f32[128,128]{1,0:T(8,128)S(1)}) custom-call(bf16[128,512]{1,0:T(8,128)(2,1)S(1)} %copy-done.3, bf16[128,512]{1,0:T(8,128)(2,1)S(1)} %collective-permute-done.refs_1_, ...), custom_call_target="tpu_custom_call" | custom-call | flops 335544320 | bytes 2228224 | tf_op jit(solution)/shard_map/pallas_call | solution.py:44
  28.3 0.1 collective-permute-start.9
  28.4 3.4 %collective-permute-start.11 = (f32[128,128]{1,0:T(8,128)S(1)}, f32[128,128]{1,0:T(8,128)S(1)}, u32[]{:S(2)}, u32[]{:S(2)}) collective-permute-start(f32[128,128]{1,0:T(8,128)S(1)} %get-tuple-element.36), channel_id=1, source_target_pairs={{0,6},{1,7},{2,4},{3,5},{4,2},{5,3},{6,0},{7,1},{8,14},{9,15},{10,... | collective-permute-start | bytes 196616 | tf_op jit(solution)/shard_map/ppermute | solution.py:16
  31.8 0.8 %collective-permute-done.9 = f32[128,128]{1,0:T(8,128)S(1)} collective-permute-done((f32[128,128]{1,0:T(8,128)S(1)}, f32[128,128]{1,0:T(8,128)S(1)}, u32[]{:S(2)}, u32[]{:S(2)}) %collective-permute-start.9) | collective-permute-done | bytes 65568 | tf_op jit(solution)/shard_map/ppermute | solution.py:16
  32.6 0.5 collective-permute-done.10
  33.1 1.9 %collective-permute-done.11 = f32[128,128]{1,0:T(8,128)S(1)} collective-permute-done((f32[128,128]{1,0:T(8,128)S(1)}, f32[128,128]{1,0:T(8,128)S(1)}, u32[]{:S(2)}, u32[]{:S(2)}) %collective-permute-start.11) | collective-permute-done | bytes 65568 | tf_op jit(solution)/shard_map/ppermute | solution.py:16
  35.0 0.6 %fusion = (bf16[128,128]{1,0:T(8,128)(2,1)S(1)}, f32[128,128]{1,0:T(8,128)}) fusion(f32[128,128]{1,0:T(8,128)S(1)} %collective-permute-done.11, f32[128,128]{1,0:T(8,128)S(1)} %collective-permute-done.10, f32[128,128]{1,0:T(8,128)S(1)} %get-tuple-element.33, f32[128,128]{1,0:T(8,128)S(1)} %collective-permute-done.9), kind=kLoop, calls=%fused_computation.1 | loop fusion | flops 65536 | bytes 360448 | tf_op jit(solution)/shard_map/convert_element_type | solution.py:199
  35.7 1.9 %collective-permute-start.14 = (bf16[128,128]{1,0:T(8,128)(2,1)S(1)}, bf16[128,128]{1,0:T(8,128)(2,1)S(1)}, u32[]{:S(2)}, u32[]{:S(2)}) collective-permute-start(bf16[128,128]{1,0:T(8,128)(2,1)S(1)} %get-tuple-element.43.refs_2_), channel_id=1, source_target_pairs={{0,6},{1,7},{2,4},{3,5},{4,2},{5,3},{6,0},{7,1},{8,14},{9,15},{10,... | collective-permute-start | bytes 98312 | tf_op jit(solution)/shard_map/ppermute | solution.py:16
  37.6 1.5 %collective-permute-start.12 = (bf16[128,128]{1,0:T(8,128)(2,1)S(1)}, bf16[128,128]{1,0:T(8,128)(2,1)S(1)}, u32[]{:S(2)}, u32[]{:S(2)}) collective-permute-start(bf16[128,128]{1,0:T(8,128)(2,1)S(1)} %get-tuple-element.43.refs_2_), channel_id=1, source_target_pairs={{0,2},{1,3},{2,0},{3,1},{4,6},{5,7},{6,4},{7,5},{8,10},{9,11},{10,... | collective-permute-start | bytes 98312 | tf_op jit(solution)/shard_map/ppermute | solution.py:16
  39.2 1.3 %collective-permute-done.14.refs_5_ = bf16[128,128]{1,0:T(8,128)(2,1)S(1)} collective-permute-done((bf16[128,128]{1,0:T(8,128)(2,1)S(1)}, bf16[128,128]{1,0:T(8,128)(2,1)S(1)}, u32[]{:S(2)}, u32[]{:S(2)}) %collective-permute-start.14) | collective-permute-done | bytes 32800 | tf_op jit(solution)/shard_map/ppermute | solution.py:16
  40.5 1.0 %collective-permute-done.13.refs_4_ = bf16[128,128]{1,0:T(8,128)(2,1)S(1)} collective-permute-done((bf16[128,128]{1,0:T(8,128)(2,1)S(1)}, bf16[128,128]{1,0:T(8,128)(2,1)S(1)}, u32[]{:S(2)}, u32[]{:S(2)}) %collective-permute-start.13) | collective-permute-done | bytes 32800 | tf_op jit(solution)/shard_map/ppermute | solution.py:16
  41.6 0.5 shard_map.87
  42.1 0.1 collective-permute-start.15
  42.1 1.5 %collective-permute-done.15 = f32[512,128]{1,0:T(8,128)S(1)} collective-permute-done((f32[512,128]{1,0:T(8,128)S(1)}, f32[512,128]{1,0:T(8,128)S(1)}, u32[]{:S(2)}, u32[]{:S(2)}) %collective-permute-start.15) | collective-permute-done | bytes 262176 | tf_op jit(solution)/shard_map/ppermute | solution.py:16
  43.8 3.0 %collective-permute-start.16 = (f32[256,128]{1,0:T(8,128)S(1)}, f32[256,128]{1,0:T(8,128)S(1)}, u32[]{:S(2)}, u32[]{:S(2)}) collective-permute-start(f32[256,128]{1,0:T(8,128)S(1)} %get-tuple-element.45), channel_id=1, source_target_pairs={{0,8},{1,9},{2,10},{3,11},{4,12},{5,13},{6,14},{7,15},{8,0},{9,1},... | collective-permute-start | bytes 393224 | tf_op jit(solution)/shard_map/ppermute | solution.py:16
  46.8 6.6 %collective-permute-done.16.arrived = f32[256,128]{1,0:T(8,128)S(1)} collective-permute-done((f32[256,128]{1,0:T(8,128)S(1)}, f32[256,128]{1,0:T(8,128)S(1)}, u32[]{:S(2)}, u32[]{:S(2)}) %collective-permute-start.16) | collective-permute-done | bytes 131104 | tf_op jit(solution)/shard_map/ppermute | solution.py:16
  53.4 1.1 %shard_map.88 = (f32[256,128]{1,0:T(8,128)}, f32[256,128]{1,0:T(8,128)}) custom-call(f32[256,128]{1,0:T(8,128)S(1)} %get-tuple-element.46.keep, f32[256,128]{1,0:T(8,128)S(1)} %collective-permute-done.16.arrived, f32[1,256,256]{2,1,0:T(8,128)S(1)} %copy-done.1, f32[256,128]{1,0:T(8,128)S(1)} %copy-done.2, f32[256,128]{1,0:T(8,128)S(1)} %copy-done), custom_call_target="tpu_custom_call" | custom-call | bytes 1048576 | tf_op jit(solution)/shard_map/pallas_call | solution.py:44
  (22 shorter events, 0.2 us)
Async XLA Ops:
  0.6 5.3 %copy-start.3 = (bf16[128,512]{1,0:T(8,128)(2,1)S(1)}, bf16[128,512]{1,0:T(8,128)(2,1)}, u32[]{:S(2)}) copy-start(bf16[128,512]{1,0:T(8,128)(2,1)} %refs_0_.3) | copy-start | bytes 393220
  0.6 20.7 %copy-start.5 = (bf16[128,128]{1,0:T(8,128)(2,1)S(1)}, bf16[128,128]{1,0:T(8,128)(2,1)}, u32[]{:S(2)}) copy-start(bf16[128,128]{1,0:T(8,128)(2,1)} %refs_8_.1) | copy-start | bytes 98308
  0.6 20.7 %collective-permute-start.5 = (bf16[256,512]{1,0:T(8,128)(2,1)}, bf16[256,512]{1,0:T(8,128)(2,1)S(1)}, u32[]{:S(2)}, u32[]{:S(2)}) collective-permute-start(bf16[256,512]{1,0:T(8,128)(2,1)} %refs_4_.1), channel_id=1, source_target_pairs={{0,1},{1,0},{2,3},{3,2},{4,5},{5,4},{6,7},{7,6},{8,9},{9,8},{10,11... | collective-permute-start | bytes 786440 | tf_op jit(solution)/shard_map/ppermute | solution.py:16
  1.2 22.9 %collective-permute-start.3 = (bf16[256,512]{1,0:T(8,128)(2,1)}, bf16[256,512]{1,0:T(8,128)(2,1)S(1)}, u32[]{:S(2)}, u32[]{:S(2)}) collective-permute-start(bf16[256,512]{1,0:T(8,128)(2,1)} %refs_4_.1), channel_id=1, source_target_pairs={{0,8},{1,9},{2,10},{3,11},{4,12},{5,13},{6,14},{7,15},{8,0},{9,1},... | collective-permute-start | bytes 786440 | tf_op jit(solution)/shard_map/ppermute | solution.py:16
  5.7 3.2 %collective-permute-start.6 = (bf16[256,128]{1,0:T(8,128)(2,1)S(1)}, bf16[256,128]{1,0:T(8,128)(2,1)S(1)}, u32[]{:S(2)}, u32[]{:S(2)}) collective-permute-start(bf16[256,128]{1,0:T(8,128)(2,1)S(1)} %convert_element_type.6.refs_6_), channel_id=1, source_target_pairs={{0,1},{1,0},{2,3},{3,2},{4,5},{5,4},{6,7},{7,6},{8,9},{9,8},{10,11... | collective-permute-start | bytes 196616 | tf_op jit(solution)/shard_map/ppermute | solution.py:16
  5.9 8.7 %collective-permute-start.2 = (bf16[128,512]{1,0:T(8,128)(2,1)S(1)}, bf16[128,512]{1,0:T(8,128)(2,1)S(1)}, u32[]{:S(2)}, u32[]{:S(2)}) collective-permute-start(bf16[128,512]{1,0:T(8,128)(2,1)S(1)} %copy-done.3), channel_id=1, source_target_pairs={{0,6},{1,7},{2,4},{3,5},{4,2},{5,3},{6,0},{7,1},{8,14},{9,15},{10,... | collective-permute-start | bytes 393224 | tf_op jit(solution)/shard_map/ppermute | solution.py:16
  8.4 12.8 %collective-permute-start.1 = (bf16[128,512]{1,0:T(8,128)(2,1)S(1)}, bf16[128,512]{1,0:T(8,128)(2,1)S(1)}, u32[]{:S(2)}, u32[]{:S(2)}) collective-permute-start(bf16[128,512]{1,0:T(8,128)(2,1)S(1)} %copy-done.3), channel_id=1, source_target_pairs={{0,4},{1,5},{2,6},{3,7},{4,0},{5,1},{6,2},{7,3},{8,12},{9,13},{10,... | collective-permute-start | bytes 393224 | tf_op jit(solution)/shard_map/ppermute | solution.py:16
  8.9 12.4 %collective-permute-start = (bf16[128,512]{1,0:T(8,128)(2,1)S(1)}, bf16[128,512]{1,0:T(8,128)(2,1)S(1)}, u32[]{:S(2)}, u32[]{:S(2)}) collective-permute-start(bf16[128,512]{1,0:T(8,128)(2,1)S(1)} %copy-done.3), channel_id=1, source_target_pairs={{0,2},{1,3},{2,0},{3,1},{4,6},{5,7},{6,4},{7,5},{8,10},{9,11},{10,... | collective-permute-start | bytes 393224 | tf_op jit(solution)/shard_map/ppermute | solution.py:16
  14.6 9.5 %collective-permute-start.4 = (bf16[256,128]{1,0:T(8,128)(2,1)S(1)}, bf16[256,128]{1,0:T(8,128)(2,1)S(1)}, u32[]{:S(2)}, u32[]{:S(2)}) collective-permute-start(bf16[256,128]{1,0:T(8,128)(2,1)S(1)} %convert_element_type.6.refs_6_), channel_id=1, source_target_pairs={{0,8},{1,9},{2,10},{3,11},{4,12},{5,13},{6,14},{7,15},{8,0},{9,1},... | collective-permute-start | bytes 196616 | tf_op jit(solution)/shard_map/ppermute | solution.py:16
  21.3 1.0 %copy-start.4 = (bf16[256,512]{1,0:T(8,128)(2,1)S(1)}, bf16[256,512]{1,0:T(8,128)(2,1)}, u32[]{:S(2)}) copy-start(bf16[256,512]{1,0:T(8,128)(2,1)} %refs_4_.1) | copy-start | bytes 786436
  24.1 1.7 %collective-permute-start.7 = (bf16[256,512]{1,0:T(8,128)(2,1)S(1)}, bf16[256,512]{1,0:T(8,128)(2,1)S(1)}, u32[]{:S(2)}, u32[]{:S(2)}) collective-permute-start(bf16[256,512]{1,0:T(8,128)(2,1)S(1)} %collective-permute-done.3.refs_4_), channel_id=1, source_target_pairs={{0,1},{1,0},{2,3},{3,2},{4,5},{5,4},{6,7},{7,6},{8,9},{9,8},{10,11... | collective-permute-start | bytes 786440 | tf_op jit(solution)/shard_map/ppermute | solution.py:16
  24.2 1.6 %collective-permute-start.8 = (bf16[256,128]{1,0:T(8,128)(2,1)S(1)}, bf16[256,128]{1,0:T(8,128)(2,1)S(1)}, u32[]{:S(2)}, u32[]{:S(2)}) collective-permute-start(bf16[256,128]{1,0:T(8,128)(2,1)S(1)} %collective-permute-done.4.refs_6_), channel_id=1, source_target_pairs={{0,1},{1,0},{2,3},{3,2},{4,5},{5,4},{6,7},{7,6},{8,9},{9,8},{10,11... | collective-permute-start | bytes 196616 | tf_op jit(solution)/shard_map/ppermute | solution.py:16
  28.3 4.3 %collective-permute-start.9 = (f32[128,128]{1,0:T(8,128)S(1)}, f32[128,128]{1,0:T(8,128)S(1)}, u32[]{:S(2)}, u32[]{:S(2)}) collective-permute-start(f32[128,128]{1,0:T(8,128)S(1)} %get-tuple-element.34), channel_id=1, source_target_pairs={{0,2},{1,3},{2,0},{3,1},{4,6},{5,7},{6,4},{7,5},{8,10},{9,11},{10,... | collective-permute-start | bytes 196616 | tf_op jit(solution)/shard_map/ppermute | solution.py:16
  28.4 4.7 %collective-permute-start.10 = (f32[128,128]{1,0:T(8,128)S(1)}, f32[128,128]{1,0:T(8,128)S(1)}, u32[]{:S(2)}, u32[]{:S(2)}) collective-permute-start(f32[128,128]{1,0:T(8,128)S(1)} %get-tuple-element.35), channel_id=1, source_target_pairs={{0,4},{1,5},{2,6},{3,7},{4,0},{5,1},{6,2},{7,3},{8,12},{9,13},{10,... | collective-permute-start | bytes 196616 | tf_op jit(solution)/shard_map/ppermute | solution.py:16
  28.4 6.6 %collective-permute-start.11 = (f32[128,128]{1,0:T(8,128)S(1)}, f32[128,128]{1,0:T(8,128)S(1)}, u32[]{:S(2)}, u32[]{:S(2)}) collective-permute-start(f32[128,128]{1,0:T(8,128)S(1)} %get-tuple-element.36), channel_id=1, source_target_pairs={{0,6},{1,7},{2,4},{3,5},{4,2},{5,3},{6,0},{7,1},{8,14},{9,15},{10,... | collective-permute-start | bytes 196616 | tf_op jit(solution)/shard_map/ppermute | solution.py:16
  35.7 4.8 %collective-permute-start.14 = (bf16[128,128]{1,0:T(8,128)(2,1)S(1)}, bf16[128,128]{1,0:T(8,128)(2,1)S(1)}, u32[]{:S(2)}, u32[]{:S(2)}) collective-permute-start(bf16[128,128]{1,0:T(8,128)(2,1)S(1)} %get-tuple-element.43.refs_2_), channel_id=1, source_target_pairs={{0,6},{1,7},{2,4},{3,5},{4,2},{5,3},{6,0},{7,1},{8,14},{9,15},{10,... | collective-permute-start | bytes 98312 | tf_op jit(solution)/shard_map/ppermute | solution.py:16
  37.6 3.9 %collective-permute-start.13 = (bf16[128,128]{1,0:T(8,128)(2,1)S(1)}, bf16[128,128]{1,0:T(8,128)(2,1)S(1)}, u32[]{:S(2)}, u32[]{:S(2)}) collective-permute-start(bf16[128,128]{1,0:T(8,128)(2,1)S(1)} %get-tuple-element.43.refs_2_), channel_id=1, source_target_pairs={{0,4},{1,5},{2,6},{3,7},{4,0},{5,1},{6,2},{7,3},{8,12},{9,13},{10,... | collective-permute-start | bytes 98312 | tf_op jit(solution)/shard_map/ppermute | solution.py:16
  37.6 3.9 %collective-permute-start.12 = (bf16[128,128]{1,0:T(8,128)(2,1)S(1)}, bf16[128,128]{1,0:T(8,128)(2,1)S(1)}, u32[]{:S(2)}, u32[]{:S(2)}) collective-permute-start(bf16[128,128]{1,0:T(8,128)(2,1)S(1)} %get-tuple-element.43.refs_2_), channel_id=1, source_target_pairs={{0,2},{1,3},{2,0},{3,1},{4,6},{5,7},{6,4},{7,5},{8,10},{9,11},{10,... | collective-permute-start | bytes 98312 | tf_op jit(solution)/shard_map/ppermute | solution.py:16
  42.1 1.6 %collective-permute-start.15 = (f32[512,128]{1,0:T(8,128)S(1)}, f32[512,128]{1,0:T(8,128)S(1)}, u32[]{:S(2)}, u32[]{:S(2)}) collective-permute-start(f32[512,128]{1,0:T(8,128)S(1)} %get-tuple-element.40), channel_id=1, source_target_pairs={{0,1},{1,0},{2,3},{3,2},{4,5},{5,4},{6,7},{7,6},{8,9},{9,8},{10,11... | collective-permute-start | bytes 786440 | tf_op jit(solution)/shard_map/ppermute | solution.py:16
  43.7 9.7 %copy-start = (f32[256,128]{1,0:T(8,128)S(1)}, f32[256,128]{1,0:T(8,128)}, u32[]{:S(2)}) copy-start(f32[256,128]{1,0:T(8,128)} %coefficients.1) | copy-start | bytes 393220
  43.7 9.7 %copy-start.1 = (f32[1,256,256]{2,1,0:T(8,128)S(1)}, f32[1,256,256]{2,1,0:T(8,128)}, u32[]{:S(2)}) copy-start(f32[1,256,256]{2,1,0:T(8,128)} %inverse.1) | copy-start | bytes 786436
  43.7 9.7 %copy-start.2 = (f32[256,128]{1,0:T(8,128)S(1)}, f32[256,128]{1,0:T(8,128)}, u32[]{:S(2)}) copy-start(f32[256,128]{1,0:T(8,128)} %momentum.1) | copy-start | bytes 393220
  43.8 9.7 %collective-permute-start.16 = (f32[256,128]{1,0:T(8,128)S(1)}, f32[256,128]{1,0:T(8,128)S(1)}, u32[]{:S(2)}, u32[]{:S(2)}) collective-permute-start(f32[256,128]{1,0:T(8,128)S(1)} %get-tuple-element.45), channel_id=1, source_target_pairs={{0,8},{1,9},{2,10},{3,11},{4,12},{5,13},{6,14},{7,15},{8,0},{9,1},... | collective-permute-start | bytes 393224 | tf_op jit(solution)/shard_map/ppermute | solution.py:16

commit v2 on v1

v2 whole, which is shorter than its diff:
```python
import functools

import jax
import jax.numpy as jnp
from jax import lax
from jax.experimental import pallas as pl
from jax.experimental.pallas import tpu as pltpu
from jax.sharding import PartitionSpec as P


F32, BF16 = jnp.float32, jnp.bfloat16
MIB = 1 << 20


def swap(x, mask, size):
    return lax.ppermute(x, "wide", [(i, i ^ mask) for i in range(size)])


def masks_of(bits):
    masks = [0]
    for bit in bits:
        masks += [m ^ bit for m in masks]
    return masks


def digits_of(bits):
    return [bits[i : i + 2] for i in range(0, len(bits), 2)]


def gather_pieces(x, digits, size):
    pieces = [x]
    for digit in digits:
        whole = pieces[0] if len(pieces) == 1 else jnp.concatenate(pieces)
        pieces = [whole] + [swap(whole, m, size) for m in masks_of(digit)[1:]]
    return pieces


def nbytes(*arrays):
    return sum(a.size * a.dtype.itemsize for a in arrays)


def whole_call(body, outs, args, scratch=(), flops=0):
    moved = nbytes(*args, *outs)
    return pl.pallas_call(
        body,
        out_shape=outs,
        in_specs=[pl.BlockSpec(memory_space=pltpu.VMEM)] * len(args),
        out_specs=[pl.BlockSpec(memory_space=pltpu.VMEM)] * len(outs),
        scratch_shapes=scratch,
        compiler_params=pltpu.CompilerParams(vmem_limit_bytes=moved + 12 * MIB),
        cost_estimate=pl.CostEstimate(flops=flops, bytes_accessed=moved, transcendentals=0),
    )(*args)


def prepare_body(features, centres, coefficients, rows, blocks, weights):
    rows[...] = features[...]
    blocks[...] = centres[...]
    weights[...] = coefficients[...].astype(BF16)


def prepare(features, centres, coefficients):
    outs = [jax.ShapeDtypeStruct(x.shape, BF16) for x in (features, centres, coefficients)]
    return whole_call(prepare_body, outs, [features, centres, coefficients])


def predict_body(nrow, ncen, first, *refs):
    rows, refs = refs[:nrow], refs[nrow:]
    blocks, refs = refs[:ncen], refs[ncen:]
    weights, refs = refs[:ncen], refs[ncen:]
    given, refs = ((), refs) if first else (refs[:nrow], refs[nrow:])
    kernel_ref, sums = refs[0], refs[1:]
    width = rows[0].shape[1]
    centres = jnp.concatenate([block[...] for block in blocks])
    coefs = jnp.concatenate([weight[...].astype(BF16) for weight in weights])
    dims = (((1,), (1,)), ((), ()))
    square = centres.astype(F32) ** 2
    high = square.astype(BF16)
    low = (square - high.astype(F32)).astype(BF16)
    ones = jnp.ones((8, width), BF16)
    norms = lax.dot_general(ones, high, dims, preferred_element_type=F32)
    norms = (norms + lax.dot_general(ones, low, dims, preferred_element_type=F32))[:1]

    def tile(x, at):
        row_norms = jnp.sum(x.astype(F32) ** 2, axis=1, keepdims=True)
        products = lax.dot_general(x, centres, dims, preferred_element_type=F32)
        k = jnp.exp((2.0 * products - row_norms - norms) * (2.0 / width)).astype(BF16)
        kernel_ref[at, :] = k
        return jnp.dot(k, coefs, preferred_element_type=F32)

    sizes = [x.shape[0] for x in rows]
    if sum(sizes) <= 512:
        part = tile(jnp.concatenate([x[...] for x in rows]), slice(None))
        starts = [sum(sizes[:n]) for n in range(nrow)]
        for n, start in enumerate(starts):
            sums[n][...] = part[start : start + sizes[n]]
    else:
        base = 0
        for x, out in zip(rows, sums):
            chunk = min(512, x.shape[0])

            @pl.loop(0, x.shape[0] // chunk)
            def _(i, x=x, out=out, base=base, chunk=chunk):
                at = pl.ds(i * chunk, chunk)
                out[at, :] = tile(x[at, :], pl.ds(base + i * chunk, chunk))

            base += x.shape[0]
    for out, before in zip(sums, given):
        out[...] += before[...]


def predict(rows, blocks, given=(), flops=None):
    blocks, weights = zip(*blocks)
    total = sum(x.shape[0] for x in rows)
    depth = sum(b.shape[0] for b in blocks)
    width = rows[0].shape[1]
    outs = weights[0].shape[1]
    shapes = [jax.ShapeDtypeStruct((total, depth), BF16)]
    shapes += [jax.ShapeDtypeStruct((x.shape[0], outs), F32) for x in rows]
    body = functools.partial(predict_body, len(rows), len(blocks), not given)
    flops = flops or 2 * total * depth * (width + outs)
    kernel, *sums = whole_call(body, shapes, [*rows, *blocks, *weights, *given], flops=flops)
    return kernel, sums


def gradient_body(layout, npiece, *refs):
    kernels, refs = refs[: len(layout)], refs[len(layout) :]
    pieces, refs = refs[:npiece], refs[npiece:]
    *outs, residual = refs
    base = 0
    for piece in pieces:
        residual[base : base + piece.shape[0], :] = piece[...]
        base += piece.shape[0]
    started = set()
    for kernel, (first_row, columns) in zip(kernels, layout):
        rows, depth = kernel.shape
        order = depth // len(columns)
        chunk = min(512, rows)
        for n, (out, place) in enumerate(columns):
            at = slice(place * order, (place + 1) * order)

            def term(i, kernel=kernel, n=n, first_row=first_row, chunk=chunk, order=order):
                return lax.dot_general(
                    kernel[pl.ds(i * chunk, chunk), n * order : (n + 1) * order],
                    residual[pl.ds(first_row + i * chunk, chunk), :],
                    (((0,), (0,)), ((), ())),
                    preferred_element_type=F32,
                )

            if (out, place) in started:
                outs[out][at, :] += term(0)
            else:
                outs[out][at, :] = term(0)
                started.add((out, place))
            if rows > chunk:

                @pl.loop(1, rows // chunk)
                def _(i, out=out, at=at, term=term):
                    outs[out][at, :] += term(i)


def gradients(kernels, layout, pieces, count):
    total = sum(p.shape[0] for p in pieces)
    columns = pieces[0].shape[1]
    out = jax.ShapeDtypeStruct((2 * count, columns), F32)
    body = functools.partial(gradient_body, layout, len(pieces))
    return whole_call(
        body,
        [out, out],
        [*kernels, *pieces],
        scratch=[pltpu.VMEM((total, columns), BF16)],
        flops=8 * total * count * columns,
    )


def update_body(batch, keep, arrived, inverse, momentum, coefficients, new_momentum, new_coefficients):
    gradient = keep[...] + arrived[...]
    nblocks, order = inverse.shape[0], inverse.shape[1]
    for b in range(nblocks):
        at = slice(b * order, (b + 1) * order)
        conditioned = jnp.dot(
            inverse[b], gradient[at], precision=lax.Precision.HIGHEST, preferred_element_type=F32
        )
        moved = 0.9 * momentum[at, :] + conditioned / batch
        new_momentum[at, :] = moved
        new_coefficients[at, :] = coefficients[at, :] - 0.5 * moved


def shards(size, features, centres, targets, coefficients, momentum, block_inverse):
    batch = features.shape[0] * size
    count = centres.shape[0]
    core, far = 1, 2
    digits = digits_of([1 << b for b in range(1, size.bit_length() - 1) if 1 << b != far])
    send = functools.partial(swap, size=size)

    own_rows, *own = prepare(features, centres, coefficients)
    rows = gather_pieces(features, digits, size)
    if len(digits) == 1:
        rows[0] = own_rows
    far_block = [send(centres, far), send(coefficients, far)]
    near = [send(centres, core), send(coefficients, core)]
    kernel_a, sums_a = predict(rows, [own], flops=4 * 10**9)
    kernel_b, sums_b = predict(rows, [near], sums_a)
    far_block, rows[-1] = lax.optimization_barrier((far_block, rows[-1]))
    distant = [far_block, [send(x, core) for x in far_block]]
    kernel_c, sums = predict(rows, distant, sums_b)
    kernels = [kernel_a, kernel_b, kernel_c]
    layout = ((0, ((0, 0),)), (0, ((1, 0),)), (0, ((0, 1), (1, 1))))

    for digit in reversed(digits):
        masks = masks_of(digit)
        if len(sums) == 1:
            sums = jnp.split(sums[0], len(masks))
        total = sums[0]
        for m, part in zip(masks[1:], sums[1:]):
            total = total + send(part, m)
        sums = [total]
    residual = sums[0] - targets.astype(F32)
    residuals = gather_pieces(residual.astype(BF16), digits, size)

    keep, give = gradients(kernels, layout, residuals, count)
    both = keep + send(give, core)
    arrived = send(both[count:], far)
    out = jax.ShapeDtypeStruct(momentum.shape, F32)
    new_momentum, new_coefficients = whole_call(
        functools.partial(update_body, batch),
        [out, out],
        [both[:count], arrived, block_inverse, momentum, coefficients],
    )
    return residual, new_momentum, new_coefficients


def solution(mesh):
    one = P(("groups", "wide"), None)
    in_specs = (one, one, one, one, one, P(("groups", "wide"), None, None))
    return jax.shard_map(
        functools.partial(shards, mesh.shape["wide"]),
        mesh=mesh,
        in_specs=in_specs,
        out_specs=(one, one, one),
        check_vma=False,
    )
```

time: 54.7 us -> 46.3 us (0.85)
  starting transfers between devices: 21.8 us -> 17.7 us
  waiting for transfers between devices: 23.5 us -> 20.2 us
  Pallas kernels: 5.83 us -> 4.91 us
  other arithmetic: 1.59 us -> 0.68 us
  local copies, waits for them, and re-layouts: 0.99 us -> 1.85 us
    ppermute x17, starting transfers between devices: 21.8 us -> 17.7 us  [swap(): return lax.ppermute(x, 'wide', [(i, i ^ mask) for i in range(size)])]
    ppermute x17, waiting for transfers between devices: 23.5 us -> 20.2 us  [swap(): return lax.ppermute(x, 'wide', [(i, i ^ mask) for i in range(size)])]
    pallas_call x4 -> x6, Pallas kernels: 5.83 us -> 4.91 us  [whole_call(): pl.pallas_call(body, out_shape=outs, in_specs=[pl.BlockSpec(memory_space=...]
    convert_element_type x1 -> x0, other arithmetic: 0.91 us -> none  [shards(): coef_half = coefficients.astype(BF16)]
    unnamed x12, local copies, waits for them, and re-layouts: 0.97 us -> 1.83 us
  transfers between devices with their start and end apart: 17 -> 17, of which waited for: 10 -> 12; matrix products, arithmetic and copies ran while one was open for 2% -> 0% of each run, Pallas kernels for 3% -> 5%
where the time goes in v2:
time: 46.3 us; the launch traced here: 46.1 us
  waiting for transfers between devices  20.2 us (44%)
  starting transfers between devices  17.7 us (38%)
  Pallas kernels  4.91 us (11%)
  local copies, waits for them, and re-layouts  1.85 us (4%)
  between operations  0.76 us (2%)
  other arithmetic  0.68 us (1%)
    ppermute x17, waiting for transfers between devices, swap(): return lax.ppermute(x, 'wide', [(i, i ^ mask) for i in range(size)])  20.2 us
    ppermute x17, starting transfers between devices, swap(): return lax.ppermute(x, 'wide', [(i, i ^ mask) for i in range(size)])  17.7 us
    pallas_call x6, Pallas kernels, whole_call(): pl.pallas_call(body, out_shape=outs, in_specs=[pl.BlockSpec(memory_space=...  4.91 us
    unnamed x12, local copies, waits for them, and re-layouts  1.83 us
  transfers between devices with their start and end apart: 17, of which 12 were waited for; matrix products, arithmetic and copies ran while one was open for 0% of the time, Pallas kernels for 5%

profile of v2, /device:TPU:0, one launch (start us, length us, event | category | flops | bytes accessed | tf_op | source)
XLA Modules:
  0.0 46.1 jit_solution(5459362296868257426)
XLA Ops:
  0.6 3.0 %collective-permute-start.2 = (bf16[256,512]{1,0:T(8,128)(2,1)}, bf16[256,512]{1,0:T(8,128)(2,1)S(1)}, u32[]{:S(2)}, u32[]{:S(2)}) collective-permute-start(bf16[256,512]{1,0:T(8,128)(2,1)} %centres.1), channel_id=1, source_target_pairs={{0,2},{1,3},{2,0},{3,1},{4,6},{5,7},{6,4},{7,5},{8,10},{9,11},{10,... | collective-permute-start | bytes 786440 | tf_op jit(solution)/shard_map/ppermute | solution.py:16
  3.7 3.6 %collective-permute-start.4 = (bf16[128,512]{1,0:T(8,128)(2,1)}, bf16[128,512]{1,0:T(8,128)(2,1)S(1)}, u32[]{:S(2)}, u32[]{:S(2)}) collective-permute-start(bf16[128,512]{1,0:T(8,128)(2,1)} %features.1), channel_id=1, source_target_pairs={{0,12},{1,13},{2,14},{3,15},{4,8},{5,9},{6,10},{7,11},{8,4},{9,5},... | collective-permute-start | bytes 393224 | tf_op jit(solution)/shard_map/ppermute | solution.py:16
  7.3 0.5 %collective-permute-start.3 = (f32[256,128]{1,0:T(8,128)}, f32[256,128]{1,0:T(8,128)S(1)}, u32[]{:S(2)}, u32[]{:S(2)}) collective-permute-start(f32[256,128]{1,0:T(8,128)} %coefficients.3), channel_id=1, source_target_pairs={{0,2},{1,3},{2,0},{3,1},{4,6},{5,7},{6,4},{7,5},{8,10},{9,11},{10,... | collective-permute-start | bytes 393224 | tf_op jit(solution)/shard_map/ppermute | solution.py:16
  7.8 0.6 %collective-permute-start.1 = (bf16[128,512]{1,0:T(8,128)(2,1)}, bf16[128,512]{1,0:T(8,128)(2,1)S(1)}, u32[]{:S(2)}, u32[]{:S(2)}) collective-permute-start(bf16[128,512]{1,0:T(8,128)(2,1)} %features.1), channel_id=1, source_target_pairs={{0,8},{1,9},{2,10},{3,11},{4,12},{5,13},{6,14},{7,15},{8,0},{9,1},... | collective-permute-start | bytes 393224 | tf_op jit(solution)/shard_map/ppermute | solution.py:16
  8.3 0.9 %copy-done = f32[256,128]{1,0:T(8,128)S(1)} copy-done((f32[256,128]{1,0:T(8,128)S(1)}, f32[256,128]{1,0:T(8,128)}, u32[]{:S(2)}) %copy-start) | copy-done | bytes 131096
  9.2 0.9 %copy-done.3 = bf16[128,512]{1,0:T(8,128)(2,1)S(1)} copy-done((bf16[128,512]{1,0:T(8,128)(2,1)S(1)}, bf16[128,512]{1,0:T(8,128)(2,1)}, u32[]{:S(2)}) %copy-start.3) | copy-done | bytes 131096
  10.1 1.0 %shard_map.85 = (bf16[128,512]{1,0:T(8,128)(2,1)S(1)}, bf16[256,512]{1,0:T(8,128)(2,1)S(1)}, bf16[256,128]{1,0:T(8,128)(2,1)S(1)}) custom-call(bf16[128,512]{1,0:T(8,128)(2,1)S(1)} %copy-done.3, bf16[256,512]{1,0:T(8,128)(2,1)} %centres.1, f32[256,128]{1,0:T(8,128)S(1)} %copy-done), custom_call_target="tpu_custom_call" | custom-call | bytes 983040 | tf_op jit(solution)/shard_map/pallas_call | solution.py:44
  11.1 1.0 %collective-permute-done.4.refs_3_ = bf16[128,512]{1,0:T(8,128)(2,1)S(1)} collective-permute-done((bf16[128,512]{1,0:T(8,128)(2,1)}, bf16[128,512]{1,0:T(8,128)(2,1)S(1)}, u32[]{:S(2)}, u32[]{:S(2)}) %collective-permute-start.4) | collective-permute-done | bytes 131104 | tf_op jit(solution)/shard_map/ppermute | solution.py:16
  12.1 0.9 %collective-permute-done.3.refs_6_ = f32[256,128]{1,0:T(8,128)S(1)} collective-permute-done((f32[256,128]{1,0:T(8,128)}, f32[256,128]{1,0:T(8,128)S(1)}, u32[]{:S(2)}, u32[]{:S(2)}) %collective-permute-start.3) | collective-permute-done | bytes 131104 | tf_op jit(solution)/shard_map/ppermute | solution.py:16
  13.0 0.5 %collective-permute-start.6 = (f32[256,128]{1,0:T(8,128)S(1)}, f32[256,128]{1,0:T(8,128)S(1)}, u32[]{:S(2)}, u32[]{:S(2)}) collective-permute-start(f32[256,128]{1,0:T(8,128)S(1)} %collective-permute-done.3.refs_6_), channel_id=1, source_target_pairs={{0,1},{1,0},{2,3},{3,2},{4,5},{5,4},{6,7},{7,6},{8,9},{9,8},{10,11... | collective-permute-start | bytes 393224 | tf_op jit(solution)/shard_map/ppermute | solution.py:16
  13.5 1.0 %collective-permute-done.refs_1_ = bf16[128,512]{1,0:T(8,128)(2,1)S(1)} collective-permute-done((bf16[128,512]{1,0:T(8,128)(2,1)}, bf16[128,512]{1,0:T(8,128)(2,1)S(1)}, u32[]{:S(2)}, u32[]{:S(2)}) %collective-permute-start) | collective-permute-done | bytes 131104 | tf_op jit(solution)/shard_map/ppermute | solution.py:16
  14.5 3.8 %collective-permute-done.1.refs_2_ = bf16[128,512]{1,0:T(8,128)(2,1)S(1)} collective-permute-done((bf16[128,512]{1,0:T(8,128)(2,1)}, bf16[128,512]{1,0:T(8,128)(2,1)S(1)}, u32[]{:S(2)}, u32[]{:S(2)}) %collective-permute-start.1) | collective-permute-done | bytes 131104 | tf_op jit(solution)/shard_map/ppermute | solution.py:16
  18.3 0.7 %shard_map.86 = (bf16[512,256]{1,0:T(8,128)(2,1)S(1)}, f32[128,128]{1,0:T(8,128)S(1)}, f32[128,128]{1,0:T(8,128)S(1)}, f32[128,128]{1,0:T(8,128)S(1)}, f32[128,128]{1,0:T(8,128)S(1)}) custom-call(bf16[128,512]{1,0:T(8,128)(2,1)S(1)} %get-tuple-element.28.refs_0_, bf16[128,512]{1,0:T(8,128)(2,1)S(1)} %collective-permute-done.refs_1_, ...), custom_call_target="tpu_custom_call" | custom-call | flops 4000000000 | bytes 1376256 | tf_op jit(solution)/shard_map/pallas_call | solution.py:44
  18.9 0.7 %shard_map.87 = (bf16[512,256]{1,0:T(8,128)(2,1)S(1)}, f32[128,128]{1,0:T(8,128)S(1)}, f32[128,128]{1,0:T(8,128)S(1)}, f32[128,128]{1,0:T(8,128)S(1)}, f32[128,128]{1,0:T(8,128)S(1)}) custom-call(bf16[128,512]{1,0:T(8,128)(2,1)S(1)} %get-tuple-element.28.refs_0_, bf16[128,512]{1,0:T(8,128)(2,1)S(1)} %collective-permute-done.refs_1_, ...), custom_call_target="tpu_custom_call" | custom-call | flops 167772160 | bytes 1703936 | tf_op jit(solution)/shard_map/pallas_call | solution.py:44
  19.6 1.0 %shard_map.88 = (bf16[512,512]{1,0:T(8,128)(2,1)S(1)}, f32[128,128]{1,0:T(8,128)S(1)}, f32[128,128]{1,0:T(8,128)S(1)}, f32[128,128]{1,0:T(8,128)S(1)}, f32[128,128]{1,0:T(8,128)S(1)}) custom-call(bf16[128,512]{1,0:T(8,128)(2,1)S(1)} %get-tuple-element.28.refs_0_, bf16[128,512]{1,0:T(8,128)(2,1)S(1)} %collective-permute-done.refs_1_, ...), custom_call_target="tpu_custom_call" | custom-call | flops 335544320 | bytes 2359296 | tf_op jit(solution)/shard_map/pallas_call | solution.py:44
  20.7 0.1 collective-permute-start.9
  20.8 3.0 %collective-permute-start.10 = (f32[128,128]{1,0:T(8,128)S(1)}, f32[128,128]{1,0:T(8,128)S(1)}, u32[]{:S(2)}, u32[]{:S(2)}) collective-permute-start(f32[128,128]{1,0:T(8,128)S(1)} %get-tuple-element.44), channel_id=1, source_target_pairs={{0,8},{1,9},{2,10},{3,11},{4,12},{5,13},{6,14},{7,15},{8,0},{9,1},... | collective-permute-start | bytes 196616 | tf_op jit(solution)/shard_map/ppermute | solution.py:16
  23.8 1.3 %collective-permute-start.11 = (f32[128,128]{1,0:T(8,128)S(1)}, f32[128,128]{1,0:T(8,128)S(1)}, u32[]{:S(2)}, u32[]{:S(2)}) collective-permute-start(f32[128,128]{1,0:T(8,128)S(1)} %get-tuple-element.45), channel_id=1, source_target_pairs={{0,12},{1,13},{2,14},{3,15},{4,8},{5,9},{6,10},{7,11},{8,4},{9,5},... | collective-permute-start | bytes 196616 | tf_op jit(solution)/shard_map/ppermute | solution.py:16
  25.1 0.6 %collective-permute-done.9 = f32[128,128]{1,0:T(8,128)S(1)} collective-permute-done((f32[128,128]{1,0:T(8,128)S(1)}, f32[128,128]{1,0:T(8,128)S(1)}, u32[]{:S(2)}, u32[]{:S(2)}) %collective-permute-start.9) | collective-permute-done | bytes 65568 | tf_op jit(solution)/shard_map/ppermute | solution.py:16
  25.7 2.6 %collective-permute-done.10 = f32[128,128]{1,0:T(8,128)S(1)} collective-permute-done((f32[128,128]{1,0:T(8,128)S(1)}, f32[128,128]{1,0:T(8,128)S(1)}, u32[]{:S(2)}, u32[]{:S(2)}) %collective-permute-start.10) | collective-permute-done | bytes 65568 | tf_op jit(solution)/shard_map/ppermute | solution.py:16
  28.3 1.6 %collective-permute-done.11 = f32[128,128]{1,0:T(8,128)S(1)} collective-permute-done((f32[128,128]{1,0:T(8,128)S(1)}, f32[128,128]{1,0:T(8,128)S(1)}, u32[]{:S(2)}, u32[]{:S(2)}) %collective-permute-start.11) | collective-permute-done | bytes 65568 | tf_op jit(solution)/shard_map/ppermute | solution.py:16
  29.9 0.6 %fusion = (bf16[128,128]{1,0:T(8,128)(2,1)S(1)}, f32[128,128]{1,0:T(8,128)}) fusion(bf16[128,128]{1,0:T(8,128)(2,1)S(1)} %copy-done.5, f32[128,128]{1,0:T(8,128)S(1)} %collective-permute-done.11, f32[128,128]{1,0:T(8,128)S(1)} %collective-permute-done.10, f32[128,128]{1,0:T(8,128)S(1)} %get-tuple-element.42, f32[128,128]{1,0:T(8,128)S(1)} %collective-permute-done.9), kind=kLoop, calls=%fused_computation.1 | loop fusion | flops 98304 | bytes 393216 | tf_op jit(solution)/shard_map/convert_element_type | solution.py:218
  30.6 1.4 %collective-permute-start.14 = (bf16[128,128]{1,0:T(8,128)(2,1)S(1)}, bf16[128,128]{1,0:T(8,128)(2,1)S(1)}, u32[]{:S(2)}, u32[]{:S(2)}) collective-permute-start(bf16[128,128]{1,0:T(8,128)(2,1)S(1)} %get-tuple-element.53.refs_3_), channel_id=1, source_target_pairs={{0,12},{1,13},{2,14},{3,15},{4,8},{5,9},{6,10},{7,11},{8,4},{9,5},... | collective-permute-start | bytes 98312 | tf_op jit(solution)/shard_map/ppermute | solution.py:16
  32.0 3.0 %collective-permute-start.12 = (bf16[128,128]{1,0:T(8,128)(2,1)S(1)}, bf16[128,128]{1,0:T(8,128)(2,1)S(1)}, u32[]{:S(2)}, u32[]{:S(2)}) collective-permute-start(bf16[128,128]{1,0:T(8,128)(2,1)S(1)} %get-tuple-element.53.refs_3_), channel_id=1, source_target_pairs={{0,4},{1,5},{2,6},{3,7},{4,0},{5,1},{6,2},{7,3},{8,12},{9,13},{10,... | collective-permute-start | bytes 98312 | tf_op jit(solution)/shard_map/ppermute | solution.py:16
  35.0 1.3 %collective-permute-done.14.refs_6_ = bf16[128,128]{1,0:T(8,128)(2,1)S(1)} collective-permute-done((bf16[128,128]{1,0:T(8,128)(2,1)S(1)}, bf16[128,128]{1,0:T(8,128)(2,1)S(1)}, u32[]{:S(2)}, u32[]{:S(2)}) %collective-permute-start.14) | collective-permute-done | bytes 32800 | tf_op jit(solution)/shard_map/ppermute | solution.py:16
  36.3 0.8 %collective-permute-done.13.refs_5_ = bf16[128,128]{1,0:T(8,128)(2,1)S(1)} collective-permute-done((bf16[128,128]{1,0:T(8,128)(2,1)S(1)}, bf16[128,128]{1,0:T(8,128)(2,1)S(1)}, u32[]{:S(2)}, u32[]{:S(2)}) %collective-permute-start.13) | collective-permute-done | bytes 32800 | tf_op jit(solution)/shard_map/ppermute | solution.py:16
  37.1 0.1 collective-permute-done.12.refs_4_
  37.2 0.5 %shard_map.89 = (f32[512,128]{1,0:T(8,128)S(1)}, f32[512,128]{1,0:T(8,128)S(1)}) custom-call(bf16[512,256]{1,0:T(8,128)(2,1)S(1)} %get-tuple-element.46.refs_0_, bf16[512,256]{1,0:T(8,128)(2,1)S(1)} %get-tuple-element.47.refs_1_, bf16[512,512]{1,0:T(8,128)(2,1)S(1)} %get-tuple-element.48.refs_2_, bf16[128,128]{1,0:T(8,128)(2,1)S(1)} %get-tuple-element.53.refs_3_, ...), custom_call_target="tpu_custom_call" | custom-call | flops 134217728 | bytes 1703936 | tf_op jit(solution)/shard_map/pallas_call | solution.py:44
  37.8 1.5 %collective-permute-done.15 = f32[512,128]{1,0:T(8,128)S(1)} collective-permute-done((f32[512,128]{1,0:T(8,128)S(1)}, f32[512,128]{1,0:T(8,128)S(1)}, u32[]{:S(2)}, u32[]{:S(2)}) %collective-permute-start.15) | collective-permute-done | bytes 262176 | tf_op jit(solution)/shard_map/ppermute | solution.py:16
  39.4 0.5 %collective-permute-start.16 = (f32[256,128]{1,0:T(8,128)S(1)}, f32[256,128]{1,0:T(8,128)S(1)}, u32[]{:S(2)}, u32[]{:S(2)}) collective-permute-start(f32[256,128]{1,0:T(8,128)S(1)} %get-tuple-element.55), channel_id=1, source_target_pairs={{0,2},{1,3},{2,0},{3,1},{4,6},{5,7},{6,4},{7,5},{8,10},{9,11},{10,... | collective-permute-start | bytes 393224 | tf_op jit(solution)/shard_map/ppermute | solution.py:16
  39.9 5.1 %collective-permute-done.16.arrived = f32[256,128]{1,0:T(8,128)S(1)} collective-permute-done((f32[256,128]{1,0:T(8,128)S(1)}, f32[256,128]{1,0:T(8,128)S(1)}, u32[]{:S(2)}, u32[]{:S(2)}) %collective-permute-start.16) | collective-permute-done | bytes 131104 | tf_op jit(solution)/shard_map/ppermute | solution.py:16
  45.0 1.1 %shard_map.90 = (f32[256,128]{1,0:T(8,128)}, f32[256,128]{1,0:T(8,128)}) custom-call(f32[256,128]{1,0:T(8,128)S(1)} %get-tuple-element.56.keep, f32[256,128]{1,0:T(8,128)S(1)} %collective-permute-done.16.arrived, f32[1,256,256]{2,1,0:T(8,128)S(1)} %copy-done.2, f32[256,128]{1,0:T(8,128)S(1)} %copy-done.4, f32[256,128]{1,0:T(8,128)S(1)} %copy-done.1), custom_call_target="tpu_custom_call" | custom-call | bytes 1048576 | tf_op jit(solution)/shard_map/pallas_call | solution.py:44
  (23 shorter events, 0.2 us)
Async XLA Ops:
  0.6 12.4 %collective-permute-start.2 = (bf16[256,512]{1,0:T(8,128)(2,1)}, bf16[256,512]{1,0:T(8,128)(2,1)S(1)}, u32[]{:S(2)}, u32[]{:S(2)}) collective-permute-start(bf16[256,512]{1,0:T(8,128)(2,1)} %centres.1), channel_id=1, source_target_pairs={{0,2},{1,3},{2,0},{3,1},{4,6},{5,7},{6,4},{7,5},{8,10},{9,11},{10,... | collective-permute-start | bytes 786440 | tf_op jit(solution)/shard_map/ppermute | solution.py:16
  3.7 8.4 %collective-permute-start.4 = (bf16[128,512]{1,0:T(8,128)(2,1)}, bf16[128,512]{1,0:T(8,128)(2,1)S(1)}, u32[]{:S(2)}, u32[]{:S(2)}) collective-permute-start(bf16[128,512]{1,0:T(8,128)(2,1)} %features.1), channel_id=1, source_target_pairs={{0,12},{1,13},{2,14},{3,15},{4,8},{5,9},{6,10},{7,11},{8,4},{9,5},... | collective-permute-start | bytes 393224 | tf_op jit(solution)/shard_map/ppermute | solution.py:16
  7.3 5.7 %collective-permute-start.3 = (f32[256,128]{1,0:T(8,128)}, f32[256,128]{1,0:T(8,128)S(1)}, u32[]{:S(2)}, u32[]{:S(2)}) collective-permute-start(f32[256,128]{1,0:T(8,128)} %coefficients.3), channel_id=1, source_target_pairs={{0,2},{1,3},{2,0},{3,1},{4,6},{5,7},{6,4},{7,5},{8,10},{9,11},{10,... | collective-permute-start | bytes 393224 | tf_op jit(solution)/shard_map/ppermute | solution.py:16
  7.8 6.7 %collective-permute-start = (bf16[128,512]{1,0:T(8,128)(2,1)}, bf16[128,512]{1,0:T(8,128)(2,1)S(1)}, u32[]{:S(2)}, u32[]{:S(2)}) collective-permute-start(bf16[128,512]{1,0:T(8,128)(2,1)} %features.1), channel_id=1, source_target_pairs={{0,4},{1,5},{2,6},{3,7},{4,0},{5,1},{6,2},{7,3},{8,12},{9,13},{10,... | collective-permute-start | bytes 393224 | tf_op jit(solution)/shard_map/ppermute | solution.py:16
  7.8 10.5 %collective-permute-start.1 = (bf16[128,512]{1,0:T(8,128)(2,1)}, bf16[128,512]{1,0:T(8,128)(2,1)S(1)}, u32[]{:S(2)}, u32[]{:S(2)}) collective-permute-start(bf16[128,512]{1,0:T(8,128)(2,1)} %features.1), channel_id=1, source_target_pairs={{0,8},{1,9},{2,10},{3,11},{4,12},{5,13},{6,14},{7,15},{8,0},{9,1},... | collective-permute-start | bytes 393224 | tf_op jit(solution)/shard_map/ppermute | solution.py:16
  8.3 0.9 %copy-start = (f32[256,128]{1,0:T(8,128)S(1)}, f32[256,128]{1,0:T(8,128)}, u32[]{:S(2)}) copy-start(f32[256,128]{1,0:T(8,128)} %coefficients.3) | copy-start | bytes 393220
  9.2 0.9 %copy-start.3 = (bf16[128,512]{1,0:T(8,128)(2,1)S(1)}, bf16[128,512]{1,0:T(8,128)(2,1)}, u32[]{:S(2)}) copy-start(bf16[128,512]{1,0:T(8,128)(2,1)} %features.1) | copy-start | bytes 393220
  12.1 6.8 %collective-permute-start.8 = (f32[256,128]{1,0:T(8,128)S(1)}, f32[256,128]{1,0:T(8,128)S(1)}, u32[]{:S(2)}, u32[]{:S(2)}) collective-permute-start(f32[256,128]{1,0:T(8,128)S(1)} %copy-done), channel_id=1, source_target_pairs={{0,1},{1,0},{2,3},{3,2},{4,5},{5,4},{6,7},{7,6},{8,9},{9,8},{10,11... | collective-permute-start | bytes 393224 | tf_op jit(solution)/shard_map/ppermute | solution.py:16
  13.0 6.0 %collective-permute-start.7 = (bf16[256,512]{1,0:T(8,128)(2,1)}, bf16[256,512]{1,0:T(8,128)(2,1)S(1)}, u32[]{:S(2)}, u32[]{:S(2)}) collective-permute-start(bf16[256,512]{1,0:T(8,128)(2,1)} %centres.1), channel_id=1, source_target_pairs={{0,1},{1,0},{2,3},{3,2},{4,5},{5,4},{6,7},{7,6},{8,9},{9,8},{10,11... | collective-permute-start | bytes 786440 | tf_op jit(solution)/shard_map/ppermute | solution.py:16
  13.0 6.6 %collective-permute-start.6 = (f32[256,128]{1,0:T(8,128)S(1)}, f32[256,128]{1,0:T(8,128)S(1)}, u32[]{:S(2)}, u32[]{:S(2)}) collective-permute-start(f32[256,128]{1,0:T(8,128)S(1)} %collective-permute-done.3.refs_6_), channel_id=1, source_target_pairs={{0,1},{1,0},{2,3},{3,2},{4,5},{5,4},{6,7},{7,6},{8,9},{9,8},{10,11... | collective-permute-start | bytes 393224 | tf_op jit(solution)/shard_map/ppermute | solution.py:16
  14.5 5.2 %collective-permute-start.5 = (bf16[256,512]{1,0:T(8,128)(2,1)S(1)}, bf16[256,512]{1,0:T(8,128)(2,1)S(1)}, u32[]{:S(2)}, u32[]{:S(2)}) collective-permute-start(bf16[256,512]{1,0:T(8,128)(2,1)S(1)} %collective-permute-done.2.refs_4_), channel_id=1, source_target_pairs={{0,1},{1,0},{2,3},{3,2},{4,5},{5,4},{6,7},{7,6},{8,9},{9,8},{10,11... | collective-permute-start | bytes 786440 | tf_op jit(solution)/shard_map/ppermute | solution.py:16
  19.6 10.3 %copy-start.5 = (bf16[128,128]{1,0:T(8,128)(2,1)S(1)}, bf16[128,128]{1,0:T(8,128)(2,1)}, u32[]{:S(2)}) copy-start(bf16[128,128]{1,0:T(8,128)(2,1)} %param.8) | copy-start | bytes 98308
  20.7 5.0 %collective-permute-start.9 = (f32[128,128]{1,0:T(8,128)S(1)}, f32[128,128]{1,0:T(8,128)S(1)}, u32[]{:S(2)}, u32[]{:S(2)}) collective-permute-start(f32[128,128]{1,0:T(8,128)S(1)} %get-tuple-element.43), channel_id=1, source_target_pairs={{0,4},{1,5},{2,6},{3,7},{4,0},{5,1},{6,2},{7,3},{8,12},{9,13},{10,... | collective-permute-start | bytes 196616 | tf_op jit(solution)/shard_map/ppermute | solution.py:16
  20.8 7.6 %collective-permute-start.10 = (f32[128,128]{1,0:T(8,128)S(1)}, f32[128,128]{1,0:T(8,128)S(1)}, u32[]{:S(2)}, u32[]{:S(2)}) collective-permute-start(f32[128,128]{1,0:T(8,128)S(1)} %get-tuple-element.44), channel_id=1, source_target_pairs={{0,8},{1,9},{2,10},{3,11},{4,12},{5,13},{6,14},{7,15},{8,0},{9,1},... | collective-permute-start | bytes 196616 | tf_op jit(solution)/shard_map/ppermute | solution.py:16
  23.8 6.1 %collective-permute-start.11 = (f32[128,128]{1,0:T(8,128)S(1)}, f32[128,128]{1,0:T(8,128)S(1)}, u32[]{:S(2)}, u32[]{:S(2)}) collective-permute-start(f32[128,128]{1,0:T(8,128)S(1)} %get-tuple-element.45), channel_id=1, source_target_pairs={{0,12},{1,13},{2,14},{3,15},{4,8},{5,9},{6,10},{7,11},{8,4},{9,5},... | collective-permute-start | bytes 196616 | tf_op jit(solution)/shard_map/ppermute | solution.py:16
  30.6 5.7 %collective-permute-start.14 = (bf16[128,128]{1,0:T(8,128)(2,1)S(1)}, bf16[128,128]{1,0:T(8,128)(2,1)S(1)}, u32[]{:S(2)}, u32[]{:S(2)}) collective-permute-start(bf16[128,128]{1,0:T(8,128)(2,1)S(1)} %get-tuple-element.53.refs_3_), channel_id=1, source_target_pairs={{0,12},{1,13},{2,14},{3,15},{4,8},{5,9},{6,10},{7,11},{8,4},{9,5},... | collective-permute-start | bytes 98312 | tf_op jit(solution)/shard_map/ppermute | solution.py:16
  32.0 5.1 %collective-permute-start.13 = (bf16[128,128]{1,0:T(8,128)(2,1)S(1)}, bf16[128,128]{1,0:T(8,128)(2,1)S(1)}, u32[]{:S(2)}, u32[]{:S(2)}) collective-permute-start(bf16[128,128]{1,0:T(8,128)(2,1)S(1)} %get-tuple-element.53.refs_3_), channel_id=1, source_target_pairs={{0,8},{1,9},{2,10},{3,11},{4,12},{5,13},{6,14},{7,15},{8,0},{9,1},... | collective-permute-start | bytes 98312 | tf_op jit(solution)/shard_map/ppermute | solution.py:16
  32.0 5.2 %collective-permute-start.12 = (bf16[128,128]{1,0:T(8,128)(2,1)S(1)}, bf16[128,128]{1,0:T(8,128)(2,1)S(1)}, u32[]{:S(2)}, u32[]{:S(2)}) collective-permute-start(bf16[128,128]{1,0:T(8,128)(2,1)S(1)} %get-tuple-element.53.refs_3_), channel_id=1, source_target_pairs={{0,4},{1,5},{2,6},{3,7},{4,0},{5,1},{6,2},{7,3},{8,12},{9,13},{10,... | collective-permute-start | bytes 98312 | tf_op jit(solution)/shard_map/ppermute | solution.py:16
  37.7 1.6 %collective-permute-start.15 = (f32[512,128]{1,0:T(8,128)S(1)}, f32[512,128]{1,0:T(8,128)S(1)}, u32[]{:S(2)}, u32[]{:S(2)}) collective-permute-start(f32[512,128]{1,0:T(8,128)S(1)} %get-tuple-element.50), channel_id=1, source_target_pairs={{0,1},{1,0},{2,3},{3,2},{4,5},{5,4},{6,7},{7,6},{8,9},{9,8},{10,11... | collective-permute-start | bytes 786440 | tf_op jit(solution)/shard_map/ppermute | solution.py:16
  39.3 5.7 %copy-start.1 = (f32[256,128]{1,0:T(8,128)S(1)}, f32[256,128]{1,0:T(8,128)}, u32[]{:S(2)}) copy-start(f32[256,128]{1,0:T(8,128)} %coefficients.3) | copy-start | bytes 393220
  39.3 5.7 %copy-start.2 = (f32[1,256,256]{2,1,0:T(8,128)S(1)}, f32[1,256,256]{2,1,0:T(8,128)}, u32[]{:S(2)}) copy-start(f32[1,256,256]{2,1,0:T(8,128)} %inverse.1) | copy-start | bytes 786436
  39.4 5.7 %copy-start.4 = (f32[256,128]{1,0:T(8,128)S(1)}, f32[256,128]{1,0:T(8,128)}, u32[]{:S(2)}) copy-start(f32[256,128]{1,0:T(8,128)} %momentum.1) | copy-start | bytes 393220
  39.4 5.6 %collective-permute-start.16 = (f32[256,128]{1,0:T(8,128)S(1)}, f32[256,128]{1,0:T(8,128)S(1)}, u32[]{:S(2)}, u32[]{:S(2)}) collective-permute-start(f32[256,128]{1,0:T(8,128)S(1)} %get-tuple-element.55), channel_id=1, source_target_pairs={{0,2},{1,3},{2,0},{3,1},{4,6},{5,7},{6,4},{7,5},{8,10},{9,11},{10,... | collective-permute-start | bytes 393224 | tf_op jit(solution)/shard_map/ppermute | solution.py:16

commit v3 on v2

--- a/solution.py
+++ b/solution.py
@@ -10,6 +10,9 @@
 
 F32, BF16 = jnp.float32, jnp.bfloat16
 MIB = 1 << 20
+SUM_ORDER = (3, 1, 2, 0)
+GATHER_ORDER = (0, 1, 2, 3)
+ROW_ORDER = (0, 1, 2, 3)
 
 
 def swap(x, mask, size):
@@ -33,6 +36,26 @@
         whole = pieces[0] if len(pieces) == 1 else jnp.concatenate(pieces)
         pieces = [whole] + [swap(whole, m, size) for m in masks_of(digit)[1:]]
     return pieces
+
+
+def relay_pieces(x, digits, size):
+    pieces = [x]
+    for digit in digits:
+        pieces = [pieces[0] if len(pieces) == 1 else jnp.concatenate(pieces)]
+        if len(digit) == 2:
+            far = swap(pieces[0], digit[1], size)
+            pieces += [swap(pieces[0], digit[0], size), far, swap(far, digit[0], size)]
+        else:
+            pieces += [swap(pieces[0], digit[0], size)]
+    return pieces
+
+
+def in_order(items, order):
+    return [items[order.index(n)] for n in range(len(items))] if len(order) == len(items) else list(items)
+
+
+def put(items, order):
+    return [items[n] for n in order] if len(order) == len(items) else list(items)
 
 
 def nbytes(*arrays):
@@ -63,10 +86,10 @@
     return whole_call(prepare_body, outs, [features, centres, coefficients])
 
 
-def predict_body(nrow, ncen, first, *refs):
-    rows, refs = refs[:nrow], refs[nrow:]
+def predict_body(nrow, ncen, nweight, first, *refs):
+    rows, refs = in_order(refs[:nrow], ROW_ORDER), refs[nrow:]
     blocks, refs = refs[:ncen], refs[ncen:]
-    weights, refs = refs[:ncen], refs[ncen:]
+    weights, refs = refs[:nweight], refs[nweight:]
     given, refs = ((), refs) if first else (refs[:nrow], refs[nrow:])
     kernel_ref, sums = refs[0], refs[1:]
     width = rows[0].shape[1]
@@ -109,36 +132,34 @@
 
 
 def predict(rows, blocks, given=(), flops=None):
-    blocks, weights = zip(*blocks)
+    blocks, weights = blocks
     total = sum(x.shape[0] for x in rows)
     depth = sum(b.shape[0] for b in blocks)
     width = rows[0].shape[1]
     outs = weights[0].shape[1]
     shapes = [jax.ShapeDtypeStruct((total, depth), BF16)]
     shapes += [jax.ShapeDtypeStruct((x.shape[0], outs), F32) for x in rows]
-    body = functools.partial(predict_body, len(rows), len(blocks), not given)
+    body = functools.partial(predict_body, len(rows), len(blocks), len(weights), not given)
     flops = flops or 2 * total * depth * (width + outs)
-    kernel, *sums = whole_call(body, shapes, [*rows, *blocks, *weights, *given], flops=flops)
+    kernel, *sums = whole_call(body, shapes, [*put(rows, ROW_ORDER), *blocks, *weights, *given], flops=flops)
     return kernel, sums
 
 
-def gradient_body(layout, npiece, *refs):
+def gradient_body(layout, npiece, nout, *refs):
     kernels, refs = refs[: len(layout)], refs[len(layout) :]
-    pieces, refs = refs[:npiece], refs[npiece:]
+    pieces, refs = in_order(refs[:npiece], GATHER_ORDER), refs[npiece:]
     *outs, residual = refs
     base = 0
     for piece in pieces:
         residual[base : base + piece.shape[0], :] = piece[...]
         base += piece.shape[0]
     started = set()
-    for kernel, (first_row, columns) in zip(kernels, layout):
-        rows, depth = kernel.shape
-        order = depth // len(columns)
+    for kernel, (first_row, first_block, blocks) in zip(kernels, layout):
+        rows, order = kernel.shape[0], outs[0].shape[0]
         chunk = min(512, rows)
-        for n, (out, place) in enumerate(columns):
-            at = slice(place * order, (place + 1) * order)
-
-            def term(i, kernel=kernel, n=n, first_row=first_row, chunk=chunk, order=order):
+        for n, out in enumerate(blocks, first_block):
+
+            def term(i, kernel=kernel, n=n, first_row=first_row, chunk=chunk):
                 return lax.dot_general(
                     kernel[pl.ds(i * chunk, chunk), n * order : (n + 1) * order],
                     residual[pl.ds(first_row + i * chunk, chunk), :],
@@ -146,34 +167,50 @@
                     preferred_element_type=F32,
                 )
 
-            if (out, place) in started:
-                outs[out][at, :] += term(0)
+            if out in started:
+                outs[out][...] += term(0)
             else:
-                outs[out][at, :] = term(0)
-                started.add((out, place))
+                outs[out][...] = term(0)
+                started.add(out)
             if rows > chunk:
 
                 @pl.loop(1, rows // chunk)
-                def _(i, out=out, at=at, term=term):
-                    outs[out][at, :] += term(i)
-
-
-def gradients(kernels, layout, pieces, count):
+                def _(i, out=out, term=term):
+                    outs[out][...] += term(i)
+
+
+def gradients(kernels, layout, pieces, count, nout=2):
     total = sum(p.shape[0] for p in pieces)
     columns = pieces[0].shape[1]
-    out = jax.ShapeDtypeStruct((2 * count, columns), F32)
-    body = functools.partial(gradient_body, layout, len(pieces))
+    out = jax.ShapeDtypeStruct((count, columns), F32)
+    body = functools.partial(gradient_body, layout, len(pieces), nout)
     return whole_call(
         body,
-        [out, out],
-        [*kernels, *pieces],
+        [out] * nout,
+        [*kernels, *put(pieces, GATHER_ORDER)],
         scratch=[pltpu.VMEM((total, columns), BF16)],
-        flops=8 * total * count * columns,
-    )
-
-
-def update_body(batch, keep, arrived, inverse, momentum, coefficients, new_momentum, new_coefficients):
-    gradient = keep[...] + arrived[...]
+        flops=4 * total * count * columns,
+    )
+
+
+def residual_body(npart, *refs):
+    *parts, targets, residual, half = refs
+    parts = in_order(parts, SUM_ORDER)
+    total = parts[0][...]
+    for part in parts[1:]:
+        total += part[...]
+    total -= targets[...].astype(F32)
+    residual[...] = total
+    half[...] = total.astype(BF16)
+
+
+def update_body(batch, npart, *refs):
+    parts, refs = refs[:npart], refs[npart:]
+    inverse, momentum, coefficients, residual, new_momentum, new_coefficients, out = refs
+    out[...] = residual[...]
+    gradient = parts[0][...]
+    for part in parts[1:]:
+        gradient += part[...]
     nblocks, order = inverse.shape[0], inverse.shape[1]
     for b in range(nblocks):
         at = slice(b * order, (b + 1) * order)
@@ -193,38 +230,45 @@
     send = functools.partial(swap, size=size)
 
     own_rows, *own = prepare(features, centres, coefficients)
-    rows = gather_pieces(features, digits, size)
+    rows = relay_pieces(features, digits, size)
     if len(digits) == 1:
         rows[0] = own_rows
-    far_block = [send(centres, far), send(coefficients, far)]
-    near = [send(centres, core), send(coefficients, core)]
-    kernel_a, sums_a = predict(rows, [own], flops=4 * 10**9)
-    kernel_b, sums_b = predict(rows, [near], sums_a)
-    far_block, rows[-1] = lax.optimization_barrier((far_block, rows[-1]))
-    distant = [far_block, [send(x, core) for x in far_block]]
+    coefficients_ = coefficients
+    far_parts = [send(part, far) for part in jnp.split(centres, 2)]
+    far_coef = send(coefficients_, far)
+    near = [send(centres, core)], [send(coefficients_, core)]
+    own = own[:1], own[1:]
+    kernel_a, sums_a = predict(rows, own, flops=4 * 10**9)
+    kernel_b, sums_b = predict(rows, near, sums_a, flops=None)
+    far_parts, far_coef, rows[-2] = lax.optimization_barrier((far_parts, far_coef, rows[-2]))
+    distant = far_parts + [send(x, core) for x in far_parts], [far_coef, send(far_coef, core)]
     kernel_c, sums = predict(rows, distant, sums_b)
-    kernels = [kernel_a, kernel_b, kernel_c]
-    layout = ((0, ((0, 0),)), (0, ((1, 0),)), (0, ((0, 1), (1, 1))))
+    far_kernels, far_layout = [kernel_c], ((0, 0, (0, 1)),)
+    near_kernels, near_layout = [kernel_a, kernel_b], ((0, 0, (0,)), (0, 0, (1,)))
 
     for digit in reversed(digits):
         masks = masks_of(digit)
         if len(sums) == 1:
             sums = jnp.split(sums[0], len(masks))
-        total = sums[0]
-        for m, part in zip(masks[1:], sums[1:]):
-            total = total + send(part, m)
-        sums = [total]
-    residual = sums[0] - targets.astype(F32)
-    residuals = gather_pieces(residual.astype(BF16), digits, size)
-
-    keep, give = gradients(kernels, layout, residuals, count)
-    both = keep + send(give, core)
-    arrived = send(both[count:], far)
+        terms = [sums[0]] + [send(part, m) for m, part in zip(masks[1:], sums[1:])]
+        sums = [functools.reduce(jnp.add, terms)] if digit is not digits[0] else terms
+    held = jax.ShapeDtypeStruct(targets.shape, F32)
+    residual, half = whole_call(
+        functools.partial(residual_body, len(sums)),
+        [held, jax.ShapeDtypeStruct(targets.shape, BF16)],
+        [*put(sums, SUM_ORDER), targets],
+    )
+    residuals = gather_pieces(half, digits, size)
+
+    layout = far_layout + tuple((r, c, tuple(o + 2 for o in out)) for r, c, out in near_layout)
+    far_keep, far_give, keep, give = gradients(far_kernels + near_kernels, layout, residuals, count, 4)
+    far_got, got = send(far_give, core), send(give, core)
+    parts = [keep, got, send(far_keep + far_got, far)]
     out = jax.ShapeDtypeStruct(momentum.shape, F32)
-    new_momentum, new_coefficients = whole_call(
-        functools.partial(update_body, batch),
-        [out, out],
-        [both[:count], arrived, block_inverse, momentum, coefficients],
+    new_momentum, new_coefficients, residual = whole_call(
+        functools.partial(update_body, batch, len(parts)),
+        [out, out, held],
+        [*parts, block_inverse, momentum, coefficients, residual],
     )
     return residual, new_momentum, new_coefficients
 

time: 46.3 us -> 44.8 us (0.968)
  starting transfers between devices: 17.7 us -> 21.7 us
  waiting for transfers between devices: 20.2 us -> 17.2 us
  Pallas kernels: 4.91 us -> 4 us
  local copies, waits for them, and re-layouts: 1.85 us -> 1.01 us
  other arithmetic: 0.68 us -> 0.02 us
    ppermute x17 -> x20, starting transfers between devices: 17.7 us -> 21.7 us  [swap(): return lax.ppermute(x, 'wide', [(i, i ^ mask) for i in range(size)])]
    ppermute x17 -> x20, waiting for transfers between devices: 20.2 us -> 17.2 us  [swap(): return lax.ppermute(x, 'wide', [(i, i ^ mask) for i in range(size)])]
    unnamed x12, local copies, waits for them, and re-layouts: 1.83 us -> 0.03 us
    split x0 -> x1, local copies, waits for them, and re-layouts: none -> 0.98 us  [shards(): far_parts = [send(part, far) for part in jnp.split(centres, 2)]]
    pallas_call x6 -> x7, Pallas kernels: 4.91 us -> 4 us  [whole_call(): pl.pallas_call(body, out_shape=outs, in_specs=[pl.BlockSpec(memory_space=...]
    convert_element_type x1 -> x0, other arithmetic: 0.65 us -> none  [shards(): residuals = gather_pieces(residual.astype(BF16), digits, size)]
  transfers between devices with their start and end apart: 17 -> 20, of which waited for: 12 -> 10; matrix products, arithmetic and copies ran while one was open for 0% -> 2% of each run, Pallas kernels for 5% -> 3%
where the time goes in v3:
time: 44.8 us; the launch traced here: 44.7 us
  starting transfers between devices  21.7 us (48%)
  waiting for transfers between devices  17.2 us (38%)
  Pallas kernels  4 us (9%)
  local copies, waits for them, and re-layouts  1.01 us (2%)
  between operations  0.79 us (2%)
    ppermute x20, starting transfers between devices, swap(): return lax.ppermute(x, 'wide', [(i, i ^ mask) for i in range(size)])  21.7 us
    ppermute x20, waiting for transfers between devices, swap(): return lax.ppermute(x, 'wide', [(i, i ^ mask) for i in range(size)])  17.2 us
    pallas_call x7, Pallas kernels, whole_call(): pl.pallas_call(body, out_shape=outs, in_specs=[pl.BlockSpec(memory_space=...  4 us
    split x1, local copies, waits for them, and re-layouts, shards(): far_parts = [send(part, far) for part in jnp.split(centres, 2)]  0.98 us
  transfers between devices with their start and end apart: 20, of which 10 were waited for; matrix products, arithmetic and copies ran while one was open for 2% of the time, Pallas kernels for 3%

profile of v3, /device:TPU:0, one launch (start us, length us, event | category | flops | bytes accessed | tf_op | source)
XLA Modules:
  0.0 44.7 jit_solution(15109897412258628734)
XLA Ops:
  0.7 4.1 %collective-permute-start.4 = (bf16[128,512]{1,0:T(8,128)(2,1)}, bf16[128,512]{1,0:T(8,128)(2,1)S(1)}, u32[]{:S(2)}, u32[]{:S(2)}) collective-permute-start(bf16[128,512]{1,0:T(8,128)(2,1)} %features.1), channel_id=1, source_target_pairs={{0,8},{1,9},{2,10},{3,11},{4,12},{5,13},{6,14},{7,15},{8,0},{9,1},... | collective-permute-start | bytes 393224 | tf_op jit(solution)/shard_map/ppermute | solution.py:19
  4.8 1.5 %collective-permute-start.3 = (f32[256,128]{1,0:T(8,128)}, f32[256,128]{1,0:T(8,128)S(1)}, u32[]{:S(2)}, u32[]{:S(2)}) collective-permute-start(f32[256,128]{1,0:T(8,128)} %refs_5_.1), channel_id=1, source_target_pairs={{0,2},{1,3},{2,0},{3,1},{4,6},{5,7},{6,4},{7,5},{8,10},{9,11},{10,... | collective-permute-start | bytes 393224 | tf_op jit(solution)/shard_map/ppermute | solution.py:19
  6.3 1.0 %fusion = (bf16[128,512]{1,0:T(8,128)(2,1)S(1)}, bf16[128,512]{1,0:T(8,128)(2,1)S(1)}) fusion(bf16[256,512]{1,0:T(8,128)(2,1)} %centres.1), kind=kLoop, calls=%fused_computation | loop fusion | bytes 524288 | tf_op jit(solution)/shard_map/split | solution.py:237
  7.3 0.6 %collective-permute-start.2 = (bf16[128,512]{1,0:T(8,128)(2,1)S(1)}, bf16[128,512]{1,0:T(8,128)(2,1)S(1)}, u32[]{:S(2)}, u32[]{:S(2)}) collective-permute-start(bf16[128,512]{1,0:T(8,128)(2,1)S(1)} %get-tuple-element.65), channel_id=1, source_target_pairs={{0,2},{1,3},{2,0},{3,1},{4,6},{5,7},{6,4},{7,5},{8,10},{9,11},{10,... | collective-permute-start | bytes 393224 | tf_op jit(solution)/shard_map/ppermute | solution.py:19
  7.8 1.5 %collective-permute-start.1 = (bf16[128,512]{1,0:T(8,128)(2,1)S(1)}, bf16[128,512]{1,0:T(8,128)(2,1)S(1)}, u32[]{:S(2)}, u32[]{:S(2)}) collective-permute-start(bf16[128,512]{1,0:T(8,128)(2,1)S(1)} %get-tuple-element.66), channel_id=1, source_target_pairs={{0,2},{1,3},{2,0},{3,1},{4,6},{5,7},{6,4},{7,5},{8,10},{9,11},{10,... | collective-permute-start | bytes 393224 | tf_op jit(solution)/shard_map/ppermute | solution.py:19
  9.4 1.6 %collective-permute-start = (bf16[128,512]{1,0:T(8,128)(2,1)S(1)}, bf16[128,512]{1,0:T(8,128)(2,1)S(1)}, u32[]{:S(2)}, u32[]{:S(2)}) collective-permute-start(bf16[128,512]{1,0:T(8,128)(2,1)S(1)} %copy-done.4), channel_id=1, source_target_pairs={{0,4},{1,5},{2,6},{3,7},{4,0},{5,1},{6,2},{7,3},{8,12},{9,13},{10,... | collective-permute-start | bytes 393224 | tf_op jit(solution)/shard_map/ppermute | solution.py:19
  10.9 0.4 collective-permute-done.4.refs_2_
  11.3 0.8 %collective-permute-start.5 = (bf16[128,512]{1,0:T(8,128)(2,1)S(1)}, bf16[128,512]{1,0:T(8,128)(2,1)S(1)}, u32[]{:S(2)}, u32[]{:S(2)}) collective-permute-start(bf16[128,512]{1,0:T(8,128)(2,1)S(1)} %collective-permute-done.4.refs_2_), channel_id=1, source_target_pairs={{0,4},{1,5},{2,6},{3,7},{4,0},{5,1},{6,2},{7,3},{8,12},{9,13},{10,... | collective-permute-start | bytes 393224 | tf_op jit(solution)/shard_map/ppermute | solution.py:19
  12.2 0.1 collective-permute-start.10
  12.3 1.5 %collective-permute-done.2.refs_5_ = bf16[128,512]{1,0:T(8,128)(2,1)S(1)} collective-permute-done((bf16[128,512]{1,0:T(8,128)(2,1)S(1)}, bf16[128,512]{1,0:T(8,128)(2,1)S(1)}, u32[]{:S(2)}, u32[]{:S(2)}) %collective-permute-start.2) | collective-permute-done | bytes 131104 | tf_op jit(solution)/shard_map/ppermute | solution.py:19
  13.8 1.8 %collective-permute-done.1.refs_4_ = bf16[128,512]{1,0:T(8,128)(2,1)S(1)} collective-permute-done((bf16[128,512]{1,0:T(8,128)(2,1)S(1)}, bf16[128,512]{1,0:T(8,128)(2,1)S(1)}, u32[]{:S(2)}, u32[]{:S(2)}) %collective-permute-start.1) | collective-permute-done | bytes 131104 | tf_op jit(solution)/shard_map/ppermute | solution.py:19
  15.6 0.5 %collective-permute-start.7 = (bf16[128,512]{1,0:T(8,128)(2,1)S(1)}, bf16[128,512]{1,0:T(8,128)(2,1)S(1)}, u32[]{:S(2)}, u32[]{:S(2)}) collective-permute-start(bf16[128,512]{1,0:T(8,128)(2,1)S(1)} %collective-permute-done.2.refs_5_), channel_id=1, source_target_pairs={{0,1},{1,0},{2,3},{3,2},{4,5},{5,4},{6,7},{7,6},{8,9},{9,8},{10,11... | collective-permute-start | bytes 393224 | tf_op jit(solution)/shard_map/ppermute | solution.py:19
  16.1 1.1 %collective-permute-done.5.refs_3_ = bf16[128,512]{1,0:T(8,128)(2,1)S(1)} collective-permute-done((bf16[128,512]{1,0:T(8,128)(2,1)S(1)}, bf16[128,512]{1,0:T(8,128)(2,1)S(1)}, u32[]{:S(2)}, u32[]{:S(2)}) %collective-permute-start.5) | collective-permute-done | bytes 131104 | tf_op jit(solution)/shard_map/ppermute | solution.py:19
  17.1 0.7 %shard_map.86 = (bf16[512,256]{1,0:T(8,128)(2,1)S(1)}, f32[128,128]{1,0:T(8,128)S(1)}, f32[128,128]{1,0:T(8,128)S(1)}, f32[128,128]{1,0:T(8,128)S(1)}, f32[128,128]{1,0:T(8,128)S(1)}) custom-call(bf16[128,512]{1,0:T(8,128)(2,1)S(1)} %get-tuple-element.34.refs_0_, bf16[128,512]{1,0:T(8,128)(2,1)S(1)} %collective-permute-done.refs_1_, ...), custom_call_target="tpu_custom_call" | custom-call | flops 4000000000 | bytes 1376256 | tf_op jit(solution)/shard_map/pallas_call | solution.py:67
  17.8 0.7 %shard_map.87 = (bf16[512,256]{1,0:T(8,128)(2,1)S(1)}, f32[128,128]{1,0:T(8,128)S(1)}, f32[128,128]{1,0:T(8,128)S(1)}, f32[128,128]{1,0:T(8,128)S(1)}, f32[128,128]{1,0:T(8,128)S(1)}) custom-call(bf16[128,512]{1,0:T(8,128)(2,1)S(1)} %get-tuple-element.34.refs_0_, bf16[128,512]{1,0:T(8,128)(2,1)S(1)} %collective-permute-done.refs_1_, ...), custom_call_target="tpu_custom_call" | custom-call | flops 167772160 | bytes 1703936 | tf_op jit(solution)/shard_map/pallas_call | solution.py:67
  18.5 1.0 %shard_map.88 = (bf16[512,512]{1,0:T(8,128)(2,1)S(1)}, f32[128,128]{1,0:T(8,128)S(1)}, f32[128,128]{1,0:T(8,128)S(1)}, f32[128,128]{1,0:T(8,128)S(1)}, f32[128,128]{1,0:T(8,128)S(1)}) custom-call(bf16[128,512]{1,0:T(8,128)(2,1)S(1)} %get-tuple-element.34.refs_0_, bf16[128,512]{1,0:T(8,128)(2,1)S(1)} %collective-permute-done.refs_1_, ...), custom_call_target="tpu_custom_call" | custom-call | flops 335544320 | bytes 2359296 | tf_op jit(solution)/shard_map/pallas_call | solution.py:67
  19.6 3.3 %collective-permute-start.11 = (f32[128,128]{1,0:T(8,128)S(1)}, f32[128,128]{1,0:T(8,128)S(1)}, u32[]{:S(2)}, u32[]{:S(2)}) collective-permute-start(f32[128,128]{1,0:T(8,128)S(1)} %get-tuple-element.52), channel_id=1, source_target_pairs={{0,12},{1,13},{2,14},{3,15},{4,8},{5,9},{6,10},{7,11},{8,4},{9,5},... | collective-permute-start | bytes 196616 | tf_op jit(solution)/shard_map/ppermute | solution.py:19
  22.9 1.2 %collective-permute-start.13 = (f32[128,128]{1,0:T(8,128)S(1)}, f32[128,128]{1,0:T(8,128)S(1)}, u32[]{:S(2)}, u32[]{:S(2)}) collective-permute-start(f32[128,128]{1,0:T(8,128)S(1)} %get-tuple-element.54), channel_id=1, source_target_pairs={{0,8},{1,9},{2,10},{3,11},{4,12},{5,13},{6,14},{7,15},{8,0},{9,1},... | collective-permute-start | bytes 196616 | tf_op jit(solution)/shard_map/ppermute | solution.py:19
  24.0 2.3 %collective-permute-done.11.refs_0_ = f32[128,128]{1,0:T(8,128)S(1)} collective-permute-done((f32[128,128]{1,0:T(8,128)S(1)}, f32[128,128]{1,0:T(8,128)S(1)}, u32[]{:S(2)}, u32[]{:S(2)}) %collective-permute-start.11) | collective-permute-done | bytes 65568 | tf_op jit(solution)/shard_map/ppermute | solution.py:19
  26.4 2.5 %collective-permute-done.12.refs_1_ = f32[128,128]{1,0:T(8,128)S(1)} collective-permute-done((f32[128,128]{1,0:T(8,128)S(1)}, f32[128,128]{1,0:T(8,128)S(1)}, u32[]{:S(2)}, u32[]{:S(2)}) %collective-permute-start.12) | collective-permute-done | bytes 65568 | tf_op jit(solution)/shard_map/ppermute | solution.py:19
  28.9 2.2 %collective-permute-start.16 = (bf16[128,128]{1,0:T(8,128)(2,1)S(1)}, bf16[128,128]{1,0:T(8,128)(2,1)S(1)}, u32[]{:S(2)}, u32[]{:S(2)}) collective-permute-start(bf16[128,128]{1,0:T(8,128)(2,1)S(1)} %get-tuple-element.56.refs_3_), channel_id=1, source_target_pairs={{0,12},{1,13},{2,14},{3,15},{4,8},{5,9},{6,10},{7,11},{8,4},{9,5},... | collective-permute-start | bytes 98312 | tf_op jit(solution)/shard_map/ppermute | solution.py:19
  31.1 0.6 %collective-permute-start.15 = (bf16[128,128]{1,0:T(8,128)(2,1)S(1)}, bf16[128,128]{1,0:T(8,128)(2,1)S(1)}, u32[]{:S(2)}, u32[]{:S(2)}) collective-permute-start(bf16[128,128]{1,0:T(8,128)(2,1)S(1)} %get-tuple-element.56.refs_3_), channel_id=1, source_target_pairs={{0,8},{1,9},{2,10},{3,11},{4,12},{5,13},{6,14},{7,15},{8,0},{9,1},... | collective-permute-start | bytes 98312 | tf_op jit(solution)/shard_map/ppermute | solution.py:19
  31.6 1.7 %collective-permute-start.14 = (bf16[128,128]{1,0:T(8,128)(2,1)S(1)}, bf16[128,128]{1,0:T(8,128)(2,1)S(1)}, u32[]{:S(2)}, u32[]{:S(2)}) collective-permute-start(bf16[128,128]{1,0:T(8,128)(2,1)S(1)} %get-tuple-element.56.refs_3_), channel_id=1, source_target_pairs={{0,4},{1,5},{2,6},{3,7},{4,0},{5,1},{6,2},{7,3},{8,12},{9,13},{10,... | collective-permute-start | bytes 98312 | tf_op jit(solution)/shard_map/ppermute | solution.py:19
  33.3 1.5 %collective-permute-done.16.refs_6_ = bf16[128,128]{1,0:T(8,128)(2,1)S(1)} collective-permute-done((bf16[128,128]{1,0:T(8,128)(2,1)S(1)}, bf16[128,128]{1,0:T(8,128)(2,1)S(1)}, u32[]{:S(2)}, u32[]{:S(2)}) %collective-permute-start.16) | collective-permute-done | bytes 32800 | tf_op jit(solution)/shard_map/ppermute | solution.py:19
  34.9 1.1 %collective-permute-done.15.refs_5_ = bf16[128,128]{1,0:T(8,128)(2,1)S(1)} collective-permute-done((bf16[128,128]{1,0:T(8,128)(2,1)S(1)}, bf16[128,128]{1,0:T(8,128)(2,1)S(1)}, u32[]{:S(2)}, u32[]{:S(2)}) %collective-permute-start.15) | collective-permute-done | bytes 32800 | tf_op jit(solution)/shard_map/ppermute | solution.py:19
  36.0 0.5 %shard_map.90 = (f32[256,128]{1,0:T(8,128)S(1)}, f32[256,128]{1,0:T(8,128)S(1)}, f32[256,128]{1,0:T(8,128)S(1)}, f32[256,128]{1,0:T(8,128)S(1)}) custom-call(bf16[512,512]{1,0:T(8,128)(2,1)S(1)} %get-tuple-element.49.refs_0_, bf16[512,256]{1,0:T(8,128)(2,1)S(1)} %get-tuple-element.50.refs_1_, bf16[512,256]{1,0:T(8,128)(2,1)S(1)} %get-tuple-element.51.refs_2_, ...), custom_call_target="tpu_custom_call" | custom-call | flops 67108864 | bytes 1703936 | tf_op jit(solution)/shard_map/pallas_call | solution.py:67
  36.5 0.1 collective-permute-start.18
  36.6 0.5 %collective-permute-start.17 = (f32[256,128]{1,0:T(8,128)S(1)}, f32[256,128]{1,0:T(8,128)S(1)}, u32[]{:S(2)}, u32[]{:S(2)}) collective-permute-start(f32[256,128]{1,0:T(8,128)S(1)} %get-tuple-element.58), channel_id=1, source_target_pairs={{0,1},{1,0},{2,3},{3,2},{4,5},{5,4},{6,7},{7,6},{8,9},{9,8},{10,11... | collective-permute-start | bytes 393224 | tf_op jit(solution)/shard_map/ppermute | solution.py:19
  37.1 0.8 %collective-permute-done.18 = f32[256,128]{1,0:T(8,128)S(1)} collective-permute-done((f32[256,128]{1,0:T(8,128)S(1)}, f32[256,128]{1,0:T(8,128)S(1)}, u32[]{:S(2)}, u32[]{:S(2)}) %collective-permute-start.18) | collective-permute-done | bytes 131104 | tf_op jit(solution)/shard_map/ppermute | solution.py:19
  37.9 1.5 %collective-permute-start.19 = (f32[256,128]{1,0:T(8,128)S(1)}, f32[256,128]{1,0:T(8,128)S(1)}, u32[]{:S(2)}, u32[]{:S(2)}) collective-permute-start(f32[256,128]{1,0:T(8,128)S(1)} %add.3), channel_id=1, source_target_pairs={{0,2},{1,3},{2,0},{3,1},{4,6},{5,7},{6,4},{7,5},{8,10},{9,11},{10,... | collective-permute-start | bytes 393224 | tf_op jit(solution)/shard_map/ppermute | solution.py:19
  39.5 4.1 %collective-permute-done.19.refs_2_ = f32[256,128]{1,0:T(8,128)S(1)} collective-permute-done((f32[256,128]{1,0:T(8,128)S(1)}, f32[256,128]{1,0:T(8,128)S(1)}, u32[]{:S(2)}, u32[]{:S(2)}) %collective-permute-start.19) | collective-permute-done | bytes 131104 | tf_op jit(solution)/shard_map/ppermute | solution.py:19
  43.6 1.1 %shard_map.91 = (f32[256,128]{1,0:T(8,128)}, f32[256,128]{1,0:T(8,128)}, f32[128,128]{1,0:T(8,128)}) custom-call(f32[256,128]{1,0:T(8,128)S(1)} %get-tuple-element.57.refs_0_, f32[256,128]{1,0:T(8,128)S(1)} %collective-permute-done.17.refs_1_, f32[256,128]{1,0:T(8,128)S(1)} %collective-permute-done.19.refs_2_, f32[1,256,256]{2,1,0:T(8,128)S(1)} %copy-done.2, ...), custom_call_target="tpu_custom_call" | custom-call | bytes 1310720 | tf_op jit(solution)/shard_map/pallas_call | solution.py:67
  (29 shorter events, 0.1 us)
Async XLA Ops:
  0.6 8.7 %copy-start.4 = (bf16[128,512]{1,0:T(8,128)(2,1)S(1)}, bf16[128,512]{1,0:T(8,128)(2,1)}, u32[]{:S(2)}) copy-start(bf16[128,512]{1,0:T(8,128)(2,1)} %features.1) | copy-start | bytes 393220
  0.6 11.5 %copy-start.1 = (f32[256,128]{1,0:T(8,128)S(1)}, f32[256,128]{1,0:T(8,128)}, u32[]{:S(2)}) copy-start(f32[256,128]{1,0:T(8,128)} %refs_5_.1) | copy-start | bytes 393220
  0.7 11.5 %copy-start = (bf16[256,512]{1,0:T(8,128)(2,1)S(1)}, bf16[256,512]{1,0:T(8,128)(2,1)}, u32[]{:S(2)}) copy-start(bf16[256,512]{1,0:T(8,128)(2,1)} %centres.1) | copy-start | bytes 786436
  0.7 10.7 %collective-permute-start.4 = (bf16[128,512]{1,0:T(8,128)(2,1)}, bf16[128,512]{1,0:T(8,128)(2,1)S(1)}, u32[]{:S(2)}, u32[]{:S(2)}) collective-permute-start(bf16[128,512]{1,0:T(8,128)(2,1)} %features.1), channel_id=1, source_target_pairs={{0,8},{1,9},{2,10},{3,11},{4,12},{5,13},{6,14},{7,15},{8,0},{9,1},... | collective-permute-start | bytes 393224 | tf_op jit(solution)/shard_map/ppermute | solution.py:19
  4.8 7.4 %collective-permute-start.3 = (f32[256,128]{1,0:T(8,128)}, f32[256,128]{1,0:T(8,128)S(1)}, u32[]{:S(2)}, u32[]{:S(2)}) collective-permute-start(f32[256,128]{1,0:T(8,128)} %refs_5_.1), channel_id=1, source_target_pairs={{0,2},{1,3},{2,0},{3,1},{4,6},{5,7},{6,4},{7,5},{8,10},{9,11},{10,... | collective-permute-start | bytes 393224 | tf_op jit(solution)/shard_map/ppermute | solution.py:19
  7.3 6.5 %collective-permute-start.2 = (bf16[128,512]{1,0:T(8,128)(2,1)S(1)}, bf16[128,512]{1,0:T(8,128)(2,1)S(1)}, u32[]{:S(2)}, u32[]{:S(2)}) collective-permute-start(bf16[128,512]{1,0:T(8,128)(2,1)S(1)} %get-tuple-element.65), channel_id=1, source_target_pairs={{0,2},{1,3},{2,0},{3,1},{4,6},{5,7},{6,4},{7,5},{8,10},{9,11},{10,... | collective-permute-start | bytes 393224 | tf_op jit(solution)/shard_map/ppermute | solution.py:19
  7.8 7.7 %collective-permute-start.1 = (bf16[128,512]{1,0:T(8,128)(2,1)S(1)}, bf16[128,512]{1,0:T(8,128)(2,1)S(1)}, u32[]{:S(2)}, u32[]{:S(2)}) collective-permute-start(bf16[128,512]{1,0:T(8,128)(2,1)S(1)} %get-tuple-element.66), channel_id=1, source_target_pairs={{0,2},{1,3},{2,0},{3,1},{4,6},{5,7},{6,4},{7,5},{8,10},{9,11},{10,... | collective-permute-start | bytes 393224 | tf_op jit(solution)/shard_map/ppermute | solution.py:19
  9.4 6.2 %collective-permute-start = (bf16[128,512]{1,0:T(8,128)(2,1)S(1)}, bf16[128,512]{1,0:T(8,128)(2,1)S(1)}, u32[]{:S(2)}, u32[]{:S(2)}) collective-permute-start(bf16[128,512]{1,0:T(8,128)(2,1)S(1)} %copy-done.4), channel_id=1, source_target_pairs={{0,4},{1,5},{2,6},{3,7},{4,0},{5,1},{6,2},{7,3},{8,12},{9,13},{10,... | collective-permute-start | bytes 393224 | tf_op jit(solution)/shard_map/ppermute | solution.py:19
  11.3 5.8 %collective-permute-start.5 = (bf16[128,512]{1,0:T(8,128)(2,1)S(1)}, bf16[128,512]{1,0:T(8,128)(2,1)S(1)}, u32[]{:S(2)}, u32[]{:S(2)}) collective-permute-start(bf16[128,512]{1,0:T(8,128)(2,1)S(1)} %collective-permute-done.4.refs_2_), channel_id=1, source_target_pairs={{0,4},{1,5},{2,6},{3,7},{4,0},{5,1},{6,2},{7,3},{8,12},{9,13},{10,... | collective-permute-start | bytes 393224 | tf_op jit(solution)/shard_map/ppermute | solution.py:19
  12.2 5.6 %collective-permute-start.10 = (f32[256,128]{1,0:T(8,128)S(1)}, f32[256,128]{1,0:T(8,128)S(1)}, u32[]{:S(2)}, u32[]{:S(2)}) collective-permute-start(f32[256,128]{1,0:T(8,128)S(1)} %copy-done.1), channel_id=1, source_target_pairs={{0,1},{1,0},{2,3},{3,2},{4,5},{5,4},{6,7},{7,6},{8,9},{9,8},{10,11... | collective-permute-start | bytes 393224 | tf_op jit(solution)/shard_map/ppermute | solution.py:19
  13.8 4.0 %collective-permute-start.9 = (bf16[256,512]{1,0:T(8,128)(2,1)S(1)}, bf16[256,512]{1,0:T(8,128)(2,1)S(1)}, u32[]{:S(2)}, u32[]{:S(2)}) collective-permute-start(bf16[256,512]{1,0:T(8,128)(2,1)S(1)} %copy-done), channel_id=1, source_target_pairs={{0,1},{1,0},{2,3},{3,2},{4,5},{5,4},{6,7},{7,6},{8,9},{9,8},{10,11... | collective-permute-start | bytes 786440 | tf_op jit(solution)/shard_map/ppermute | solution.py:19
  15.6 2.9 %collective-permute-start.6 = (bf16[128,512]{1,0:T(8,128)(2,1)S(1)}, bf16[128,512]{1,0:T(8,128)(2,1)S(1)}, u32[]{:S(2)}, u32[]{:S(2)}) collective-permute-start(bf16[128,512]{1,0:T(8,128)(2,1)S(1)} %collective-permute-done.1.refs_4_), channel_id=1, source_target_pairs={{0,1},{1,0},{2,3},{3,2},{4,5},{5,4},{6,7},{7,6},{8,9},{9,8},{10,11... | collective-permute-start | bytes 393224 | tf_op jit(solution)/shard_map/ppermute | solution.py:19
  15.6 2.9 %collective-permute-start.7 = (bf16[128,512]{1,0:T(8,128)(2,1)S(1)}, bf16[128,512]{1,0:T(8,128)(2,1)S(1)}, u32[]{:S(2)}, u32[]{:S(2)}) collective-permute-start(bf16[128,512]{1,0:T(8,128)(2,1)S(1)} %collective-permute-done.2.refs_5_), channel_id=1, source_target_pairs={{0,1},{1,0},{2,3},{3,2},{4,5},{5,4},{6,7},{7,6},{8,9},{9,8},{10,11... | collective-permute-start | bytes 393224 | tf_op jit(solution)/shard_map/ppermute | solution.py:19
  17.1 1.4 %collective-permute-start.8 = (f32[256,128]{1,0:T(8,128)S(1)}, f32[256,128]{1,0:T(8,128)S(1)}, u32[]{:S(2)}, u32[]{:S(2)}) collective-permute-start(f32[256,128]{1,0:T(8,128)S(1)} %collective-permute-done.3.refs_8_), channel_id=1, source_target_pairs={{0,1},{1,0},{2,3},{3,2},{4,5},{5,4},{6,7},{7,6},{8,9},{9,8},{10,11... | collective-permute-start | bytes 393224 | tf_op jit(solution)/shard_map/ppermute | solution.py:19
  18.5 10.3 %copy-start.5 = (bf16[128,128]{1,0:T(8,128)(2,1)S(1)}, bf16[128,128]{1,0:T(8,128)(2,1)}, u32[]{:S(2)}) copy-start(bf16[128,128]{1,0:T(8,128)(2,1)} %refs_4_.2) | copy-start | bytes 98308
  19.6 6.8 %collective-permute-start.11 = (f32[128,128]{1,0:T(8,128)S(1)}, f32[128,128]{1,0:T(8,128)S(1)}, u32[]{:S(2)}, u32[]{:S(2)}) collective-permute-start(f32[128,128]{1,0:T(8,128)S(1)} %get-tuple-element.52), channel_id=1, source_target_pairs={{0,12},{1,13},{2,14},{3,15},{4,8},{5,9},{6,10},{7,11},{8,4},{9,5},... | collective-permute-start | bytes 196616 | tf_op jit(solution)/shard_map/ppermute | solution.py:19
  22.9 6.0 %collective-permute-start.12 = (f32[128,128]{1,0:T(8,128)S(1)}, f32[128,128]{1,0:T(8,128)S(1)}, u32[]{:S(2)}, u32[]{:S(2)}) collective-permute-start(f32[128,128]{1,0:T(8,128)S(1)} %get-tuple-element.53), channel_id=1, source_target_pairs={{0,4},{1,5},{2,6},{3,7},{4,0},{5,1},{6,2},{7,3},{8,12},{9,13},{10,... | collective-permute-start | bytes 196616 | tf_op jit(solution)/shard_map/ppermute | solution.py:19
  22.9 6.0 %collective-permute-start.13 = (f32[128,128]{1,0:T(8,128)S(1)}, f32[128,128]{1,0:T(8,128)S(1)}, u32[]{:S(2)}, u32[]{:S(2)}) collective-permute-start(f32[128,128]{1,0:T(8,128)S(1)} %get-tuple-element.54), channel_id=1, source_target_pairs={{0,8},{1,9},{2,10},{3,11},{4,12},{5,13},{6,14},{7,15},{8,0},{9,1},... | collective-permute-start | bytes 196616 | tf_op jit(solution)/shard_map/ppermute | solution.py:19
  28.9 6.0 %collective-permute-start.16 = (bf16[128,128]{1,0:T(8,128)(2,1)S(1)}, bf16[128,128]{1,0:T(8,128)(2,1)S(1)}, u32[]{:S(2)}, u32[]{:S(2)}) collective-permute-start(bf16[128,128]{1,0:T(8,128)(2,1)S(1)} %get-tuple-element.56.refs_3_), channel_id=1, source_target_pairs={{0,12},{1,13},{2,14},{3,15},{4,8},{5,9},{6,10},{7,11},{8,4},{9,5},... | collective-permute-start | bytes 98312 | tf_op jit(solution)/shard_map/ppermute | solution.py:19
  31.1 5.0 %collective-permute-start.15 = (bf16[128,128]{1,0:T(8,128)(2,1)S(1)}, bf16[128,128]{1,0:T(8,128)(2,1)S(1)}, u32[]{:S(2)}, u32[]{:S(2)}) collective-permute-start(bf16[128,128]{1,0:T(8,128)(2,1)S(1)} %get-tuple-element.56.refs_3_), channel_id=1, source_target_pairs={{0,8},{1,9},{2,10},{3,11},{4,12},{5,13},{6,14},{7,15},{8,0},{9,1},... | collective-permute-start | bytes 98312 | tf_op jit(solution)/shard_map/ppermute | solution.py:19
  31.6 4.4 %collective-permute-start.14 = (bf16[128,128]{1,0:T(8,128)(2,1)S(1)}, bf16[128,128]{1,0:T(8,128)(2,1)S(1)}, u32[]{:S(2)}, u32[]{:S(2)}) collective-permute-start(bf16[128,128]{1,0:T(8,128)(2,1)S(1)} %get-tuple-element.56.refs_3_), channel_id=1, source_target_pairs={{0,4},{1,5},{2,6},{3,7},{4,0},{5,1},{6,2},{7,3},{8,12},{9,13},{10,... | collective-permute-start | bytes 98312 | tf_op jit(solution)/shard_map/ppermute | solution.py:19
  36.5 7.1 %copy-start.2 = (f32[1,256,256]{2,1,0:T(8,128)S(1)}, f32[1,256,256]{2,1,0:T(8,128)}, u32[]{:S(2)}) copy-start(f32[1,256,256]{2,1,0:T(8,128)} %refs_3_.1) | copy-start | bytes 786436
  36.5 1.4 %collective-permute-start.18 = (f32[256,128]{1,0:T(8,128)S(1)}, f32[256,128]{1,0:T(8,128)S(1)}, u32[]{:S(2)}, u32[]{:S(2)}) collective-permute-start(f32[256,128]{1,0:T(8,128)S(1)} %get-tuple-element.60), channel_id=1, source_target_pairs={{0,1},{1,0},{2,3},{3,2},{4,5},{5,4},{6,7},{7,6},{8,9},{9,8},{10,11... | collective-permute-start | bytes 393224 | tf_op jit(solution)/shard_map/ppermute | solution.py:19
  36.6 2.9 %collective-permute-start.17 = (f32[256,128]{1,0:T(8,128)S(1)}, f32[256,128]{1,0:T(8,128)S(1)}, u32[]{:S(2)}, u32[]{:S(2)}) collective-permute-start(f32[256,128]{1,0:T(8,128)S(1)} %get-tuple-element.58), channel_id=1, source_target_pairs={{0,1},{1,0},{2,3},{3,2},{4,5},{5,4},{6,7},{7,6},{8,9},{9,8},{10,11... | collective-permute-start | bytes 393224 | tf_op jit(solution)/shard_map/ppermute | solution.py:19
  37.9 5.6 %copy-start.3 = (f32[256,128]{1,0:T(8,128)S(1)}, f32[256,128]{1,0:T(8,128)}, u32[]{:S(2)}) copy-start(f32[256,128]{1,0:T(8,128)} %refs_4_.3) | copy-start | bytes 393220
  37.9 5.6 %collective-permute-start.19 = (f32[256,128]{1,0:T(8,128)S(1)}, f32[256,128]{1,0:T(8,128)S(1)}, u32[]{:S(2)}, u32[]{:S(2)}) collective-permute-start(f32[256,128]{1,0:T(8,128)S(1)} %add.3), channel_id=1, source_target_pairs={{0,2},{1,3},{2,0},{3,1},{4,6},{5,7},{6,4},{7,5},{8,10},{9,11},{10,... | collective-permute-start | bytes 393224 | tf_op jit(solution)/shard_map/ppermute | solution.py:19

commit v4 on v3

--- a/solution.py
+++ b/solution.py
@@ -1,4 +1,5 @@
 import functools
+import math
 
 import jax
 import jax.numpy as jnp
@@ -10,9 +11,6 @@
 
 F32, BF16 = jnp.float32, jnp.bfloat16
 MIB = 1 << 20
-SUM_ORDER = (3, 1, 2, 0)
-GATHER_ORDER = (0, 1, 2, 3)
-ROW_ORDER = (0, 1, 2, 3)
 
 
 def swap(x, mask, size):
@@ -48,14 +46,6 @@
         else:
             pieces += [swap(pieces[0], digit[0], size)]
     return pieces
-
-
-def in_order(items, order):
-    return [items[order.index(n)] for n in range(len(items))] if len(order) == len(items) else list(items)
-
-
-def put(items, order):
-    return [items[n] for n in order] if len(order) == len(items) else list(items)
 
 
 def nbytes(*arrays):
@@ -87,7 +77,7 @@
 
 
 def predict_body(nrow, ncen, nweight, first, *refs):
-    rows, refs = in_order(refs[:nrow], ROW_ORDER), refs[nrow:]
+    rows, refs = refs[:nrow], refs[nrow:]
     blocks, refs = refs[:ncen], refs[ncen:]
     weights, refs = refs[:nweight], refs[nweight:]
     given, refs = ((), refs) if first else (refs[:nrow], refs[nrow:])
@@ -96,12 +86,8 @@
     centres = jnp.concatenate([block[...] for block in blocks])
     coefs = jnp.concatenate([weight[...].astype(BF16) for weight in weights])
     dims = (((1,), (1,)), ((), ()))
-    square = centres.astype(F32) ** 2
-    high = square.astype(BF16)
-    low = (square - high.astype(F32)).astype(BF16)
-    ones = jnp.ones((8, width), BF16)
-    norms = lax.dot_general(ones, high, dims, preferred_element_type=F32)
-    norms = (norms + lax.dot_general(ones, low, dims, preferred_element_type=F32))[:1]
+    norms = jnp.sum(centres.astype(F32) ** 2, axis=1, keepdims=True)
+    norms = jnp.transpose(jnp.broadcast_to(norms, (centres.shape[0], 128)))[:1]
 
     def tile(x, at):
         row_norms = jnp.sum(x.astype(F32) ** 2, axis=1, keepdims=True)
@@ -141,13 +127,13 @@
     shapes += [jax.ShapeDtypeStruct((x.shape[0], outs), F32) for x in rows]
     body = functools.partial(predict_body, len(rows), len(blocks), len(weights), not given)
     flops = flops or 2 * total * depth * (width + outs)
-    kernel, *sums = whole_call(body, shapes, [*put(rows, ROW_ORDER), *blocks, *weights, *given], flops=flops)
+    kernel, *sums = whole_call(body, shapes, [*rows, *blocks, *weights, *given], flops=flops)
     return kernel, sums
 
 
 def gradient_body(layout, npiece, nout, *refs):
     kernels, refs = refs[: len(layout)], refs[len(layout) :]
-    pieces, refs = in_order(refs[:npiece], GATHER_ORDER), refs[npiece:]
+    pieces, refs = refs[:npiece], refs[npiece:]
     *outs, residual = refs
     base = 0
     for piece in pieces:
@@ -187,21 +173,10 @@
     return whole_call(
         body,
         [out] * nout,
-        [*kernels, *put(pieces, GATHER_ORDER)],
+        [*kernels, *pieces],
         scratch=[pltpu.VMEM((total, columns), BF16)],
         flops=4 * total * count * columns,
     )
-
-
-def residual_body(npart, *refs):
-    *parts, targets, residual, half = refs
-    parts = in_order(parts, SUM_ORDER)
-    total = parts[0][...]
-    for part in parts[1:]:
-        total += part[...]
-    total -= targets[...].astype(F32)
-    residual[...] = total
-    half[...] = total.astype(BF16)
 
 
 def update_body(batch, npart, *refs):
@@ -233,31 +208,30 @@
     rows = relay_pieces(features, digits, size)
     if len(digits) == 1:
         rows[0] = own_rows
-    coefficients_ = coefficients
     far_parts = [send(part, far) for part in jnp.split(centres, 2)]
-    far_coef = send(coefficients_, far)
-    near = [send(centres, core)], [send(coefficients_, core)]
+    far_coef = send(coefficients, far)
+    near = [send(centres, core)], [send(coefficients, core)]
     own = own[:1], own[1:]
     kernel_a, sums_a = predict(rows, own, flops=4 * 10**9)
-    kernel_b, sums_b = predict(rows, near, sums_a, flops=None)
+    kernel_b, sums_b = predict(rows, near, sums_a)
     far_parts, far_coef, rows[-2] = lax.optimization_barrier((far_parts, far_coef, rows[-2]))
     distant = far_parts + [send(x, core) for x in far_parts], [far_coef, send(far_coef, core)]
     kernel_c, sums = predict(rows, distant, sums_b)
     far_kernels, far_layout = [kernel_c], ((0, 0, (0, 1)),)
     near_kernels, near_layout = [kernel_a, kernel_b], ((0, 0, (0,)), (0, 0, (1,)))
 
+    scale = 2.0 ** math.floor(math.log2(65504 / (5.05 * 4 * count)))
     for digit in reversed(digits):
         masks = masks_of(digit)
         if len(sums) == 1:
             sums = jnp.split(sums[0], len(masks))
-        terms = [sums[0]] + [send(part, m) for m, part in zip(masks[1:], sums[1:])]
-        sums = [functools.reduce(jnp.add, terms)] if digit is not digits[0] else terms
+        kind, factor = (jnp.float16, scale) if digit is digits[-1] else (F32, 1.0)
+        sent = [(factor * part).astype(kind) for part in sums[1:]]
+        got = [send(part, m).astype(F32) for m, part in zip(masks[1:], sent)]
+        sums = [sums[0] + functools.reduce(jnp.add, got) / factor]
+    residual = sums[0] - targets.astype(F32)
+    half = residual.astype(BF16)
     held = jax.ShapeDtypeStruct(targets.shape, F32)
-    residual, half = whole_call(
-        functools.partial(residual_body, len(sums)),
-        [held, jax.ShapeDtypeStruct(targets.shape, BF16)],
-        [*put(sums, SUM_ORDER), targets],
-    )
     residuals = gather_pieces(half, digits, size)
 
     layout = far_layout + tuple((r, c, tuple(o + 2 for o in out)) for r, c, out in near_layout)

time: 44.8 us -> 42.9 us (0.958)
  waiting for transfers between devices: 17.2 us -> 15.8 us
  Pallas kernels: 4 us -> 3.42 us
    ppermute x20, waiting for transfers between devices: 17.2 us -> 15.8 us  [swap(): return lax.ppermute(x, 'wide', [(i, i ^ mask) for i in range(size)])]
    pallas_call x7 -> x6, Pallas kernels: 4 us -> 3.42 us  [whole_call(): pl.pallas_call(body, out_shape=outs, in_specs=[pl.BlockSpec(memory_space=...]
  transfers between devices with their start and end apart: 20 -> 20, of which waited for: 10 -> 12; matrix products, arithmetic and copies ran while one was open for 2% -> 2% of each run, Pallas kernels for 3% -> 3%
where the time goes in v4:
time: 42.9 us; the launch traced here: 42.8 us
  starting transfers between devices  21.7 us (51%)
  waiting for transfers between devices  15.8 us (37%)
  Pallas kernels  3.42 us (8%)
  local copies, waits for them, and re-layouts  1.01 us (2%)
  between operations  0.81 us (2%)
    ppermute x20, starting transfers between devices, swap(): return lax.ppermute(x, 'wide', [(i, i ^ mask) for i in range(size)])  21.7 us
    ppermute x20, waiting for transfers between devices, swap(): return lax.ppermute(x, 'wide', [(i, i ^ mask) for i in range(size)])  15.8 us
    pallas_call x6, Pallas kernels, whole_call(): pl.pallas_call(body, out_shape=outs, in_specs=[pl.BlockSpec(memory_space=...  3.42 us
    split x1, local copies, waits for them, and re-layouts, shards(): far_parts = [send(part, far) for part in jnp.split(centres, 2)]  0.98 us
  transfers between devices with their start and end apart: 20, of which 12 were waited for; matrix products, arithmetic and copies ran while one was open for 2% of the time, Pallas kernels for 3%

profile of v4, /device:TPU:0, one launch (start us, length us, event | category | flops | bytes accessed | tf_op | source)
XLA Modules:
  0.0 42.8 jit_solution(8110148051826812993)
XLA Ops:
  0.7 4.1 %collective-permute-start.4 = (bf16[128,512]{1,0:T(8,128)(2,1)}, bf16[128,512]{1,0:T(8,128)(2,1)S(1)}, u32[]{:S(2)}, u32[]{:S(2)}) collective-permute-start(bf16[128,512]{1,0:T(8,128)(2,1)} %features.1), channel_id=1, source_target_pairs={{0,8},{1,9},{2,10},{3,11},{4,12},{5,13},{6,14},{7,15},{8,0},{9,1},... | collective-permute-start | bytes 393224 | tf_op jit(solution)/shard_map/ppermute | solution.py:17
  4.8 1.5 %collective-permute-start.3 = (f32[256,128]{1,0:T(8,128)}, f32[256,128]{1,0:T(8,128)S(1)}, u32[]{:S(2)}, u32[]{:S(2)}) collective-permute-start(f32[256,128]{1,0:T(8,128)} %refs_5_.1), channel_id=1, source_target_pairs={{0,2},{1,3},{2,0},{3,1},{4,6},{5,7},{6,4},{7,5},{8,10},{9,11},{10,... | collective-permute-start | bytes 393224 | tf_op jit(solution)/shard_map/ppermute | solution.py:17
  6.3 1.0 %fusion.1 = (bf16[128,512]{1,0:T(8,128)(2,1)S(1)}, bf16[128,512]{1,0:T(8,128)(2,1)S(1)}) fusion(bf16[256,512]{1,0:T(8,128)(2,1)} %centres.1), kind=kLoop, calls=%fused_computation.5 | loop fusion | bytes 524288 | tf_op jit(solution)/shard_map/split | solution.py:211
  7.3 0.6 %collective-permute-start.2 = (bf16[128,512]{1,0:T(8,128)(2,1)S(1)}, bf16[128,512]{1,0:T(8,128)(2,1)S(1)}, u32[]{:S(2)}, u32[]{:S(2)}) collective-permute-start(bf16[128,512]{1,0:T(8,128)(2,1)S(1)} %get-tuple-element.63), channel_id=1, source_target_pairs={{0,2},{1,3},{2,0},{3,1},{4,6},{5,7},{6,4},{7,5},{8,10},{9,11},{10,... | collective-permute-start | bytes 393224 | tf_op jit(solution)/shard_map/ppermute | solution.py:17
  7.8 1.5 %collective-permute-start.1 = (bf16[128,512]{1,0:T(8,128)(2,1)S(1)}, bf16[128,512]{1,0:T(8,128)(2,1)S(1)}, u32[]{:S(2)}, u32[]{:S(2)}) collective-permute-start(bf16[128,512]{1,0:T(8,128)(2,1)S(1)} %get-tuple-element.64), channel_id=1, source_target_pairs={{0,2},{1,3},{2,0},{3,1},{4,6},{5,7},{6,4},{7,5},{8,10},{9,11},{10,... | collective-permute-start | bytes 393224 | tf_op jit(solution)/shard_map/ppermute | solution.py:17
  9.4 1.6 %collective-permute-start = (bf16[128,512]{1,0:T(8,128)(2,1)S(1)}, bf16[128,512]{1,0:T(8,128)(2,1)S(1)}, u32[]{:S(2)}, u32[]{:S(2)}) collective-permute-start(bf16[128,512]{1,0:T(8,128)(2,1)S(1)} %copy-done.4), channel_id=1, source_target_pairs={{0,4},{1,5},{2,6},{3,7},{4,0},{5,1},{6,2},{7,3},{8,12},{9,13},{10,... | collective-permute-start | bytes 393224 | tf_op jit(solution)/shard_map/ppermute | solution.py:17
  10.9 0.4 collective-permute-done.4.refs_2_
  11.3 0.8 %collective-permute-start.5 = (bf16[128,512]{1,0:T(8,128)(2,1)S(1)}, bf16[128,512]{1,0:T(8,128)(2,1)S(1)}, u32[]{:S(2)}, u32[]{:S(2)}) collective-permute-start(bf16[128,512]{1,0:T(8,128)(2,1)S(1)} %collective-permute-done.4.refs_2_), channel_id=1, source_target_pairs={{0,4},{1,5},{2,6},{3,7},{4,0},{5,1},{6,2},{7,3},{8,12},{9,13},{10,... | collective-permute-start | bytes 393224 | tf_op jit(solution)/shard_map/ppermute | solution.py:17
  12.3 1.5 %collective-permute-done.2.refs_5_ = bf16[128,512]{1,0:T(8,128)(2,1)S(1)} collective-permute-done((bf16[128,512]{1,0:T(8,128)(2,1)S(1)}, bf16[128,512]{1,0:T(8,128)(2,1)S(1)}, u32[]{:S(2)}, u32[]{:S(2)}) %collective-permute-start.2) | collective-permute-done | bytes 131104 | tf_op jit(solution)/shard_map/ppermute | solution.py:17
  13.8 1.8 %collective-permute-done.1.refs_4_ = bf16[128,512]{1,0:T(8,128)(2,1)S(1)} collective-permute-done((bf16[128,512]{1,0:T(8,128)(2,1)S(1)}, bf16[128,512]{1,0:T(8,128)(2,1)S(1)}, u32[]{:S(2)}, u32[]{:S(2)}) %collective-permute-start.1) | collective-permute-done | bytes 131104 | tf_op jit(solution)/shard_map/ppermute | solution.py:17
  15.6 0.5 %collective-permute-start.7 = (bf16[128,512]{1,0:T(8,128)(2,1)S(1)}, bf16[128,512]{1,0:T(8,128)(2,1)S(1)}, u32[]{:S(2)}, u32[]{:S(2)}) collective-permute-start(bf16[128,512]{1,0:T(8,128)(2,1)S(1)} %collective-permute-done.2.refs_5_), channel_id=1, source_target_pairs={{0,1},{1,0},{2,3},{3,2},{4,5},{5,4},{6,7},{7,6},{8,9},{9,8},{10,11... | collective-permute-start | bytes 393224 | tf_op jit(solution)/shard_map/ppermute | solution.py:17
  16.1 1.1 %collective-permute-done.5.refs_3_ = bf16[128,512]{1,0:T(8,128)(2,1)S(1)} collective-permute-done((bf16[128,512]{1,0:T(8,128)(2,1)S(1)}, bf16[128,512]{1,0:T(8,128)(2,1)S(1)}, u32[]{:S(2)}, u32[]{:S(2)}) %collective-permute-start.5) | collective-permute-done | bytes 131104 | tf_op jit(solution)/shard_map/ppermute | solution.py:17
  17.1 0.5 %shard_map.86 = (bf16[512,256]{1,0:T(8,128)(2,1)S(1)}, f32[128,128]{1,0:T(8,128)S(1)}, f32[128,128]{1,0:T(8,128)S(1)}, f32[128,128]{1,0:T(8,128)S(1)}, f32[128,128]{1,0:T(8,128)S(1)}) custom-call(bf16[128,512]{1,0:T(8,128)(2,1)S(1)} %get-tuple-element.32.refs_0_, bf16[128,512]{1,0:T(8,128)(2,1)S(1)} %collective-permute-done.refs_1_, ...), custom_call_target="tpu_custom_call" | custom-call | flops 4000000000 | bytes 1376256 | tf_op jit(solution)/shard_map/pallas_call | solution.py:57
  17.7 0.5 %shard_map.87 = (bf16[512,256]{1,0:T(8,128)(2,1)S(1)}, f32[128,128]{1,0:T(8,128)S(1)}, f32[128,128]{1,0:T(8,128)S(1)}, f32[128,128]{1,0:T(8,128)S(1)}, f32[128,128]{1,0:T(8,128)S(1)}) custom-call(bf16[128,512]{1,0:T(8,128)(2,1)S(1)} %get-tuple-element.32.refs_0_, bf16[128,512]{1,0:T(8,128)(2,1)S(1)} %collective-permute-done.refs_1_, ...), custom_call_target="tpu_custom_call" | custom-call | flops 167772160 | bytes 1703936 | tf_op jit(solution)/shard_map/pallas_call | solution.py:57
  18.3 0.2 collective-permute-done.8.refs_9_
  18.5 0.7 %shard_map.88 = (bf16[512,512]{1,0:T(8,128)(2,1)S(1)}, f32[128,128]{1,0:T(8,128)S(1)}, f32[128,128]{1,0:T(8,128)S(1)}, f32[128,128]{1,0:T(8,128)S(1)}, f32[128,128]{1,0:T(8,128)S(1)}) custom-call(bf16[128,512]{1,0:T(8,128)(2,1)S(1)} %get-tuple-element.32.refs_0_, bf16[128,512]{1,0:T(8,128)(2,1)S(1)} %collective-permute-done.refs_1_, ...), custom_call_target="tpu_custom_call" | custom-call | flops 335544320 | bytes 2359296 | tf_op jit(solution)/shard_map/pallas_call | solution.py:57
  19.3 3.3 %collective-permute-start.13 = (f16[128,128]{1,0:T(8,128)(2,1)S(1)}, f16[128,128]{1,0:T(8,128)(2,1)S(1)}, u32[]{:S(2)}, u32[]{:S(2)}) collective-permute-start(f16[128,128]{1,0:T(8,128)(2,1)S(1)} %multiply_convert_fusion), channel_id=1, source_target_pairs={{0,12},{1,13},{2,14},{3,15},{4,8},{5,9},{6,10},{7,11},{8,4},{9,5},... | collective-permute-start | bytes 98312 | tf_op jit(solution)/shard_map/ppermute | solution.py:17
  22.6 1.2 %collective-permute-start.11 = (f16[128,128]{1,0:T(8,128)(2,1)S(1)}, f16[128,128]{1,0:T(8,128)(2,1)S(1)}, u32[]{:S(2)}, u32[]{:S(2)}) collective-permute-start(f16[128,128]{1,0:T(8,128)(2,1)S(1)} %multiply_convert_fusion.2), channel_id=1, source_target_pairs={{0,4},{1,5},{2,6},{3,7},{4,0},{5,1},{6,2},{7,3},{8,12},{9,13},{10,... | collective-permute-start | bytes 98312 | tf_op jit(solution)/shard_map/ppermute | solution.py:17
  23.7 1.6 %collective-permute-done.13 = f16[128,128]{1,0:T(8,128)(2,1)S(1)} collective-permute-done((f16[128,128]{1,0:T(8,128)(2,1)S(1)}, f16[128,128]{1,0:T(8,128)(2,1)S(1)}, u32[]{:S(2)}, u32[]{:S(2)}) %collective-permute-start.13) | collective-permute-done | bytes 32800 | tf_op jit(solution)/shard_map/ppermute | solution.py:17
  25.3 2.1 %collective-permute-done.12 = f16[128,128]{1,0:T(8,128)(2,1)S(1)} collective-permute-done((f16[128,128]{1,0:T(8,128)(2,1)S(1)}, f16[128,128]{1,0:T(8,128)(2,1)S(1)}, u32[]{:S(2)}, u32[]{:S(2)}) %collective-permute-start.12) | collective-permute-done | bytes 32800 | tf_op jit(solution)/shard_map/ppermute | solution.py:17
  27.4 1.7 %collective-permute-start.16 = (bf16[128,128]{1,0:T(8,128)(2,1)S(1)}, bf16[128,128]{1,0:T(8,128)(2,1)S(1)}, u32[]{:S(2)}, u32[]{:S(2)}) collective-permute-start(bf16[128,128]{1,0:T(8,128)(2,1)S(1)} %get-tuple-element.61.refs_3_), channel_id=1, source_target_pairs={{0,12},{1,13},{2,14},{3,15},{4,8},{5,9},{6,10},{7,11},{8,4},{9,5},... | collective-permute-start | bytes 98312 | tf_op jit(solution)/shard_map/ppermute | solution.py:17
  29.1 0.5 %collective-permute-start.15 = (bf16[128,128]{1,0:T(8,128)(2,1)S(1)}, bf16[128,128]{1,0:T(8,128)(2,1)S(1)}, u32[]{:S(2)}, u32[]{:S(2)}) collective-permute-start(bf16[128,128]{1,0:T(8,128)(2,1)S(1)} %get-tuple-element.61.refs_3_), channel_id=1, source_target_pairs={{0,8},{1,9},{2,10},{3,11},{4,12},{5,13},{6,14},{7,15},{8,0},{9,1},... | collective-permute-start | bytes 98312 | tf_op jit(solution)/shard_map/ppermute | solution.py:17
  29.6 2.3 %collective-permute-start.14 = (bf16[128,128]{1,0:T(8,128)(2,1)S(1)}, bf16[128,128]{1,0:T(8,128)(2,1)S(1)}, u32[]{:S(2)}, u32[]{:S(2)}) collective-permute-start(bf16[128,128]{1,0:T(8,128)(2,1)S(1)} %get-tuple-element.61.refs_3_), channel_id=1, source_target_pairs={{0,4},{1,5},{2,6},{3,7},{4,0},{5,1},{6,2},{7,3},{8,12},{9,13},{10,... | collective-permute-start | bytes 98312 | tf_op jit(solution)/shard_map/ppermute | solution.py:17
  31.9 1.5 %collective-permute-done.16.refs_6_ = bf16[128,128]{1,0:T(8,128)(2,1)S(1)} collective-permute-done((bf16[128,128]{1,0:T(8,128)(2,1)S(1)}, bf16[128,128]{1,0:T(8,128)(2,1)S(1)}, u32[]{:S(2)}, u32[]{:S(2)}) %collective-permute-start.16) | collective-permute-done | bytes 32800 | tf_op jit(solution)/shard_map/ppermute | solution.py:17
  33.4 0.6 %collective-permute-done.15.refs_5_ = bf16[128,128]{1,0:T(8,128)(2,1)S(1)} collective-permute-done((bf16[128,128]{1,0:T(8,128)(2,1)S(1)}, bf16[128,128]{1,0:T(8,128)(2,1)S(1)}, u32[]{:S(2)}, u32[]{:S(2)}) %collective-permute-start.15) | collective-permute-done | bytes 32800 | tf_op jit(solution)/shard_map/ppermute | solution.py:17
  34.1 0.1 collective-permute-done.14.refs_4_
  34.1 0.5 %shard_map.89 = (f32[256,128]{1,0:T(8,128)S(1)}, f32[256,128]{1,0:T(8,128)S(1)}, f32[256,128]{1,0:T(8,128)S(1)}, f32[256,128]{1,0:T(8,128)S(1)}) custom-call(bf16[512,512]{1,0:T(8,128)(2,1)S(1)} %get-tuple-element.47.refs_0_, bf16[512,256]{1,0:T(8,128)(2,1)S(1)} %get-tuple-element.48.refs_1_, bf16[512,256]{1,0:T(8,128)(2,1)S(1)} %get-tuple-element.49.refs_2_, ...), custom_call_target="tpu_custom_call" | custom-call | flops 67108864 | bytes 1703936 | tf_op jit(solution)/shard_map/pallas_call | solution.py:57
  34.7 0.5 %collective-permute-start.17 = (f32[256,128]{1,0:T(8,128)S(1)}, f32[256,128]{1,0:T(8,128)S(1)}, u32[]{:S(2)}, u32[]{:S(2)}) collective-permute-start(f32[256,128]{1,0:T(8,128)S(1)} %get-tuple-element.55), channel_id=1, source_target_pairs={{0,1},{1,0},{2,3},{3,2},{4,5},{5,4},{6,7},{7,6},{8,9},{9,8},{10,11... | collective-permute-start | bytes 393224 | tf_op jit(solution)/shard_map/ppermute | solution.py:17
  35.2 0.8 %collective-permute-done.18 = f32[256,128]{1,0:T(8,128)S(1)} collective-permute-done((f32[256,128]{1,0:T(8,128)S(1)}, f32[256,128]{1,0:T(8,128)S(1)}, u32[]{:S(2)}, u32[]{:S(2)}) %collective-permute-start.18) | collective-permute-done | bytes 131104 | tf_op jit(solution)/shard_map/ppermute | solution.py:17
  36.1 1.5 %collective-permute-start.19 = (f32[256,128]{1,0:T(8,128)S(1)}, f32[256,128]{1,0:T(8,128)S(1)}, u32[]{:S(2)}, u32[]{:S(2)}) collective-permute-start(f32[256,128]{1,0:T(8,128)S(1)} %add.15), channel_id=1, source_target_pairs={{0,2},{1,3},{2,0},{3,1},{4,6},{5,7},{6,4},{7,5},{8,10},{9,11},{10,... | collective-permute-start | bytes 393224 | tf_op jit(solution)/shard_map/ppermute | solution.py:17
  37.6 4.1 %collective-permute-done.19.refs_2_ = f32[256,128]{1,0:T(8,128)S(1)} collective-permute-done((f32[256,128]{1,0:T(8,128)S(1)}, f32[256,128]{1,0:T(8,128)S(1)}, u32[]{:S(2)}, u32[]{:S(2)}) %collective-permute-start.19) | collective-permute-done | bytes 131104 | tf_op jit(solution)/shard_map/ppermute | solution.py:17
  41.7 1.1 %shard_map.90 = (f32[256,128]{1,0:T(8,128)}, f32[256,128]{1,0:T(8,128)}, f32[128,128]{1,0:T(8,128)}) custom-call(f32[256,128]{1,0:T(8,128)S(1)} %get-tuple-element.54.refs_0_, f32[256,128]{1,0:T(8,128)S(1)} %collective-permute-done.17.refs_1_, f32[256,128]{1,0:T(8,128)S(1)} %collective-permute-done.19.refs_2_, f32[1,256,256]{2,1,0:T(8,128)S(1)} %copy-done.2, ...), custom_call_target="tpu_custom_call" | custom-call | bytes 1310720 | tf_op jit(solution)/shard_map/pallas_call | solution.py:57
  (32 shorter events, 0.3 us)
Async XLA Ops:
  0.6 8.7 %copy-start.4 = (bf16[128,512]{1,0:T(8,128)(2,1)S(1)}, bf16[128,512]{1,0:T(8,128)(2,1)}, u32[]{:S(2)}) copy-start(bf16[128,512]{1,0:T(8,128)(2,1)} %features.1) | copy-start | bytes 393220
  0.6 11.5 %copy-start.1 = (f32[256,128]{1,0:T(8,128)S(1)}, f32[256,128]{1,0:T(8,128)}, u32[]{:S(2)}) copy-start(f32[256,128]{1,0:T(8,128)} %refs_5_.1) | copy-start | bytes 393220
  0.7 11.5 %copy-start = (bf16[256,512]{1,0:T(8,128)(2,1)S(1)}, bf16[256,512]{1,0:T(8,128)(2,1)}, u32[]{:S(2)}) copy-start(bf16[256,512]{1,0:T(8,128)(2,1)} %centres.1) | copy-start | bytes 786436
  0.7 10.7 %collective-permute-start.4 = (bf16[128,512]{1,0:T(8,128)(2,1)}, bf16[128,512]{1,0:T(8,128)(2,1)S(1)}, u32[]{:S(2)}, u32[]{:S(2)}) collective-permute-start(bf16[128,512]{1,0:T(8,128)(2,1)} %features.1), channel_id=1, source_target_pairs={{0,8},{1,9},{2,10},{3,11},{4,12},{5,13},{6,14},{7,15},{8,0},{9,1},... | collective-permute-start | bytes 393224 | tf_op jit(solution)/shard_map/ppermute | solution.py:17
  4.8 7.4 %collective-permute-start.3 = (f32[256,128]{1,0:T(8,128)}, f32[256,128]{1,0:T(8,128)S(1)}, u32[]{:S(2)}, u32[]{:S(2)}) collective-permute-start(f32[256,128]{1,0:T(8,128)} %refs_5_.1), channel_id=1, source_target_pairs={{0,2},{1,3},{2,0},{3,1},{4,6},{5,7},{6,4},{7,5},{8,10},{9,11},{10,... | collective-permute-start | bytes 393224 | tf_op jit(solution)/shard_map/ppermute | solution.py:17
  7.3 6.5 %collective-permute-start.2 = (bf16[128,512]{1,0:T(8,128)(2,1)S(1)}, bf16[128,512]{1,0:T(8,128)(2,1)S(1)}, u32[]{:S(2)}, u32[]{:S(2)}) collective-permute-start(bf16[128,512]{1,0:T(8,128)(2,1)S(1)} %get-tuple-element.63), channel_id=1, source_target_pairs={{0,2},{1,3},{2,0},{3,1},{4,6},{5,7},{6,4},{7,5},{8,10},{9,11},{10,... | collective-permute-start | bytes 393224 | tf_op jit(solution)/shard_map/ppermute | solution.py:17
  7.8 7.7 %collective-permute-start.1 = (bf16[128,512]{1,0:T(8,128)(2,1)S(1)}, bf16[128,512]{1,0:T(8,128)(2,1)S(1)}, u32[]{:S(2)}, u32[]{:S(2)}) collective-permute-start(bf16[128,512]{1,0:T(8,128)(2,1)S(1)} %get-tuple-element.64), channel_id=1, source_target_pairs={{0,2},{1,3},{2,0},{3,1},{4,6},{5,7},{6,4},{7,5},{8,10},{9,11},{10,... | collective-permute-start | bytes 393224 | tf_op jit(solution)/shard_map/ppermute | solution.py:17
  9.4 6.2 %collective-permute-start = (bf16[128,512]{1,0:T(8,128)(2,1)S(1)}, bf16[128,512]{1,0:T(8,128)(2,1)S(1)}, u32[]{:S(2)}, u32[]{:S(2)}) collective-permute-start(bf16[128,512]{1,0:T(8,128)(2,1)S(1)} %copy-done.4), channel_id=1, source_target_pairs={{0,4},{1,5},{2,6},{3,7},{4,0},{5,1},{6,2},{7,3},{8,12},{9,13},{10,... | collective-permute-start | bytes 393224 | tf_op jit(solution)/shard_map/ppermute | solution.py:17
  11.3 5.8 %collective-permute-start.5 = (bf16[128,512]{1,0:T(8,128)(2,1)S(1)}, bf16[128,512]{1,0:T(8,128)(2,1)S(1)}, u32[]{:S(2)}, u32[]{:S(2)}) collective-permute-start(bf16[128,512]{1,0:T(8,128)(2,1)S(1)} %collective-permute-done.4.refs_2_), channel_id=1, source_target_pairs={{0,4},{1,5},{2,6},{3,7},{4,0},{5,1},{6,2},{7,3},{8,12},{9,13},{10,... | collective-permute-start | bytes 393224 | tf_op jit(solution)/shard_map/ppermute | solution.py:17
  12.2 5.5 %collective-permute-start.10 = (f32[256,128]{1,0:T(8,128)S(1)}, f32[256,128]{1,0:T(8,128)S(1)}, u32[]{:S(2)}, u32[]{:S(2)}) collective-permute-start(f32[256,128]{1,0:T(8,128)S(1)} %copy-done.1), channel_id=1, source_target_pairs={{0,1},{1,0},{2,3},{3,2},{4,5},{5,4},{6,7},{7,6},{8,9},{9,8},{10,11... | collective-permute-start | bytes 393224 | tf_op jit(solution)/shard_map/ppermute | solution.py:17
  13.8 3.9 %collective-permute-start.9 = (bf16[256,512]{1,0:T(8,128)(2,1)S(1)}, bf16[256,512]{1,0:T(8,128)(2,1)S(1)}, u32[]{:S(2)}, u32[]{:S(2)}) collective-permute-start(bf16[256,512]{1,0:T(8,128)(2,1)S(1)} %copy-done), channel_id=1, source_target_pairs={{0,1},{1,0},{2,3},{3,2},{4,5},{5,4},{6,7},{7,6},{8,9},{9,8},{10,11... | collective-permute-start | bytes 786440 | tf_op jit(solution)/shard_map/ppermute | solution.py:17
  15.6 2.7 %collective-permute-start.6 = (bf16[128,512]{1,0:T(8,128)(2,1)S(1)}, bf16[128,512]{1,0:T(8,128)(2,1)S(1)}, u32[]{:S(2)}, u32[]{:S(2)}) collective-permute-start(bf16[128,512]{1,0:T(8,128)(2,1)S(1)} %collective-permute-done.1.refs_4_), channel_id=1, source_target_pairs={{0,1},{1,0},{2,3},{3,2},{4,5},{5,4},{6,7},{7,6},{8,9},{9,8},{10,11... | collective-permute-start | bytes 393224 | tf_op jit(solution)/shard_map/ppermute | solution.py:17
  15.6 2.7 %collective-permute-start.7 = (bf16[128,512]{1,0:T(8,128)(2,1)S(1)}, bf16[128,512]{1,0:T(8,128)(2,1)S(1)}, u32[]{:S(2)}, u32[]{:S(2)}) collective-permute-start(bf16[128,512]{1,0:T(8,128)(2,1)S(1)} %collective-permute-done.2.refs_5_), channel_id=1, source_target_pairs={{0,1},{1,0},{2,3},{3,2},{4,5},{5,4},{6,7},{7,6},{8,9},{9,8},{10,11... | collective-permute-start | bytes 393224 | tf_op jit(solution)/shard_map/ppermute | solution.py:17
  17.1 1.3 %collective-permute-start.8 = (f32[256,128]{1,0:T(8,128)S(1)}, f32[256,128]{1,0:T(8,128)S(1)}, u32[]{:S(2)}, u32[]{:S(2)}) collective-permute-start(f32[256,128]{1,0:T(8,128)S(1)} %collective-permute-done.3.refs_8_), channel_id=1, source_target_pairs={{0,1},{1,0},{2,3},{3,2},{4,5},{5,4},{6,7},{7,6},{8,9},{9,8},{10,11... | collective-permute-start | bytes 393224 | tf_op jit(solution)/shard_map/ppermute | solution.py:17
  19.3 8.1 %copy-start.5 = (bf16[128,128]{1,0:T(8,128)(2,1)S(1)}, bf16[128,128]{1,0:T(8,128)(2,1)}, u32[]{:S(2)}) copy-start(bf16[128,128]{1,0:T(8,128)(2,1)} %param.8) | copy-start | bytes 98308
  19.3 6.0 %collective-permute-start.13 = (f16[128,128]{1,0:T(8,128)(2,1)S(1)}, f16[128,128]{1,0:T(8,128)(2,1)S(1)}, u32[]{:S(2)}, u32[]{:S(2)}) collective-permute-start(f16[128,128]{1,0:T(8,128)(2,1)S(1)} %multiply_convert_fusion), channel_id=1, source_target_pairs={{0,12},{1,13},{2,14},{3,15},{4,8},{5,9},{6,10},{7,11},{8,4},{9,5},... | collective-permute-start | bytes 98312 | tf_op jit(solution)/shard_map/ppermute | solution.py:17
  22.6 4.8 %collective-permute-start.12 = (f16[128,128]{1,0:T(8,128)(2,1)S(1)}, f16[128,128]{1,0:T(8,128)(2,1)S(1)}, u32[]{:S(2)}, u32[]{:S(2)}) collective-permute-start(f16[128,128]{1,0:T(8,128)(2,1)S(1)} %multiply_convert_fusion.1), channel_id=1, source_target_pairs={{0,8},{1,9},{2,10},{3,11},{4,12},{5,13},{6,14},{7,15},{8,0},{9,1},... | collective-permute-start | bytes 98312 | tf_op jit(solution)/shard_map/ppermute | solution.py:17
  22.6 4.8 %collective-permute-start.11 = (f16[128,128]{1,0:T(8,128)(2,1)S(1)}, f16[128,128]{1,0:T(8,128)(2,1)S(1)}, u32[]{:S(2)}, u32[]{:S(2)}) collective-permute-start(f16[128,128]{1,0:T(8,128)(2,1)S(1)} %multiply_convert_fusion.2), channel_id=1, source_target_pairs={{0,4},{1,5},{2,6},{3,7},{4,0},{5,1},{6,2},{7,3},{8,12},{9,13},{10,... | collective-permute-start | bytes 98312 | tf_op jit(solution)/shard_map/ppermute | solution.py:17
  27.4 6.0 %collective-permute-start.16 = (bf16[128,128]{1,0:T(8,128)(2,1)S(1)}, bf16[128,128]{1,0:T(8,128)(2,1)S(1)}, u32[]{:S(2)}, u32[]{:S(2)}) collective-permute-start(bf16[128,128]{1,0:T(8,128)(2,1)S(1)} %get-tuple-element.61.refs_3_), channel_id=1, source_target_pairs={{0,12},{1,13},{2,14},{3,15},{4,8},{5,9},{6,10},{7,11},{8,4},{9,5},... | collective-permute-start | bytes 98312 | tf_op jit(solution)/shard_map/ppermute | solution.py:17
  29.1 4.9 %collective-permute-start.15 = (bf16[128,128]{1,0:T(8,128)(2,1)S(1)}, bf16[128,128]{1,0:T(8,128)(2,1)S(1)}, u32[]{:S(2)}, u32[]{:S(2)}) collective-permute-start(bf16[128,128]{1,0:T(8,128)(2,1)S(1)} %get-tuple-element.61.refs_3_), channel_id=1, source_target_pairs={{0,8},{1,9},{2,10},{3,11},{4,12},{5,13},{6,14},{7,15},{8,0},{9,1},... | collective-permute-start | bytes 98312 | tf_op jit(solution)/shard_map/ppermute | solution.py:17
  29.6 4.5 %collective-permute-start.14 = (bf16[128,128]{1,0:T(8,128)(2,1)S(1)}, bf16[128,128]{1,0:T(8,128)(2,1)S(1)}, u32[]{:S(2)}, u32[]{:S(2)}) collective-permute-start(bf16[128,128]{1,0:T(8,128)(2,1)S(1)} %get-tuple-element.61.refs_3_), channel_id=1, source_target_pairs={{0,4},{1,5},{2,6},{3,7},{4,0},{5,1},{6,2},{7,3},{8,12},{9,13},{10,... | collective-permute-start | bytes 98312 | tf_op jit(solution)/shard_map/ppermute | solution.py:17
  34.6 7.1 %copy-start.2 = (f32[1,256,256]{2,1,0:T(8,128)S(1)}, f32[1,256,256]{2,1,0:T(8,128)}, u32[]{:S(2)}) copy-start(f32[1,256,256]{2,1,0:T(8,128)} %refs_3_.1) | copy-start | bytes 786436
  34.6 1.4 %collective-permute-start.18 = (f32[256,128]{1,0:T(8,128)S(1)}, f32[256,128]{1,0:T(8,128)S(1)}, u32[]{:S(2)}, u32[]{:S(2)}) collective-permute-start(f32[256,128]{1,0:T(8,128)S(1)} %get-tuple-element.57), channel_id=1, source_target_pairs={{0,1},{1,0},{2,3},{3,2},{4,5},{5,4},{6,7},{7,6},{8,9},{9,8},{10,11... | collective-permute-start | bytes 393224 | tf_op jit(solution)/shard_map/ppermute | solution.py:17
  34.7 2.9 %collective-permute-start.17 = (f32[256,128]{1,0:T(8,128)S(1)}, f32[256,128]{1,0:T(8,128)S(1)}, u32[]{:S(2)}, u32[]{:S(2)}) collective-permute-start(f32[256,128]{1,0:T(8,128)S(1)} %get-tuple-element.55), channel_id=1, source_target_pairs={{0,1},{1,0},{2,3},{3,2},{4,5},{5,4},{6,7},{7,6},{8,9},{9,8},{10,11... | collective-permute-start | bytes 393224 | tf_op jit(solution)/shard_map/ppermute | solution.py:17
  36.1 5.6 %copy-start.3 = (f32[256,128]{1,0:T(8,128)S(1)}, f32[256,128]{1,0:T(8,128)}, u32[]{:S(2)}) copy-start(f32[256,128]{1,0:T(8,128)} %refs_4_.1) | copy-start | bytes 393220
  36.1 5.6 %collective-permute-start.19 = (f32[256,128]{1,0:T(8,128)S(1)}, f32[256,128]{1,0:T(8,128)S(1)}, u32[]{:S(2)}, u32[]{:S(2)}) collective-permute-start(f32[256,128]{1,0:T(8,128)S(1)} %add.15), channel_id=1, source_target_pairs={{0,2},{1,3},{2,0},{3,1},{4,6},{5,7},{6,4},{7,5},{8,10},{9,11},{10,... | collective-permute-start | bytes 393224 | tf_op jit(solution)/shard_map/ppermute | solution.py:17

commit v5 on v4

--- a/solution.py
+++ b/solution.py
@@ -131,14 +131,17 @@
     return kernel, sums
 
 
-def gradient_body(layout, npiece, nout, *refs):
+def gradient_body(layout, npiece, first, *refs):
     kernels, refs = refs[: len(layout)], refs[len(layout) :]
     pieces, refs = refs[:npiece], refs[npiece:]
-    *outs, residual = refs
-    base = 0
-    for piece in pieces:
-        residual[base : base + piece.shape[0], :] = piece[...]
-        base += piece.shape[0]
+    if first:
+        *outs, residual = refs
+        base = 0
+        for piece in [pieces[0], *pieces[:0:-1]]:
+            residual[base : base + piece.shape[0], :] = piece[...]
+            base += piece.shape[0]
+    else:
+        outs, residual = refs, pieces[0]
     started = set()
     for kernel, (first_row, first_block, blocks) in zip(kernels, layout):
         rows, order = kernel.shape[0], outs[0].shape[0]
@@ -165,18 +168,13 @@
                     outs[out][...] += term(i)
 
 
-def gradients(kernels, layout, pieces, count, nout=2):
+def gradients(kernels, layout, pieces, count):
     total = sum(p.shape[0] for p in pieces)
     columns = pieces[0].shape[1]
     out = jax.ShapeDtypeStruct((count, columns), F32)
-    body = functools.partial(gradient_body, layout, len(pieces), nout)
-    return whole_call(
-        body,
-        [out] * nout,
-        [*kernels, *pieces],
-        scratch=[pltpu.VMEM((total, columns), BF16)],
-        flops=4 * total * count * columns,
-    )
+    joined = [jax.ShapeDtypeStruct((total, columns), BF16)] if len(pieces) > 1 else []
+    body = functools.partial(gradient_body, layout, len(pieces), len(pieces) > 1)
+    return whole_call(body, [out, out] + joined, [*kernels, pieces[0], *pieces[:0:-1]], flops=4 * total * count * columns)
 
 
 def update_body(batch, npart, *refs):
@@ -234,10 +232,10 @@
     held = jax.ShapeDtypeStruct(targets.shape, F32)
     residuals = gather_pieces(half, digits, size)
 
-    layout = far_layout + tuple((r, c, tuple(o + 2 for o in out)) for r, c, out in near_layout)
-    far_keep, far_give, keep, give = gradients(far_kernels + near_kernels, layout, residuals, count, 4)
-    far_got, got = send(far_give, core), send(give, core)
-    parts = [keep, got, send(far_keep + far_got, far)]
+    far_keep, far_give, joined = gradients(far_kernels, far_layout, residuals, count)
+    arrived = send(far_keep + send(far_give, core), far)
+    keep, give = gradients(near_kernels, near_layout, [joined], count)
+    parts = [keep, send(give, core), arrived]
     out = jax.ShapeDtypeStruct(momentum.shape, F32)
     new_momentum, new_coefficients, residual = whole_call(
         functools.partial(update_body, batch, len(parts)),

time: 42.9 us -> 42.9 us (level)
    pallas_call x6 -> x7, Pallas kernels: 3.42 us -> 3.63 us  [whole_call(): pl.pallas_call(body, out_shape=outs, in_specs=[pl.BlockSpec(memory_space=...]
where the time goes in v5:
time: 42.9 us; the launch traced here: 42.7 us
  starting transfers between devices  21.8 us (51%)
  waiting for transfers between devices  15.4 us (36%)
  Pallas kernels  3.63 us (8%)
  local copies, waits for them, and re-layouts  1.01 us (2%)
  between operations  0.81 us (2%)
    ppermute x20, starting transfers between devices, swap(): return lax.ppermute(x, 'wide', [(i, i ^ mask) for i in range(size)])  21.8 us
    ppermute x20, waiting for transfers between devices, swap(): return lax.ppermute(x, 'wide', [(i, i ^ mask) for i in range(size)])  15.4 us
    pallas_call x7, Pallas kernels, whole_call(): pl.pallas_call(body, out_shape=outs, in_specs=[pl.BlockSpec(memory_space=...  3.63 us
    split x1, local copies, waits for them, and re-layouts, shards(): far_parts = [send(part, far) for part in jnp.split(centres, 2)]  0.98 us
  transfers between devices with their start and end apart: 20, of which 12 were waited for; matrix products, arithmetic and copies ran while one was open for 2% of the time, Pallas kernels for 3%

profile of v5, /device:TPU:0, one launch (start us, length us, event | category | flops | bytes accessed | tf_op | source)
XLA Modules:
  0.0 42.7 jit_solution(2233522109810117725)
XLA Ops:
  0.7 4.1 %collective-permute-start.1 = (bf16[128,512]{1,0:T(8,128)(2,1)}, bf16[128,512]{1,0:T(8,128)(2,1)S(1)}, u32[]{:S(2)}, u32[]{:S(2)}) collective-permute-start(bf16[128,512]{1,0:T(8,128)(2,1)} %features.1), channel_id=1, source_target_pairs={{0,8},{1,9},{2,10},{3,11},{4,12},{5,13},{6,14},{7,15},{8,0},{9,1},... | collective-permute-start | bytes 393224 | tf_op jit(solution)/shard_map/ppermute | solution.py:17
  4.8 1.0 %fusion.1 = (bf16[128,512]{1,0:T(8,128)(2,1)S(1)}, bf16[128,512]{1,0:T(8,128)(2,1)S(1)}) fusion(bf16[256,512]{1,0:T(8,128)(2,1)} %centres.1), kind=kLoop, calls=%fused_computation.5 | loop fusion | bytes 524288 | tf_op jit(solution)/shard_map/split | solution.py:209
  5.8 1.6 %collective-permute-start.5 = (bf16[128,512]{1,0:T(8,128)(2,1)S(1)}, bf16[128,512]{1,0:T(8,128)(2,1)S(1)}, u32[]{:S(2)}, u32[]{:S(2)}) collective-permute-start(bf16[128,512]{1,0:T(8,128)(2,1)S(1)} %get-tuple-element.66), channel_id=1, source_target_pairs={{0,2},{1,3},{2,0},{3,1},{4,6},{5,7},{6,4},{7,5},{8,10},{9,11},{10,... | collective-permute-start | bytes 393224 | tf_op jit(solution)/shard_map/ppermute | solution.py:17
  7.3 0.5 %collective-permute-start.6 = (bf16[128,512]{1,0:T(8,128)(2,1)S(1)}, bf16[128,512]{1,0:T(8,128)(2,1)S(1)}, u32[]{:S(2)}, u32[]{:S(2)}) collective-permute-start(bf16[128,512]{1,0:T(8,128)(2,1)S(1)} %get-tuple-element.65), channel_id=1, source_target_pairs={{0,2},{1,3},{2,0},{3,1},{4,6},{5,7},{6,4},{7,5},{8,10},{9,11},{10,... | collective-permute-start | bytes 393224 | tf_op jit(solution)/shard_map/ppermute | solution.py:17
  7.8 1.5 %collective-permute-start.7 = (f32[256,128]{1,0:T(8,128)S(1)}, f32[256,128]{1,0:T(8,128)S(1)}, u32[]{:S(2)}, u32[]{:S(2)}) collective-permute-start(f32[256,128]{1,0:T(8,128)S(1)} %copy-done.1), channel_id=1, source_target_pairs={{0,2},{1,3},{2,0},{3,1},{4,6},{5,7},{6,4},{7,5},{8,10},{9,11},{10,... | collective-permute-start | bytes 393224 | tf_op jit(solution)/shard_map/ppermute | solution.py:17
  9.4 1.6 %collective-permute-start = (bf16[128,512]{1,0:T(8,128)(2,1)S(1)}, bf16[128,512]{1,0:T(8,128)(2,1)S(1)}, u32[]{:S(2)}, u32[]{:S(2)}) collective-permute-start(bf16[128,512]{1,0:T(8,128)(2,1)S(1)} %copy-done.4), channel_id=1, source_target_pairs={{0,4},{1,5},{2,6},{3,7},{4,0},{5,1},{6,2},{7,3},{8,12},{9,13},{10,... | collective-permute-start | bytes 393224 | tf_op jit(solution)/shard_map/ppermute | solution.py:17
  10.9 0.4 collective-permute-done.1.refs_2_
  11.3 0.8 %collective-permute-start.2 = (bf16[128,512]{1,0:T(8,128)(2,1)S(1)}, bf16[128,512]{1,0:T(8,128)(2,1)S(1)}, u32[]{:S(2)}, u32[]{:S(2)}) collective-permute-start(bf16[128,512]{1,0:T(8,128)(2,1)S(1)} %collective-permute-done.1.refs_2_), channel_id=1, source_target_pairs={{0,4},{1,5},{2,6},{3,7},{4,0},{5,1},{6,2},{7,3},{8,12},{9,13},{10,... | collective-permute-start | bytes 393224 | tf_op jit(solution)/shard_map/ppermute | solution.py:17
  12.3 2.7 %collective-permute-done.6.refs_5_ = bf16[128,512]{1,0:T(8,128)(2,1)S(1)} collective-permute-done((bf16[128,512]{1,0:T(8,128)(2,1)S(1)}, bf16[128,512]{1,0:T(8,128)(2,1)S(1)}, u32[]{:S(2)}, u32[]{:S(2)}) %collective-permute-start.6) | collective-permute-done | bytes 131104 | tf_op jit(solution)/shard_map/ppermute | solution.py:17
  15.0 1.4 %collective-permute-done.7.refs_8_ = f32[256,128]{1,0:T(8,128)S(1)} collective-permute-done((f32[256,128]{1,0:T(8,128)S(1)}, f32[256,128]{1,0:T(8,128)S(1)}, u32[]{:S(2)}, u32[]{:S(2)}) %collective-permute-start.7) | collective-permute-done | bytes 131104 | tf_op jit(solution)/shard_map/ppermute | solution.py:17
  16.4 0.5 %collective-permute-start.9 = (bf16[128,512]{1,0:T(8,128)(2,1)S(1)}, bf16[128,512]{1,0:T(8,128)(2,1)S(1)}, u32[]{:S(2)}, u32[]{:S(2)}) collective-permute-start(bf16[128,512]{1,0:T(8,128)(2,1)S(1)} %collective-permute-done.6.refs_5_), channel_id=1, source_target_pairs={{0,1},{1,0},{2,3},{3,2},{4,5},{5,4},{6,7},{7,6},{8,9},{9,8},{10,11... | collective-permute-start | bytes 393224 | tf_op jit(solution)/shard_map/ppermute | solution.py:17
  16.9 0.2 collective-permute-done.2.refs_3_
  17.1 0.5 %shard_map.86 = (bf16[512,256]{1,0:T(8,128)(2,1)S(1)}, f32[128,128]{1,0:T(8,128)S(1)}, f32[128,128]{1,0:T(8,128)S(1)}, f32[128,128]{1,0:T(8,128)S(1)}, f32[128,128]{1,0:T(8,128)S(1)}) custom-call(bf16[128,512]{1,0:T(8,128)(2,1)S(1)} %get-tuple-element.33.refs_0_, bf16[128,512]{1,0:T(8,128)(2,1)S(1)} %collective-permute-done.refs_1_, ...), custom_call_target="tpu_custom_call" | custom-call | flops 4000000000 | bytes 1376256 | tf_op jit(solution)/shard_map/pallas_call | solution.py:57
  17.7 0.5 %shard_map.87 = (bf16[512,256]{1,0:T(8,128)(2,1)S(1)}, f32[128,128]{1,0:T(8,128)S(1)}, f32[128,128]{1,0:T(8,128)S(1)}, f32[128,128]{1,0:T(8,128)S(1)}, f32[128,128]{1,0:T(8,128)S(1)}) custom-call(bf16[128,512]{1,0:T(8,128)(2,1)S(1)} %get-tuple-element.33.refs_0_, bf16[128,512]{1,0:T(8,128)(2,1)S(1)} %collective-permute-done.refs_1_, ...), custom_call_target="tpu_custom_call" | custom-call | flops 167772160 | bytes 1703936 | tf_op jit(solution)/shard_map/pallas_call | solution.py:57
  18.3 0.2 collective-permute-done.10.refs_9_
  18.5 0.7 %shard_map.88 = (bf16[512,512]{1,0:T(8,128)(2,1)S(1)}, f32[128,128]{1,0:T(8,128)S(1)}, f32[128,128]{1,0:T(8,128)S(1)}, f32[128,128]{1,0:T(8,128)S(1)}, f32[128,128]{1,0:T(8,128)S(1)}) custom-call(bf16[128,512]{1,0:T(8,128)(2,1)S(1)} %get-tuple-element.33.refs_0_, bf16[128,512]{1,0:T(8,128)(2,1)S(1)} %collective-permute-done.refs_1_, ...), custom_call_target="tpu_custom_call" | custom-call | flops 335544320 | bytes 2359296 | tf_op jit(solution)/shard_map/pallas_call | solution.py:57
  19.2 3.3 %collective-permute-start.13 = (f16[128,128]{1,0:T(8,128)(2,1)S(1)}, f16[128,128]{1,0:T(8,128)(2,1)S(1)}, u32[]{:S(2)}, u32[]{:S(2)}) collective-permute-start(f16[128,128]{1,0:T(8,128)(2,1)S(1)} %multiply_convert_fusion), channel_id=1, source_target_pairs={{0,12},{1,13},{2,14},{3,15},{4,8},{5,9},{6,10},{7,11},{8,4},{9,5},... | collective-permute-start | bytes 98312 | tf_op jit(solution)/shard_map/ppermute | solution.py:17
  22.7 1.2 %collective-permute-start.11 = (f16[128,128]{1,0:T(8,128)(2,1)S(1)}, f16[128,128]{1,0:T(8,128)(2,1)S(1)}, u32[]{:S(2)}, u32[]{:S(2)}) collective-permute-start(f16[128,128]{1,0:T(8,128)(2,1)S(1)} %multiply_convert_fusion.2), channel_id=1, source_target_pairs={{0,4},{1,5},{2,6},{3,7},{4,0},{5,1},{6,2},{7,3},{8,12},{9,13},{10,... | collective-permute-start | bytes 98312 | tf_op jit(solution)/shard_map/ppermute | solution.py:17
  23.9 1.3 %collective-permute-done.13 = f16[128,128]{1,0:T(8,128)(2,1)S(1)} collective-permute-done((f16[128,128]{1,0:T(8,128)(2,1)S(1)}, f16[128,128]{1,0:T(8,128)(2,1)S(1)}, u32[]{:S(2)}, u32[]{:S(2)}) %collective-permute-start.13) | collective-permute-done | bytes 32800 | tf_op jit(solution)/shard_map/ppermute | solution.py:17
  25.2 2.3 %collective-permute-done.12 = f16[128,128]{1,0:T(8,128)(2,1)S(1)} collective-permute-done((f16[128,128]{1,0:T(8,128)(2,1)S(1)}, f16[128,128]{1,0:T(8,128)(2,1)S(1)}, u32[]{:S(2)}, u32[]{:S(2)}) %collective-permute-start.12) | collective-permute-done | bytes 32800 | tf_op jit(solution)/shard_map/ppermute | solution.py:17
  27.5 1.7 %collective-permute-start.14 = (bf16[128,128]{1,0:T(8,128)(2,1)S(1)}, bf16[128,128]{1,0:T(8,128)(2,1)S(1)}, u32[]{:S(2)}, u32[]{:S(2)}) collective-permute-start(bf16[128,128]{1,0:T(8,128)(2,1)S(1)} %get-tuple-element.63.refs_1_), channel_id=1, source_target_pairs={{0,12},{1,13},{2,14},{3,15},{4,8},{5,9},{6,10},{7,11},{8,4},{9,5},... | collective-permute-start | bytes 98312 | tf_op jit(solution)/shard_map/ppermute | solution.py:17
  29.2 0.5 %collective-permute-start.15 = (bf16[128,128]{1,0:T(8,128)(2,1)S(1)}, bf16[128,128]{1,0:T(8,128)(2,1)S(1)}, u32[]{:S(2)}, u32[]{:S(2)}) collective-permute-start(bf16[128,128]{1,0:T(8,128)(2,1)S(1)} %get-tuple-element.63.refs_1_), channel_id=1, source_target_pairs={{0,8},{1,9},{2,10},{3,11},{4,12},{5,13},{6,14},{7,15},{8,0},{9,1},... | collective-permute-start | bytes 98312 | tf_op jit(solution)/shard_map/ppermute | solution.py:17
  29.7 2.2 %collective-permute-start.16 = (bf16[128,128]{1,0:T(8,128)(2,1)S(1)}, bf16[128,128]{1,0:T(8,128)(2,1)S(1)}, u32[]{:S(2)}, u32[]{:S(2)}) collective-permute-start(bf16[128,128]{1,0:T(8,128)(2,1)S(1)} %get-tuple-element.63.refs_1_), channel_id=1, source_target_pairs={{0,4},{1,5},{2,6},{3,7},{4,0},{5,1},{6,2},{7,3},{8,12},{9,13},{10,... | collective-permute-start | bytes 98312 | tf_op jit(solution)/shard_map/ppermute | solution.py:17
  32.0 1.3 %collective-permute-done.14.refs_2_ = bf16[128,128]{1,0:T(8,128)(2,1)S(1)} collective-permute-done((bf16[128,128]{1,0:T(8,128)(2,1)S(1)}, bf16[128,128]{1,0:T(8,128)(2,1)S(1)}, u32[]{:S(2)}, u32[]{:S(2)}) %collective-permute-start.14) | collective-permute-done | bytes 32800 | tf_op jit(solution)/shard_map/ppermute | solution.py:17
  33.3 0.9 %collective-permute-done.15.refs_3_ = bf16[128,128]{1,0:T(8,128)(2,1)S(1)} collective-permute-done((bf16[128,128]{1,0:T(8,128)(2,1)S(1)}, bf16[128,128]{1,0:T(8,128)(2,1)S(1)}, u32[]{:S(2)}, u32[]{:S(2)}) %collective-permute-start.15) | collective-permute-done | bytes 32800 | tf_op jit(solution)/shard_map/ppermute | solution.py:17
  34.2 0.4 shard_map.89
  34.6 0.3 shard_map.90
  35.0 0.6 %collective-permute-start.17 = (f32[256,128]{1,0:T(8,128)S(1)}, f32[256,128]{1,0:T(8,128)S(1)}, u32[]{:S(2)}, u32[]{:S(2)}) collective-permute-start(f32[256,128]{1,0:T(8,128)S(1)} %get-tuple-element.57), channel_id=1, source_target_pairs={{0,1},{1,0},{2,3},{3,2},{4,5},{5,4},{6,7},{7,6},{8,9},{9,8},{10,11... | collective-permute-start | bytes 393224 | tf_op jit(solution)/shard_map/ppermute | solution.py:17
  35.6 0.4 collective-permute-done.18
  36.0 1.5 %collective-permute-start.19 = (f32[256,128]{1,0:T(8,128)S(1)}, f32[256,128]{1,0:T(8,128)S(1)}, u32[]{:S(2)}, u32[]{:S(2)}) collective-permute-start(f32[256,128]{1,0:T(8,128)S(1)} %add.15), channel_id=1, source_target_pairs={{0,2},{1,3},{2,0},{3,1},{4,6},{5,7},{6,4},{7,5},{8,10},{9,11},{10,... | collective-permute-start | bytes 393224 | tf_op jit(solution)/shard_map/ppermute | solution.py:17
  37.5 4.2 %collective-permute-done.19.refs_2_ = f32[256,128]{1,0:T(8,128)S(1)} collective-permute-done((f32[256,128]{1,0:T(8,128)S(1)}, f32[256,128]{1,0:T(8,128)S(1)}, u32[]{:S(2)}, u32[]{:S(2)}) %collective-permute-start.19) | collective-permute-done | bytes 131104 | tf_op jit(solution)/shard_map/ppermute | solution.py:17
  41.6 1.1 %shard_map.91 = (f32[256,128]{1,0:T(8,128)}, f32[256,128]{1,0:T(8,128)}, f32[128,128]{1,0:T(8,128)}) custom-call(f32[256,128]{1,0:T(8,128)S(1)} %get-tuple-element.56.refs_0_, f32[256,128]{1,0:T(8,128)S(1)} %collective-permute-done.17.refs_1_, f32[256,128]{1,0:T(8,128)S(1)} %collective-permute-done.19.refs_2_, f32[1,256,256]{2,1,0:T(8,128)S(1)} %copy-done.2, ...), custom_call_target="tpu_custom_call" | custom-call | bytes 1310720 | tf_op jit(solution)/shard_map/pallas_call | solution.py:57
  (33 shorter events, 0.4 us)
Async XLA Ops:
  0.6 8.7 %copy-start.4 = (bf16[128,512]{1,0:T(8,128)(2,1)S(1)}, bf16[128,512]{1,0:T(8,128)(2,1)}, u32[]{:S(2)}) copy-start(bf16[128,512]{1,0:T(8,128)(2,1)} %features.1) | copy-start | bytes 393220
  0.6 11.5 %copy-start = (bf16[256,512]{1,0:T(8,128)(2,1)S(1)}, bf16[256,512]{1,0:T(8,128)(2,1)}, u32[]{:S(2)}) copy-start(bf16[256,512]{1,0:T(8,128)(2,1)} %centres.1) | copy-start | bytes 786436
  0.7 7.2 %copy-start.1 = (f32[256,128]{1,0:T(8,128)S(1)}, f32[256,128]{1,0:T(8,128)}, u32[]{:S(2)}) copy-start(f32[256,128]{1,0:T(8,128)} %refs_5_.1) | copy-start | bytes 393220
  0.7 10.7 %collective-permute-start.1 = (bf16[128,512]{1,0:T(8,128)(2,1)}, bf16[128,512]{1,0:T(8,128)(2,1)S(1)}, u32[]{:S(2)}, u32[]{:S(2)}) collective-permute-start(bf16[128,512]{1,0:T(8,128)(2,1)} %features.1), channel_id=1, source_target_pairs={{0,8},{1,9},{2,10},{3,11},{4,12},{5,13},{6,14},{7,15},{8,0},{9,1},... | collective-permute-start | bytes 393224 | tf_op jit(solution)/shard_map/ppermute | solution.py:17
  5.8 6.5 %collective-permute-start.5 = (bf16[128,512]{1,0:T(8,128)(2,1)S(1)}, bf16[128,512]{1,0:T(8,128)(2,1)S(1)}, u32[]{:S(2)}, u32[]{:S(2)}) collective-permute-start(bf16[128,512]{1,0:T(8,128)(2,1)S(1)} %get-tuple-element.66), channel_id=1, source_target_pairs={{0,2},{1,3},{2,0},{3,1},{4,6},{5,7},{6,4},{7,5},{8,10},{9,11},{10,... | collective-permute-start | bytes 393224 | tf_op jit(solution)/shard_map/ppermute | solution.py:17
  7.3 7.7 %collective-permute-start.6 = (bf16[128,512]{1,0:T(8,128)(2,1)S(1)}, bf16[128,512]{1,0:T(8,128)(2,1)S(1)}, u32[]{:S(2)}, u32[]{:S(2)}) collective-permute-start(bf16[128,512]{1,0:T(8,128)(2,1)S(1)} %get-tuple-element.65), channel_id=1, source_target_pairs={{0,2},{1,3},{2,0},{3,1},{4,6},{5,7},{6,4},{7,5},{8,10},{9,11},{10,... | collective-permute-start | bytes 393224 | tf_op jit(solution)/shard_map/ppermute | solution.py:17
  7.8 8.5 %collective-permute-start.7 = (f32[256,128]{1,0:T(8,128)S(1)}, f32[256,128]{1,0:T(8,128)S(1)}, u32[]{:S(2)}, u32[]{:S(2)}) collective-permute-start(f32[256,128]{1,0:T(8,128)S(1)} %copy-done.1), channel_id=1, source_target_pairs={{0,2},{1,3},{2,0},{3,1},{4,6},{5,7},{6,4},{7,5},{8,10},{9,11},{10,... | collective-permute-start | bytes 393224 | tf_op jit(solution)/shard_map/ppermute | solution.py:17
  9.4 7.0 %collective-permute-start = (bf16[128,512]{1,0:T(8,128)(2,1)S(1)}, bf16[128,512]{1,0:T(8,128)(2,1)S(1)}, u32[]{:S(2)}, u32[]{:S(2)}) collective-permute-start(bf16[128,512]{1,0:T(8,128)(2,1)S(1)} %copy-done.4), channel_id=1, source_target_pairs={{0,4},{1,5},{2,6},{3,7},{4,0},{5,1},{6,2},{7,3},{8,12},{9,13},{10,... | collective-permute-start | bytes 393224 | tf_op jit(solution)/shard_map/ppermute | solution.py:17
  11.3 5.8 %collective-permute-start.2 = (bf16[128,512]{1,0:T(8,128)(2,1)S(1)}, bf16[128,512]{1,0:T(8,128)(2,1)S(1)}, u32[]{:S(2)}, u32[]{:S(2)}) collective-permute-start(bf16[128,512]{1,0:T(8,128)(2,1)S(1)} %collective-permute-done.1.refs_2_), channel_id=1, source_target_pairs={{0,4},{1,5},{2,6},{3,7},{4,0},{5,1},{6,2},{7,3},{8,12},{9,13},{10,... | collective-permute-start | bytes 393224 | tf_op jit(solution)/shard_map/ppermute | solution.py:17
  12.2 5.5 %collective-permute-start.3 = (bf16[256,512]{1,0:T(8,128)(2,1)S(1)}, bf16[256,512]{1,0:T(8,128)(2,1)S(1)}, u32[]{:S(2)}, u32[]{:S(2)}) collective-permute-start(bf16[256,512]{1,0:T(8,128)(2,1)S(1)} %copy-done), channel_id=1, source_target_pairs={{0,1},{1,0},{2,3},{3,2},{4,5},{5,4},{6,7},{7,6},{8,9},{9,8},{10,11... | collective-permute-start | bytes 786440 | tf_op jit(solution)/shard_map/ppermute | solution.py:17
  15.0 2.7 %collective-permute-start.4 = (f32[256,128]{1,0:T(8,128)S(1)}, f32[256,128]{1,0:T(8,128)S(1)}, u32[]{:S(2)}, u32[]{:S(2)}) collective-permute-start(f32[256,128]{1,0:T(8,128)S(1)} %copy-done.1), channel_id=1, source_target_pairs={{0,1},{1,0},{2,3},{3,2},{4,5},{5,4},{6,7},{7,6},{8,9},{9,8},{10,11... | collective-permute-start | bytes 393224 | tf_op jit(solution)/shard_map/ppermute | solution.py:17
  16.4 1.9 %collective-permute-start.8 = (bf16[128,512]{1,0:T(8,128)(2,1)S(1)}, bf16[128,512]{1,0:T(8,128)(2,1)S(1)}, u32[]{:S(2)}, u32[]{:S(2)}) collective-permute-start(bf16[128,512]{1,0:T(8,128)(2,1)S(1)} %collective-permute-done.5.refs_4_), channel_id=1, source_target_pairs={{0,1},{1,0},{2,3},{3,2},{4,5},{5,4},{6,7},{7,6},{8,9},{9,8},{10,11... | collective-permute-start | bytes 393224 | tf_op jit(solution)/shard_map/ppermute | solution.py:17
  16.4 1.9 %collective-permute-start.9 = (bf16[128,512]{1,0:T(8,128)(2,1)S(1)}, bf16[128,512]{1,0:T(8,128)(2,1)S(1)}, u32[]{:S(2)}, u32[]{:S(2)}) collective-permute-start(bf16[128,512]{1,0:T(8,128)(2,1)S(1)} %collective-permute-done.6.refs_5_), channel_id=1, source_target_pairs={{0,1},{1,0},{2,3},{3,2},{4,5},{5,4},{6,7},{7,6},{8,9},{9,8},{10,11... | collective-permute-start | bytes 393224 | tf_op jit(solution)/shard_map/ppermute | solution.py:17
  17.1 1.3 %collective-permute-start.10 = (f32[256,128]{1,0:T(8,128)S(1)}, f32[256,128]{1,0:T(8,128)S(1)}, u32[]{:S(2)}, u32[]{:S(2)}) collective-permute-start(f32[256,128]{1,0:T(8,128)S(1)} %collective-permute-done.7.refs_8_), channel_id=1, source_target_pairs={{0,1},{1,0},{2,3},{3,2},{4,5},{5,4},{6,7},{7,6},{8,9},{9,8},{10,11... | collective-permute-start | bytes 393224 | tf_op jit(solution)/shard_map/ppermute | solution.py:17
  19.2 5.9 %collective-permute-start.13 = (f16[128,128]{1,0:T(8,128)(2,1)S(1)}, f16[128,128]{1,0:T(8,128)(2,1)S(1)}, u32[]{:S(2)}, u32[]{:S(2)}) collective-permute-start(f16[128,128]{1,0:T(8,128)(2,1)S(1)} %multiply_convert_fusion), channel_id=1, source_target_pairs={{0,12},{1,13},{2,14},{3,15},{4,8},{5,9},{6,10},{7,11},{8,4},{9,5},... | collective-permute-start | bytes 98312 | tf_op jit(solution)/shard_map/ppermute | solution.py:17
  22.6 4.9 %collective-permute-start.12 = (f16[128,128]{1,0:T(8,128)(2,1)S(1)}, f16[128,128]{1,0:T(8,128)(2,1)S(1)}, u32[]{:S(2)}, u32[]{:S(2)}) collective-permute-start(f16[128,128]{1,0:T(8,128)(2,1)S(1)} %multiply_convert_fusion.1), channel_id=1, source_target_pairs={{0,8},{1,9},{2,10},{3,11},{4,12},{5,13},{6,14},{7,15},{8,0},{9,1},... | collective-permute-start | bytes 98312 | tf_op jit(solution)/shard_map/ppermute | solution.py:17
  22.7 4.8 %copy-start.5 = (bf16[128,128]{1,0:T(8,128)(2,1)S(1)}, bf16[128,128]{1,0:T(8,128)(2,1)}, u32[]{:S(2)}) copy-start(bf16[128,128]{1,0:T(8,128)(2,1)} %param.8) | copy-start | bytes 98308
  22.7 4.8 %collective-permute-start.11 = (f16[128,128]{1,0:T(8,128)(2,1)S(1)}, f16[128,128]{1,0:T(8,128)(2,1)S(1)}, u32[]{:S(2)}, u32[]{:S(2)}) collective-permute-start(f16[128,128]{1,0:T(8,128)(2,1)S(1)} %multiply_convert_fusion.2), channel_id=1, source_target_pairs={{0,4},{1,5},{2,6},{3,7},{4,0},{5,1},{6,2},{7,3},{8,12},{9,13},{10,... | collective-permute-start | bytes 98312 | tf_op jit(solution)/shard_map/ppermute | solution.py:17
  27.5 5.8 %collective-permute-start.14 = (bf16[128,128]{1,0:T(8,128)(2,1)S(1)}, bf16[128,128]{1,0:T(8,128)(2,1)S(1)}, u32[]{:S(2)}, u32[]{:S(2)}) collective-permute-start(bf16[128,128]{1,0:T(8,128)(2,1)S(1)} %get-tuple-element.63.refs_1_), channel_id=1, source_target_pairs={{0,12},{1,13},{2,14},{3,15},{4,8},{5,9},{6,10},{7,11},{8,4},{9,5},... | collective-permute-start | bytes 98312 | tf_op jit(solution)/shard_map/ppermute | solution.py:17
  29.2 4.9 %collective-permute-start.15 = (bf16[128,128]{1,0:T(8,128)(2,1)S(1)}, bf16[128,128]{1,0:T(8,128)(2,1)S(1)}, u32[]{:S(2)}, u32[]{:S(2)}) collective-permute-start(bf16[128,128]{1,0:T(8,128)(2,1)S(1)} %get-tuple-element.63.refs_1_), channel_id=1, source_target_pairs={{0,8},{1,9},{2,10},{3,11},{4,12},{5,13},{6,14},{7,15},{8,0},{9,1},... | collective-permute-start | bytes 98312 | tf_op jit(solution)/shard_map/ppermute | solution.py:17
  29.7 4.4 %collective-permute-start.16 = (bf16[128,128]{1,0:T(8,128)(2,1)S(1)}, bf16[128,128]{1,0:T(8,128)(2,1)S(1)}, u32[]{:S(2)}, u32[]{:S(2)}) collective-permute-start(bf16[128,128]{1,0:T(8,128)(2,1)S(1)} %get-tuple-element.63.refs_1_), channel_id=1, source_target_pairs={{0,4},{1,5},{2,6},{3,7},{4,0},{5,1},{6,2},{7,3},{8,12},{9,13},{10,... | collective-permute-start | bytes 98312 | tf_op jit(solution)/shard_map/ppermute | solution.py:17
  34.6 1.4 %collective-permute-start.18 = (f32[256,128]{1,0:T(8,128)S(1)}, f32[256,128]{1,0:T(8,128)S(1)}, u32[]{:S(2)}, u32[]{:S(2)}) collective-permute-start(f32[256,128]{1,0:T(8,128)S(1)} %get-tuple-element.59), channel_id=1, source_target_pairs={{0,1},{1,0},{2,3},{3,2},{4,5},{5,4},{6,7},{7,6},{8,9},{9,8},{10,11... | collective-permute-start | bytes 393224 | tf_op jit(solution)/shard_map/ppermute | solution.py:17
  35.0 6.6 %copy-start.2 = (f32[1,256,256]{2,1,0:T(8,128)S(1)}, f32[1,256,256]{2,1,0:T(8,128)}, u32[]{:S(2)}) copy-start(f32[1,256,256]{2,1,0:T(8,128)} %refs_3_.1) | copy-start | bytes 786436
  35.0 2.5 %collective-permute-start.17 = (f32[256,128]{1,0:T(8,128)S(1)}, f32[256,128]{1,0:T(8,128)S(1)}, u32[]{:S(2)}, u32[]{:S(2)}) collective-permute-start(f32[256,128]{1,0:T(8,128)S(1)} %get-tuple-element.57), channel_id=1, source_target_pairs={{0,1},{1,0},{2,3},{3,2},{4,5},{5,4},{6,7},{7,6},{8,9},{9,8},{10,11... | collective-permute-start | bytes 393224 | tf_op jit(solution)/shard_map/ppermute | solution.py:17
  36.0 5.6 %copy-start.3 = (f32[256,128]{1,0:T(8,128)S(1)}, f32[256,128]{1,0:T(8,128)}, u32[]{:S(2)}) copy-start(f32[256,128]{1,0:T(8,128)} %refs_4_.1) | copy-start | bytes 393220
  36.0 5.6 %collective-permute-start.19 = (f32[256,128]{1,0:T(8,128)S(1)}, f32[256,128]{1,0:T(8,128)S(1)}, u32[]{:S(2)}, u32[]{:S(2)}) collective-permute-start(f32[256,128]{1,0:T(8,128)S(1)} %add.15), channel_id=1, source_target_pairs={{0,2},{1,3},{2,0},{3,1},{4,6},{5,7},{6,4},{7,5},{8,10},{9,11},{10,... | collective-permute-start | bytes 393224 | tf_op jit(solution)/shard_map/ppermute | solution.py:17

commit v6 on v5

--- a/solution.py
+++ b/solution.py
@@ -232,8 +232,11 @@
     held = jax.ShapeDtypeStruct(targets.shape, F32)
     residuals = gather_pieces(half, digits, size)
 
+    bound = 2 * sum(p.shape[0] for p in residuals) * (5.05 * size * count + 24)
+    scale = 2.0 ** math.floor(math.log2(65504 / bound))
+    kind, factor = (jnp.float16, scale) if scale >= 2.0**-10 else (F32, 1.0)
     far_keep, far_give, joined = gradients(far_kernels, far_layout, residuals, count)
-    arrived = send(far_keep + send(far_give, core), far)
+    arrived = send((factor * (far_keep + send(far_give, core))).astype(kind), far).astype(F32) / factor
     keep, give = gradients(near_kernels, near_layout, [joined], count)
     parts = [keep, send(give, core), arrived]
     out = jax.ShapeDtypeStruct(momentum.shape, F32)

time: 42.9 us -> 41.6 us (0.970)
  waiting for transfers between devices: 15.4 us -> 14.6 us
  starting transfers between devices: 21.8 us -> 21.3 us
    ppermute x20, waiting for transfers between devices: 15.4 us -> 14.6 us  [swap(): return lax.ppermute(x, 'wide', [(i, i ^ mask) for i in range(size)])]
    ppermute x20, starting transfers between devices: 21.8 us -> 21.3 us  [swap(): return lax.ppermute(x, 'wide', [(i, i ^ mask) for i in range(size)])]
where the time goes in v6:
time: 41.6 us; the launch traced here: 41.5 us
  starting transfers between devices  21.3 us (51%)
  waiting for transfers between devices  14.6 us (35%)
  Pallas kernels  3.63 us (9%)
  local copies, waits for them, and re-layouts  1.01 us (2%)
  between operations  0.84 us (2%)
    ppermute x20, starting transfers between devices, swap(): return lax.ppermute(x, 'wide', [(i, i ^ mask) for i in range(size)])  21.3 us
    ppermute x20, waiting for transfers between devices, swap(): return lax.ppermute(x, 'wide', [(i, i ^ mask) for i in range(size)])  14.6 us
    pallas_call x7, Pallas kernels, whole_call(): pl.pallas_call(body, out_shape=outs, in_specs=[pl.BlockSpec(memory_space=...  3.63 us
    split x1, local copies, waits for them, and re-layouts, shards(): far_parts = [send(part, far) for part in jnp.split(centres, 2)]  0.98 us
  transfers between devices with their start and end apart: 20, of which 12 were waited for; matrix products, arithmetic and copies ran while one was open for 2% of the time, Pallas kernels for 3%

profile of v6, /device:TPU:0, one launch (start us, length us, event | category | flops | bytes accessed | tf_op | source)
XLA Modules:
  0.0 41.5 jit_solution(15020317860760354642)
XLA Ops:
  0.7 4.1 %collective-permute-start.1 = (bf16[128,512]{1,0:T(8,128)(2,1)}, bf16[128,512]{1,0:T(8,128)(2,1)S(1)}, u32[]{:S(2)}, u32[]{:S(2)}) collective-permute-start(bf16[128,512]{1,0:T(8,128)(2,1)} %features.1), channel_id=1, source_target_pairs={{0,8},{1,9},{2,10},{3,11},{4,12},{5,13},{6,14},{7,15},{8,0},{9,1},... | collective-permute-start | bytes 393224 | tf_op jit(solution)/shard_map/ppermute | solution.py:17
  4.8 1.0 %fusion.1 = (bf16[128,512]{1,0:T(8,128)(2,1)S(1)}, bf16[128,512]{1,0:T(8,128)(2,1)S(1)}) fusion(bf16[256,512]{1,0:T(8,128)(2,1)} %centres.1), kind=kLoop, calls=%fused_computation.7 | loop fusion | bytes 524288 | tf_op jit(solution)/shard_map/split | solution.py:209
  5.8 1.6 %collective-permute-start.5 = (bf16[128,512]{1,0:T(8,128)(2,1)S(1)}, bf16[128,512]{1,0:T(8,128)(2,1)S(1)}, u32[]{:S(2)}, u32[]{:S(2)}) collective-permute-start(bf16[128,512]{1,0:T(8,128)(2,1)S(1)} %get-tuple-element.66), channel_id=1, source_target_pairs={{0,2},{1,3},{2,0},{3,1},{4,6},{5,7},{6,4},{7,5},{8,10},{9,11},{10,... | collective-permute-start | bytes 393224 | tf_op jit(solution)/shard_map/ppermute | solution.py:17
  7.3 0.5 %collective-permute-start.6 = (bf16[128,512]{1,0:T(8,128)(2,1)S(1)}, bf16[128,512]{1,0:T(8,128)(2,1)S(1)}, u32[]{:S(2)}, u32[]{:S(2)}) collective-permute-start(bf16[128,512]{1,0:T(8,128)(2,1)S(1)} %get-tuple-element.65), channel_id=1, source_target_pairs={{0,2},{1,3},{2,0},{3,1},{4,6},{5,7},{6,4},{7,5},{8,10},{9,11},{10,... | collective-permute-start | bytes 393224 | tf_op jit(solution)/shard_map/ppermute | solution.py:17
  7.8 1.5 %collective-permute-start.7 = (f32[256,128]{1,0:T(8,128)S(1)}, f32[256,128]{1,0:T(8,128)S(1)}, u32[]{:S(2)}, u32[]{:S(2)}) collective-permute-start(f32[256,128]{1,0:T(8,128)S(1)} %copy-done.1), channel_id=1, source_target_pairs={{0,2},{1,3},{2,0},{3,1},{4,6},{5,7},{6,4},{7,5},{8,10},{9,11},{10,... | collective-permute-start | bytes 393224 | tf_op jit(solution)/shard_map/ppermute | solution.py:17
  9.4 1.6 %collective-permute-start = (bf16[128,512]{1,0:T(8,128)(2,1)S(1)}, bf16[128,512]{1,0:T(8,128)(2,1)S(1)}, u32[]{:S(2)}, u32[]{:S(2)}) collective-permute-start(bf16[128,512]{1,0:T(8,128)(2,1)S(1)} %copy-done.4), channel_id=1, source_target_pairs={{0,4},{1,5},{2,6},{3,7},{4,0},{5,1},{6,2},{7,3},{8,12},{9,13},{10,... | collective-permute-start | bytes 393224 | tf_op jit(solution)/shard_map/ppermute | solution.py:17
  10.9 0.4 collective-permute-done.1.refs_2_
  11.3 0.8 %collective-permute-start.2 = (bf16[128,512]{1,0:T(8,128)(2,1)S(1)}, bf16[128,512]{1,0:T(8,128)(2,1)S(1)}, u32[]{:S(2)}, u32[]{:S(2)}) collective-permute-start(bf16[128,512]{1,0:T(8,128)(2,1)S(1)} %collective-permute-done.1.refs_2_), channel_id=1, source_target_pairs={{0,4},{1,5},{2,6},{3,7},{4,0},{5,1},{6,2},{7,3},{8,12},{9,13},{10,... | collective-permute-start | bytes 393224 | tf_op jit(solution)/shard_map/ppermute | solution.py:17
  12.3 2.7 %collective-permute-done.6.refs_5_ = bf16[128,512]{1,0:T(8,128)(2,1)S(1)} collective-permute-done((bf16[128,512]{1,0:T(8,128)(2,1)S(1)}, bf16[128,512]{1,0:T(8,128)(2,1)S(1)}, u32[]{:S(2)}, u32[]{:S(2)}) %collective-permute-start.6) | collective-permute-done | bytes 131104 | tf_op jit(solution)/shard_map/ppermute | solution.py:17
  15.0 1.4 %collective-permute-done.7.refs_8_ = f32[256,128]{1,0:T(8,128)S(1)} collective-permute-done((f32[256,128]{1,0:T(8,128)S(1)}, f32[256,128]{1,0:T(8,128)S(1)}, u32[]{:S(2)}, u32[]{:S(2)}) %collective-permute-start.7) | collective-permute-done | bytes 131104 | tf_op jit(solution)/shard_map/ppermute | solution.py:17
  16.4 0.5 %collective-permute-start.9 = (bf16[128,512]{1,0:T(8,128)(2,1)S(1)}, bf16[128,512]{1,0:T(8,128)(2,1)S(1)}, u32[]{:S(2)}, u32[]{:S(2)}) collective-permute-start(bf16[128,512]{1,0:T(8,128)(2,1)S(1)} %collective-permute-done.6.refs_5_), channel_id=1, source_target_pairs={{0,1},{1,0},{2,3},{3,2},{4,5},{5,4},{6,7},{7,6},{8,9},{9,8},{10,11... | collective-permute-start | bytes 393224 | tf_op jit(solution)/shard_map/ppermute | solution.py:17
  16.9 0.2 collective-permute-done.2.refs_3_
  17.1 0.5 %shard_map.86 = (bf16[512,256]{1,0:T(8,128)(2,1)S(1)}, f32[128,128]{1,0:T(8,128)S(1)}, f32[128,128]{1,0:T(8,128)S(1)}, f32[128,128]{1,0:T(8,128)S(1)}, f32[128,128]{1,0:T(8,128)S(1)}) custom-call(bf16[128,512]{1,0:T(8,128)(2,1)S(1)} %get-tuple-element.33.refs_0_, bf16[128,512]{1,0:T(8,128)(2,1)S(1)} %collective-permute-done.refs_1_, ...), custom_call_target="tpu_custom_call" | custom-call | flops 4000000000 | bytes 1376256 | tf_op jit(solution)/shard_map/pallas_call | solution.py:57
  17.7 0.5 %shard_map.87 = (bf16[512,256]{1,0:T(8,128)(2,1)S(1)}, f32[128,128]{1,0:T(8,128)S(1)}, f32[128,128]{1,0:T(8,128)S(1)}, f32[128,128]{1,0:T(8,128)S(1)}, f32[128,128]{1,0:T(8,128)S(1)}) custom-call(bf16[128,512]{1,0:T(8,128)(2,1)S(1)} %get-tuple-element.33.refs_0_, bf16[128,512]{1,0:T(8,128)(2,1)S(1)} %collective-permute-done.refs_1_, ...), custom_call_target="tpu_custom_call" | custom-call | flops 167772160 | bytes 1703936 | tf_op jit(solution)/shard_map/pallas_call | solution.py:57
  18.3 0.2 collective-permute-done.10.refs_9_
  18.5 0.7 %shard_map.88 = (bf16[512,512]{1,0:T(8,128)(2,1)S(1)}, f32[128,128]{1,0:T(8,128)S(1)}, f32[128,128]{1,0:T(8,128)S(1)}, f32[128,128]{1,0:T(8,128)S(1)}, f32[128,128]{1,0:T(8,128)S(1)}) custom-call(bf16[128,512]{1,0:T(8,128)(2,1)S(1)} %get-tuple-element.33.refs_0_, bf16[128,512]{1,0:T(8,128)(2,1)S(1)} %collective-permute-done.refs_1_, ...), custom_call_target="tpu_custom_call" | custom-call | flops 335544320 | bytes 2359296 | tf_op jit(solution)/shard_map/pallas_call | solution.py:57
  19.2 3.3 %collective-permute-start.13 = (f16[128,128]{1,0:T(8,128)(2,1)S(1)}, f16[128,128]{1,0:T(8,128)(2,1)S(1)}, u32[]{:S(2)}, u32[]{:S(2)}) collective-permute-start(f16[128,128]{1,0:T(8,128)(2,1)S(1)} %multiply_convert_fusion.1), channel_id=1, source_target_pairs={{0,12},{1,13},{2,14},{3,15},{4,8},{5,9},{6,10},{7,11},{8,4},{9,5},... | collective-permute-start | bytes 98312 | tf_op jit(solution)/shard_map/ppermute | solution.py:17
  22.7 1.2 %collective-permute-start.11 = (f16[128,128]{1,0:T(8,128)(2,1)S(1)}, f16[128,128]{1,0:T(8,128)(2,1)S(1)}, u32[]{:S(2)}, u32[]{:S(2)}) collective-permute-start(f16[128,128]{1,0:T(8,128)(2,1)S(1)} %multiply_convert_fusion.3), channel_id=1, source_target_pairs={{0,4},{1,5},{2,6},{3,7},{4,0},{5,1},{6,2},{7,3},{8,12},{9,13},{10,... | collective-permute-start | bytes 98312 | tf_op jit(solution)/shard_map/ppermute | solution.py:17
  23.9 1.3 %collective-permute-done.13 = f16[128,128]{1,0:T(8,128)(2,1)S(1)} collective-permute-done((f16[128,128]{1,0:T(8,128)(2,1)S(1)}, f16[128,128]{1,0:T(8,128)(2,1)S(1)}, u32[]{:S(2)}, u32[]{:S(2)}) %collective-permute-start.13) | collective-permute-done | bytes 32800 | tf_op jit(solution)/shard_map/ppermute | solution.py:17
  25.2 2.3 %collective-permute-done.12 = f16[128,128]{1,0:T(8,128)(2,1)S(1)} collective-permute-done((f16[128,128]{1,0:T(8,128)(2,1)S(1)}, f16[128,128]{1,0:T(8,128)(2,1)S(1)}, u32[]{:S(2)}, u32[]{:S(2)}) %collective-permute-start.12) | collective-permute-done | bytes 32800 | tf_op jit(solution)/shard_map/ppermute | solution.py:17
  27.5 1.7 %collective-permute-start.14 = (bf16[128,128]{1,0:T(8,128)(2,1)S(1)}, bf16[128,128]{1,0:T(8,128)(2,1)S(1)}, u32[]{:S(2)}, u32[]{:S(2)}) collective-permute-start(bf16[128,128]{1,0:T(8,128)(2,1)S(1)} %get-tuple-element.63.refs_1_), channel_id=1, source_target_pairs={{0,12},{1,13},{2,14},{3,15},{4,8},{5,9},{6,10},{7,11},{8,4},{9,5},... | collective-permute-start | bytes 98312 | tf_op jit(solution)/shard_map/ppermute | solution.py:17
  29.2 0.5 %collective-permute-start.15 = (bf16[128,128]{1,0:T(8,128)(2,1)S(1)}, bf16[128,128]{1,0:T(8,128)(2,1)S(1)}, u32[]{:S(2)}, u32[]{:S(2)}) collective-permute-start(bf16[128,128]{1,0:T(8,128)(2,1)S(1)} %get-tuple-element.63.refs_1_), channel_id=1, source_target_pairs={{0,8},{1,9},{2,10},{3,11},{4,12},{5,13},{6,14},{7,15},{8,0},{9,1},... | collective-permute-start | bytes 98312 | tf_op jit(solution)/shard_map/ppermute | solution.py:17
  29.7 2.2 %collective-permute-start.16 = (bf16[128,128]{1,0:T(8,128)(2,1)S(1)}, bf16[128,128]{1,0:T(8,128)(2,1)S(1)}, u32[]{:S(2)}, u32[]{:S(2)}) collective-permute-start(bf16[128,128]{1,0:T(8,128)(2,1)S(1)} %get-tuple-element.63.refs_1_), channel_id=1, source_target_pairs={{0,4},{1,5},{2,6},{3,7},{4,0},{5,1},{6,2},{7,3},{8,12},{9,13},{10,... | collective-permute-start | bytes 98312 | tf_op jit(solution)/shard_map/ppermute | solution.py:17
  32.0 1.3 %collective-permute-done.14.refs_2_ = bf16[128,128]{1,0:T(8,128)(2,1)S(1)} collective-permute-done((bf16[128,128]{1,0:T(8,128)(2,1)S(1)}, bf16[128,128]{1,0:T(8,128)(2,1)S(1)}, u32[]{:S(2)}, u32[]{:S(2)}) %collective-permute-start.14) | collective-permute-done | bytes 32800 | tf_op jit(solution)/shard_map/ppermute | solution.py:17
  33.3 0.9 %collective-permute-done.15.refs_3_ = bf16[128,128]{1,0:T(8,128)(2,1)S(1)} collective-permute-done((bf16[128,128]{1,0:T(8,128)(2,1)S(1)}, bf16[128,128]{1,0:T(8,128)(2,1)S(1)}, u32[]{:S(2)}, u32[]{:S(2)}) %collective-permute-start.15) | collective-permute-done | bytes 32800 | tf_op jit(solution)/shard_map/ppermute | solution.py:17
  34.2 0.4 shard_map.89
  34.6 1.3 %collective-permute-done.18 = f32[256,128]{1,0:T(8,128)S(1)} collective-permute-done((f32[256,128]{1,0:T(8,128)S(1)}, f32[256,128]{1,0:T(8,128)S(1)}, u32[]{:S(2)}, u32[]{:S(2)}) %collective-permute-start.18) | collective-permute-done | bytes 131104 | tf_op jit(solution)/shard_map/ppermute | solution.py:17
  36.0 1.5 %collective-permute-start.19 = (f16[256,128]{1,0:T(8,128)(2,1)S(1)}, f16[256,128]{1,0:T(8,128)(2,1)S(1)}, u32[]{:S(2)}, u32[]{:S(2)}) collective-permute-start(f16[256,128]{1,0:T(8,128)(2,1)S(1)} %multiply_convert_fusion), channel_id=1, source_target_pairs={{0,2},{1,3},{2,0},{3,1},{4,6},{5,7},{6,4},{7,5},{8,10},{9,11},{10,... | collective-permute-start | bytes 196616 | tf_op jit(solution)/shard_map/ppermute | solution.py:17
  37.5 0.3 shard_map.90
  37.8 0.1 collective-permute-start.17
  37.9 2.4 %collective-permute-done.19 = f16[256,128]{1,0:T(8,128)(2,1)S(1)} collective-permute-done((f16[256,128]{1,0:T(8,128)(2,1)S(1)}, f16[256,128]{1,0:T(8,128)(2,1)S(1)}, u32[]{:S(2)}, u32[]{:S(2)}) %collective-permute-start.19) | collective-permute-done | bytes 65568 | tf_op jit(solution)/shard_map/ppermute | solution.py:17
  40.4 1.1 %shard_map.91 = (f32[256,128]{1,0:T(8,128)}, f32[256,128]{1,0:T(8,128)}, f32[128,128]{1,0:T(8,128)}) custom-call(f32[256,128]{1,0:T(8,128)S(1)} %get-tuple-element.56.refs_0_, f32[256,128]{1,0:T(8,128)S(1)} %collective-permute-done.17.refs_1_, f32[256,128]{1,0:T(8,128)S(1)} %convert_multiply_fusion.refs_2_, f32[1,256,256]{2,1,0:T(8,128)S(1)} %copy-done.2, ...), custom_call_target="tpu_custom_call" | custom-call | bytes 1310720 | tf_op jit(solution)/shard_map/pallas_call | solution.py:57
  (34 shorter events, 0.5 us)
Async XLA Ops:
  0.6 8.7 %copy-start.4 = (bf16[128,512]{1,0:T(8,128)(2,1)S(1)}, bf16[128,512]{1,0:T(8,128)(2,1)}, u32[]{:S(2)}) copy-start(bf16[128,512]{1,0:T(8,128)(2,1)} %features.1) | copy-start | bytes 393220
  0.6 11.5 %copy-start = (bf16[256,512]{1,0:T(8,128)(2,1)S(1)}, bf16[256,512]{1,0:T(8,128)(2,1)}, u32[]{:S(2)}) copy-start(bf16[256,512]{1,0:T(8,128)(2,1)} %centres.1) | copy-start | bytes 786436
  0.7 7.2 %copy-start.1 = (f32[256,128]{1,0:T(8,128)S(1)}, f32[256,128]{1,0:T(8,128)}, u32[]{:S(2)}) copy-start(f32[256,128]{1,0:T(8,128)} %refs_5_.1) | copy-start | bytes 393220
  0.7 10.7 %collective-permute-start.1 = (bf16[128,512]{1,0:T(8,128)(2,1)}, bf16[128,512]{1,0:T(8,128)(2,1)S(1)}, u32[]{:S(2)}, u32[]{:S(2)}) collective-permute-start(bf16[128,512]{1,0:T(8,128)(2,1)} %features.1), channel_id=1, source_target_pairs={{0,8},{1,9},{2,10},{3,11},{4,12},{5,13},{6,14},{7,15},{8,0},{9,1},... | collective-permute-start | bytes 393224 | tf_op jit(solution)/shard_map/ppermute | solution.py:17
  5.8 6.5 %collective-permute-start.5 = (bf16[128,512]{1,0:T(8,128)(2,1)S(1)}, bf16[128,512]{1,0:T(8,128)(2,1)S(1)}, u32[]{:S(2)}, u32[]{:S(2)}) collective-permute-start(bf16[128,512]{1,0:T(8,128)(2,1)S(1)} %get-tuple-element.66), channel_id=1, source_target_pairs={{0,2},{1,3},{2,0},{3,1},{4,6},{5,7},{6,4},{7,5},{8,10},{9,11},{10,... | collective-permute-start | bytes 393224 | tf_op jit(solution)/shard_map/ppermute | solution.py:17
  7.3 7.7 %collective-permute-start.6 = (bf16[128,512]{1,0:T(8,128)(2,1)S(1)}, bf16[128,512]{1,0:T(8,128)(2,1)S(1)}, u32[]{:S(2)}, u32[]{:S(2)}) collective-permute-start(bf16[128,512]{1,0:T(8,128)(2,1)S(1)} %get-tuple-element.65), channel_id=1, source_target_pairs={{0,2},{1,3},{2,0},{3,1},{4,6},{5,7},{6,4},{7,5},{8,10},{9,11},{10,... | collective-permute-start | bytes 393224 | tf_op jit(solution)/shard_map/ppermute | solution.py:17
  7.8 8.5 %collective-permute-start.7 = (f32[256,128]{1,0:T(8,128)S(1)}, f32[256,128]{1,0:T(8,128)S(1)}, u32[]{:S(2)}, u32[]{:S(2)}) collective-permute-start(f32[256,128]{1,0:T(8,128)S(1)} %copy-done.1), channel_id=1, source_target_pairs={{0,2},{1,3},{2,0},{3,1},{4,6},{5,7},{6,4},{7,5},{8,10},{9,11},{10,... | collective-permute-start | bytes 393224 | tf_op jit(solution)/shard_map/ppermute | solution.py:17
  9.4 7.0 %collective-permute-start = (bf16[128,512]{1,0:T(8,128)(2,1)S(1)}, bf16[128,512]{1,0:T(8,128)(2,1)S(1)}, u32[]{:S(2)}, u32[]{:S(2)}) collective-permute-start(bf16[128,512]{1,0:T(8,128)(2,1)S(1)} %copy-done.4), channel_id=1, source_target_pairs={{0,4},{1,5},{2,6},{3,7},{4,0},{5,1},{6,2},{7,3},{8,12},{9,13},{10,... | collective-permute-start | bytes 393224 | tf_op jit(solution)/shard_map/ppermute | solution.py:17
  11.3 5.8 %collective-permute-start.2 = (bf16[128,512]{1,0:T(8,128)(2,1)S(1)}, bf16[128,512]{1,0:T(8,128)(2,1)S(1)}, u32[]{:S(2)}, u32[]{:S(2)}) collective-permute-start(bf16[128,512]{1,0:T(8,128)(2,1)S(1)} %collective-permute-done.1.refs_2_), channel_id=1, source_target_pairs={{0,4},{1,5},{2,6},{3,7},{4,0},{5,1},{6,2},{7,3},{8,12},{9,13},{10,... | collective-permute-start | bytes 393224 | tf_op jit(solution)/shard_map/ppermute | solution.py:17
  12.2 5.5 %collective-permute-start.3 = (bf16[256,512]{1,0:T(8,128)(2,1)S(1)}, bf16[256,512]{1,0:T(8,128)(2,1)S(1)}, u32[]{:S(2)}, u32[]{:S(2)}) collective-permute-start(bf16[256,512]{1,0:T(8,128)(2,1)S(1)} %copy-done), channel_id=1, source_target_pairs={{0,1},{1,0},{2,3},{3,2},{4,5},{5,4},{6,7},{7,6},{8,9},{9,8},{10,11... | collective-permute-start | bytes 786440 | tf_op jit(solution)/shard_map/ppermute | solution.py:17
  15.0 2.7 %collective-permute-start.4 = (f32[256,128]{1,0:T(8,128)S(1)}, f32[256,128]{1,0:T(8,128)S(1)}, u32[]{:S(2)}, u32[]{:S(2)}) collective-permute-start(f32[256,128]{1,0:T(8,128)S(1)} %copy-done.1), channel_id=1, source_target_pairs={{0,1},{1,0},{2,3},{3,2},{4,5},{5,4},{6,7},{7,6},{8,9},{9,8},{10,11... | collective-permute-start | bytes 393224 | tf_op jit(solution)/shard_map/ppermute | solution.py:17
  16.4 1.9 %collective-permute-start.8 = (bf16[128,512]{1,0:T(8,128)(2,1)S(1)}, bf16[128,512]{1,0:T(8,128)(2,1)S(1)}, u32[]{:S(2)}, u32[]{:S(2)}) collective-permute-start(bf16[128,512]{1,0:T(8,128)(2,1)S(1)} %collective-permute-done.5.refs_4_), channel_id=1, source_target_pairs={{0,1},{1,0},{2,3},{3,2},{4,5},{5,4},{6,7},{7,6},{8,9},{9,8},{10,11... | collective-permute-start | bytes 393224 | tf_op jit(solution)/shard_map/ppermute | solution.py:17
  16.4 1.9 %collective-permute-start.9 = (bf16[128,512]{1,0:T(8,128)(2,1)S(1)}, bf16[128,512]{1,0:T(8,128)(2,1)S(1)}, u32[]{:S(2)}, u32[]{:S(2)}) collective-permute-start(bf16[128,512]{1,0:T(8,128)(2,1)S(1)} %collective-permute-done.6.refs_5_), channel_id=1, source_target_pairs={{0,1},{1,0},{2,3},{3,2},{4,5},{5,4},{6,7},{7,6},{8,9},{9,8},{10,11... | collective-permute-start | bytes 393224 | tf_op jit(solution)/shard_map/ppermute | solution.py:17
  17.1 1.3 %collective-permute-start.10 = (f32[256,128]{1,0:T(8,128)S(1)}, f32[256,128]{1,0:T(8,128)S(1)}, u32[]{:S(2)}, u32[]{:S(2)}) collective-permute-start(f32[256,128]{1,0:T(8,128)S(1)} %collective-permute-done.7.refs_8_), channel_id=1, source_target_pairs={{0,1},{1,0},{2,3},{3,2},{4,5},{5,4},{6,7},{7,6},{8,9},{9,8},{10,11... | collective-permute-start | bytes 393224 | tf_op jit(solution)/shard_map/ppermute | solution.py:17
  19.2 5.9 %collective-permute-start.13 = (f16[128,128]{1,0:T(8,128)(2,1)S(1)}, f16[128,128]{1,0:T(8,128)(2,1)S(1)}, u32[]{:S(2)}, u32[]{:S(2)}) collective-permute-start(f16[128,128]{1,0:T(8,128)(2,1)S(1)} %multiply_convert_fusion.1), channel_id=1, source_target_pairs={{0,12},{1,13},{2,14},{3,15},{4,8},{5,9},{6,10},{7,11},{8,4},{9,5},... | collective-permute-start | bytes 98312 | tf_op jit(solution)/shard_map/ppermute | solution.py:17
  22.6 4.9 %collective-permute-start.12 = (f16[128,128]{1,0:T(8,128)(2,1)S(1)}, f16[128,128]{1,0:T(8,128)(2,1)S(1)}, u32[]{:S(2)}, u32[]{:S(2)}) collective-permute-start(f16[128,128]{1,0:T(8,128)(2,1)S(1)} %multiply_convert_fusion.2), channel_id=1, source_target_pairs={{0,8},{1,9},{2,10},{3,11},{4,12},{5,13},{6,14},{7,15},{8,0},{9,1},... | collective-permute-start | bytes 98312 | tf_op jit(solution)/shard_map/ppermute | solution.py:17
  22.7 4.8 %copy-start.5 = (bf16[128,128]{1,0:T(8,128)(2,1)S(1)}, bf16[128,128]{1,0:T(8,128)(2,1)}, u32[]{:S(2)}) copy-start(bf16[128,128]{1,0:T(8,128)(2,1)} %param.8) | copy-start | bytes 98308
  22.7 4.8 %collective-permute-start.11 = (f16[128,128]{1,0:T(8,128)(2,1)S(1)}, f16[128,128]{1,0:T(8,128)(2,1)S(1)}, u32[]{:S(2)}, u32[]{:S(2)}) collective-permute-start(f16[128,128]{1,0:T(8,128)(2,1)S(1)} %multiply_convert_fusion.3), channel_id=1, source_target_pairs={{0,4},{1,5},{2,6},{3,7},{4,0},{5,1},{6,2},{7,3},{8,12},{9,13},{10,... | collective-permute-start | bytes 98312 | tf_op jit(solution)/shard_map/ppermute | solution.py:17
  27.5 5.8 %collective-permute-start.14 = (bf16[128,128]{1,0:T(8,128)(2,1)S(1)}, bf16[128,128]{1,0:T(8,128)(2,1)S(1)}, u32[]{:S(2)}, u32[]{:S(2)}) collective-permute-start(bf16[128,128]{1,0:T(8,128)(2,1)S(1)} %get-tuple-element.63.refs_1_), channel_id=1, source_target_pairs={{0,12},{1,13},{2,14},{3,15},{4,8},{5,9},{6,10},{7,11},{8,4},{9,5},... | collective-permute-start | bytes 98312 | tf_op jit(solution)/shard_map/ppermute | solution.py:17
  29.2 4.9 %collective-permute-start.15 = (bf16[128,128]{1,0:T(8,128)(2,1)S(1)}, bf16[128,128]{1,0:T(8,128)(2,1)S(1)}, u32[]{:S(2)}, u32[]{:S(2)}) collective-permute-start(bf16[128,128]{1,0:T(8,128)(2,1)S(1)} %get-tuple-element.63.refs_1_), channel_id=1, source_target_pairs={{0,8},{1,9},{2,10},{3,11},{4,12},{5,13},{6,14},{7,15},{8,0},{9,1},... | collective-permute-start | bytes 98312 | tf_op jit(solution)/shard_map/ppermute | solution.py:17
  29.7 4.4 %collective-permute-start.16 = (bf16[128,128]{1,0:T(8,128)(2,1)S(1)}, bf16[128,128]{1,0:T(8,128)(2,1)S(1)}, u32[]{:S(2)}, u32[]{:S(2)}) collective-permute-start(bf16[128,128]{1,0:T(8,128)(2,1)S(1)} %get-tuple-element.63.refs_1_), channel_id=1, source_target_pairs={{0,4},{1,5},{2,6},{3,7},{4,0},{5,1},{6,2},{7,3},{8,12},{9,13},{10,... | collective-permute-start | bytes 98312 | tf_op jit(solution)/shard_map/ppermute | solution.py:17
  34.6 1.4 %collective-permute-start.18 = (f32[256,128]{1,0:T(8,128)S(1)}, f32[256,128]{1,0:T(8,128)S(1)}, u32[]{:S(2)}, u32[]{:S(2)}) collective-permute-start(f32[256,128]{1,0:T(8,128)S(1)} %get-tuple-element.59), channel_id=1, source_target_pairs={{0,1},{1,0},{2,3},{3,2},{4,5},{5,4},{6,7},{7,6},{8,9},{9,8},{10,11... | collective-permute-start | bytes 393224 | tf_op jit(solution)/shard_map/ppermute | solution.py:17
  36.0 4.3 %collective-permute-start.19 = (f16[256,128]{1,0:T(8,128)(2,1)S(1)}, f16[256,128]{1,0:T(8,128)(2,1)S(1)}, u32[]{:S(2)}, u32[]{:S(2)}) collective-permute-start(f16[256,128]{1,0:T(8,128)(2,1)S(1)} %multiply_convert_fusion), channel_id=1, source_target_pairs={{0,2},{1,3},{2,0},{3,1},{4,6},{5,7},{6,4},{7,5},{8,10},{9,11},{10,... | collective-permute-start | bytes 196616 | tf_op jit(solution)/shard_map/ppermute | solution.py:17
  37.5 2.9 %copy-start.2 = (f32[1,256,256]{2,1,0:T(8,128)S(1)}, f32[1,256,256]{2,1,0:T(8,128)}, u32[]{:S(2)}) copy-start(f32[1,256,256]{2,1,0:T(8,128)} %refs_3_.1) | copy-start | bytes 786436
  37.8 2.6 %copy-start.3 = (f32[256,128]{1,0:T(8,128)S(1)}, f32[256,128]{1,0:T(8,128)}, u32[]{:S(2)}) copy-start(f32[256,128]{1,0:T(8,128)} %refs_4_.1) | copy-start | bytes 393220
  37.8 2.5 %collective-permute-start.17 = (f32[256,128]{1,0:T(8,128)S(1)}, f32[256,128]{1,0:T(8,128)S(1)}, u32[]{:S(2)}, u32[]{:S(2)}) collective-permute-start(f32[256,128]{1,0:T(8,128)S(1)} %get-tuple-element.57), channel_id=1, source_target_pairs={{0,1},{1,0},{2,3},{3,2},{4,5},{5,4},{6,7},{7,6},{8,9},{9,8},{10,11... | collective-permute-start | bytes 393224 | tf_op jit(solution)/shard_map/ppermute | solution.py:17

commit v7 on v6

--- a/solution.py
+++ b/solution.py
@@ -210,9 +210,9 @@
     far_coef = send(coefficients, far)
     near = [send(centres, core)], [send(coefficients, core)]
     own = own[:1], own[1:]
-    kernel_a, sums_a = predict(rows, own, flops=4 * 10**9)
+    kernel_a, sums_a = predict(rows, own, flops=8 * 10**9)
     kernel_b, sums_b = predict(rows, near, sums_a)
-    far_parts, far_coef, rows[-2] = lax.optimization_barrier((far_parts, far_coef, rows[-2]))
+    far_parts, rows[-2] = lax.optimization_barrier((far_parts, rows[-2]))
     distant = far_parts + [send(x, core) for x in far_parts], [far_coef, send(far_coef, core)]
     kernel_c, sums = predict(rows, distant, sums_b)
     far_kernels, far_layout = [kernel_c], ((0, 0, (0, 1)),)

time: 41.6 us -> 41.5 us (level)
    ppermute x20, waiting for transfers between devices: 14.6 us -> 14.2 us  [swap(): return lax.ppermute(x, 'wide', [(i, i ^ mask) for i in range(size)])]
  transfers between devices with their start and end apart: 20 -> 20, of which waited for: 12 -> 11; matrix products, arithmetic and copies ran while one was open for 2% -> 2% of each run, Pallas kernels for 3% -> 4%
where the time goes in v7:
time: 41.5 us; the launch traced here: 41.3 us
  starting transfers between devices  21.6 us (52%)
  waiting for transfers between devices  14.2 us (34%)
  Pallas kernels  3.63 us (9%)
  local copies, waits for them, and re-layouts  1.01 us (2%)
  between operations  0.84 us (2%)
    ppermute x20, starting transfers between devices, swap(): return lax.ppermute(x, 'wide', [(i, i ^ mask) for i in range(size)])  21.6 us
    ppermute x20, waiting for transfers between devices, swap(): return lax.ppermute(x, 'wide', [(i, i ^ mask) for i in range(size)])  14.2 us
    pallas_call x7, Pallas kernels, whole_call(): pl.pallas_call(body, out_shape=outs, in_specs=[pl.BlockSpec(memory_space=...  3.63 us
    split x1, local copies, waits for them, and re-layouts, shards(): far_parts = [send(part, far) for part in jnp.split(centres, 2)]  0.98 us
  transfers between devices with their start and end apart: 20, of which 11 were waited for; matrix products, arithmetic and copies ran while one was open for 2% of the time, Pallas kernels for 4%

profile of v7, /device:TPU:0, one launch (start us, length us, event | category | flops | bytes accessed | tf_op | source)
XLA Modules:
  0.0 41.3 jit_solution(14206183840758395042)
XLA Ops:
  0.7 4.1 %collective-permute-start.1 = (bf16[128,512]{1,0:T(8,128)(2,1)}, bf16[128,512]{1,0:T(8,128)(2,1)S(1)}, u32[]{:S(2)}, u32[]{:S(2)}) collective-permute-start(bf16[128,512]{1,0:T(8,128)(2,1)} %features.1), channel_id=1, source_target_pairs={{0,8},{1,9},{2,10},{3,11},{4,12},{5,13},{6,14},{7,15},{8,0},{9,1},... | collective-permute-start | bytes 393224 | tf_op jit(solution)/shard_map/ppermute | solution.py:17
  4.8 1.0 %fusion.1 = (bf16[128,512]{1,0:T(8,128)(2,1)S(1)}, bf16[128,512]{1,0:T(8,128)(2,1)S(1)}) fusion(bf16[256,512]{1,0:T(8,128)(2,1)} %centres.1), kind=kLoop, calls=%fused_computation.7 | loop fusion | bytes 524288 | tf_op jit(solution)/shard_map/split | solution.py:209
  5.8 1.6 %collective-permute-start.5 = (bf16[128,512]{1,0:T(8,128)(2,1)S(1)}, bf16[128,512]{1,0:T(8,128)(2,1)S(1)}, u32[]{:S(2)}, u32[]{:S(2)}) collective-permute-start(bf16[128,512]{1,0:T(8,128)(2,1)S(1)} %get-tuple-element.64), channel_id=1, source_target_pairs={{0,2},{1,3},{2,0},{3,1},{4,6},{5,7},{6,4},{7,5},{8,10},{9,11},{10,... | collective-permute-start | bytes 393224 | tf_op jit(solution)/shard_map/ppermute | solution.py:17
  7.3 0.5 %collective-permute-start.6 = (bf16[128,512]{1,0:T(8,128)(2,1)S(1)}, bf16[128,512]{1,0:T(8,128)(2,1)S(1)}, u32[]{:S(2)}, u32[]{:S(2)}) collective-permute-start(bf16[128,512]{1,0:T(8,128)(2,1)S(1)} %get-tuple-element.63), channel_id=1, source_target_pairs={{0,2},{1,3},{2,0},{3,1},{4,6},{5,7},{6,4},{7,5},{8,10},{9,11},{10,... | collective-permute-start | bytes 393224 | tf_op jit(solution)/shard_map/ppermute | solution.py:17
  7.8 1.6 %collective-permute-start = (bf16[128,512]{1,0:T(8,128)(2,1)S(1)}, bf16[128,512]{1,0:T(8,128)(2,1)S(1)}, u32[]{:S(2)}, u32[]{:S(2)}) collective-permute-start(bf16[128,512]{1,0:T(8,128)(2,1)S(1)} %copy-done.4), channel_id=1, source_target_pairs={{0,4},{1,5},{2,6},{3,7},{4,0},{5,1},{6,2},{7,3},{8,12},{9,13},{10,... | collective-permute-start | bytes 393224 | tf_op jit(solution)/shard_map/ppermute | solution.py:17
  9.4 1.5 %collective-permute-start.9 = (f32[256,128]{1,0:T(8,128)S(1)}, f32[256,128]{1,0:T(8,128)S(1)}, u32[]{:S(2)}, u32[]{:S(2)}) collective-permute-start(f32[256,128]{1,0:T(8,128)S(1)} %copy-done.1), channel_id=1, source_target_pairs={{0,2},{1,3},{2,0},{3,1},{4,6},{5,7},{6,4},{7,5},{8,10},{9,11},{10,... | collective-permute-start | bytes 393224 | tf_op jit(solution)/shard_map/ppermute | solution.py:17
  10.9 0.4 %collective-permute-done.1.refs_2_ = bf16[128,512]{1,0:T(8,128)(2,1)S(1)} collective-permute-done((bf16[128,512]{1,0:T(8,128)(2,1)}, bf16[128,512]{1,0:T(8,128)(2,1)S(1)}, u32[]{:S(2)}, u32[]{:S(2)}) %collective-permute-start.1) | collective-permute-done | bytes 131104 | tf_op jit(solution)/shard_map/ppermute | solution.py:17
  11.4 0.8 %collective-permute-start.2 = (bf16[128,512]{1,0:T(8,128)(2,1)S(1)}, bf16[128,512]{1,0:T(8,128)(2,1)S(1)}, u32[]{:S(2)}, u32[]{:S(2)}) collective-permute-start(bf16[128,512]{1,0:T(8,128)(2,1)S(1)} %collective-permute-done.1.refs_2_), channel_id=1, source_target_pairs={{0,4},{1,5},{2,6},{3,7},{4,0},{5,1},{6,2},{7,3},{8,12},{9,13},{10,... | collective-permute-start | bytes 393224 | tf_op jit(solution)/shard_map/ppermute | solution.py:17
  12.3 2.7 %collective-permute-done.6.refs_5_ = bf16[128,512]{1,0:T(8,128)(2,1)S(1)} collective-permute-done((bf16[128,512]{1,0:T(8,128)(2,1)S(1)}, bf16[128,512]{1,0:T(8,128)(2,1)S(1)}, u32[]{:S(2)}, u32[]{:S(2)}) %collective-permute-start.6) | collective-permute-done | bytes 131104 | tf_op jit(solution)/shard_map/ppermute | solution.py:17
  15.0 0.5 %collective-permute-start.7 = (bf16[128,512]{1,0:T(8,128)(2,1)S(1)}, bf16[128,512]{1,0:T(8,128)(2,1)S(1)}, u32[]{:S(2)}, u32[]{:S(2)}) collective-permute-start(bf16[128,512]{1,0:T(8,128)(2,1)S(1)} %collective-permute-done.5.refs_4_), channel_id=1, source_target_pairs={{0,1},{1,0},{2,3},{3,2},{4,5},{5,4},{6,7},{7,6},{8,9},{9,8},{10,11... | collective-permute-start | bytes 393224 | tf_op jit(solution)/shard_map/ppermute | solution.py:17
  15.5 0.9 %collective-permute-done.9.refs_8_ = f32[256,128]{1,0:T(8,128)S(1)} collective-permute-done((f32[256,128]{1,0:T(8,128)S(1)}, f32[256,128]{1,0:T(8,128)S(1)}, u32[]{:S(2)}, u32[]{:S(2)}) %collective-permute-start.9) | collective-permute-done | bytes 131104 | tf_op jit(solution)/shard_map/ppermute | solution.py:17
  16.4 0.3 collective-permute-done.2.refs_3_
  16.7 0.2 collective-permute-start.10
  16.9 0.5 %shard_map.86 = (bf16[512,256]{1,0:T(8,128)(2,1)S(1)}, f32[128,128]{1,0:T(8,128)S(1)}, f32[128,128]{1,0:T(8,128)S(1)}, f32[128,128]{1,0:T(8,128)S(1)}, f32[128,128]{1,0:T(8,128)S(1)}) custom-call(bf16[128,512]{1,0:T(8,128)(2,1)S(1)} %get-tuple-element.32.refs_0_, bf16[128,512]{1,0:T(8,128)(2,1)S(1)} %collective-permute-done.refs_1_, ...), custom_call_target="tpu_custom_call" | custom-call | flops 8000000000 | bytes 1376256 | tf_op jit(solution)/shard_map/pallas_call | solution.py:57
  17.5 0.5 %shard_map.87 = (bf16[512,256]{1,0:T(8,128)(2,1)S(1)}, f32[128,128]{1,0:T(8,128)S(1)}, f32[128,128]{1,0:T(8,128)S(1)}, f32[128,128]{1,0:T(8,128)S(1)}, f32[128,128]{1,0:T(8,128)S(1)}) custom-call(bf16[128,512]{1,0:T(8,128)(2,1)S(1)} %get-tuple-element.32.refs_0_, bf16[128,512]{1,0:T(8,128)(2,1)S(1)} %collective-permute-done.refs_1_, ...), custom_call_target="tpu_custom_call" | custom-call | flops 167772160 | bytes 1703936 | tf_op jit(solution)/shard_map/pallas_call | solution.py:57
  18.0 0.7 %shard_map.88 = (bf16[512,512]{1,0:T(8,128)(2,1)S(1)}, f32[128,128]{1,0:T(8,128)S(1)}, f32[128,128]{1,0:T(8,128)S(1)}, f32[128,128]{1,0:T(8,128)S(1)}, f32[128,128]{1,0:T(8,128)S(1)}) custom-call(bf16[128,512]{1,0:T(8,128)(2,1)S(1)} %get-tuple-element.32.refs_0_, bf16[128,512]{1,0:T(8,128)(2,1)S(1)} %collective-permute-done.refs_1_, ...), custom_call_target="tpu_custom_call" | custom-call | flops 335544320 | bytes 2359296 | tf_op jit(solution)/shard_map/pallas_call | solution.py:57
  18.8 3.7 %collective-permute-start.13 = (f16[128,128]{1,0:T(8,128)(2,1)S(1)}, f16[128,128]{1,0:T(8,128)(2,1)S(1)}, u32[]{:S(2)}, u32[]{:S(2)}) collective-permute-start(f16[128,128]{1,0:T(8,128)(2,1)S(1)} %multiply_convert_fusion.1), channel_id=1, source_target_pairs={{0,12},{1,13},{2,14},{3,15},{4,8},{5,9},{6,10},{7,11},{8,4},{9,5},... | collective-permute-start | bytes 98312 | tf_op jit(solution)/shard_map/ppermute | solution.py:17
  22.6 0.8 %collective-permute-start.11 = (f16[128,128]{1,0:T(8,128)(2,1)S(1)}, f16[128,128]{1,0:T(8,128)(2,1)S(1)}, u32[]{:S(2)}, u32[]{:S(2)}) collective-permute-start(f16[128,128]{1,0:T(8,128)(2,1)S(1)} %multiply_convert_fusion.3), channel_id=1, source_target_pairs={{0,4},{1,5},{2,6},{3,7},{4,0},{5,1},{6,2},{7,3},{8,12},{9,13},{10,... | collective-permute-start | bytes 98312 | tf_op jit(solution)/shard_map/ppermute | solution.py:17
  23.4 1.2 %collective-permute-done.13 = f16[128,128]{1,0:T(8,128)(2,1)S(1)} collective-permute-done((f16[128,128]{1,0:T(8,128)(2,1)S(1)}, f16[128,128]{1,0:T(8,128)(2,1)S(1)}, u32[]{:S(2)}, u32[]{:S(2)}) %collective-permute-start.13) | collective-permute-done | bytes 32800 | tf_op jit(solution)/shard_map/ppermute | solution.py:17
  24.6 2.8 %collective-permute-done.12 = f16[128,128]{1,0:T(8,128)(2,1)S(1)} collective-permute-done((f16[128,128]{1,0:T(8,128)(2,1)S(1)}, f16[128,128]{1,0:T(8,128)(2,1)S(1)}, u32[]{:S(2)}, u32[]{:S(2)}) %collective-permute-start.12) | collective-permute-done | bytes 32800 | tf_op jit(solution)/shard_map/ppermute | solution.py:17
  27.4 1.7 %collective-permute-start.14 = (bf16[128,128]{1,0:T(8,128)(2,1)S(1)}, bf16[128,128]{1,0:T(8,128)(2,1)S(1)}, u32[]{:S(2)}, u32[]{:S(2)}) collective-permute-start(bf16[128,128]{1,0:T(8,128)(2,1)S(1)} %get-tuple-element.61.refs_1_), channel_id=1, source_target_pairs={{0,12},{1,13},{2,14},{3,15},{4,8},{5,9},{6,10},{7,11},{8,4},{9,5},... | collective-permute-start | bytes 98312 | tf_op jit(solution)/shard_map/ppermute | solution.py:17
  29.1 0.6 %collective-permute-start.15 = (bf16[128,128]{1,0:T(8,128)(2,1)S(1)}, bf16[128,128]{1,0:T(8,128)(2,1)S(1)}, u32[]{:S(2)}, u32[]{:S(2)}) collective-permute-start(bf16[128,128]{1,0:T(8,128)(2,1)S(1)} %get-tuple-element.61.refs_1_), channel_id=1, source_target_pairs={{0,8},{1,9},{2,10},{3,11},{4,12},{5,13},{6,14},{7,15},{8,0},{9,1},... | collective-permute-start | bytes 98312 | tf_op jit(solution)/shard_map/ppermute | solution.py:17
  29.6 2.2 %collective-permute-start.16 = (bf16[128,128]{1,0:T(8,128)(2,1)S(1)}, bf16[128,128]{1,0:T(8,128)(2,1)S(1)}, u32[]{:S(2)}, u32[]{:S(2)}) collective-permute-start(bf16[128,128]{1,0:T(8,128)(2,1)S(1)} %get-tuple-element.61.refs_1_), channel_id=1, source_target_pairs={{0,4},{1,5},{2,6},{3,7},{4,0},{5,1},{6,2},{7,3},{8,12},{9,13},{10,... | collective-permute-start | bytes 98312 | tf_op jit(solution)/shard_map/ppermute | solution.py:17
  31.8 1.5 %collective-permute-done.14.refs_2_ = bf16[128,128]{1,0:T(8,128)(2,1)S(1)} collective-permute-done((bf16[128,128]{1,0:T(8,128)(2,1)S(1)}, bf16[128,128]{1,0:T(8,128)(2,1)S(1)}, u32[]{:S(2)}, u32[]{:S(2)}) %collective-permute-start.14) | collective-permute-done | bytes 32800 | tf_op jit(solution)/shard_map/ppermute | solution.py:17
  33.3 0.7 %collective-permute-done.15.refs_3_ = bf16[128,128]{1,0:T(8,128)(2,1)S(1)} collective-permute-done((bf16[128,128]{1,0:T(8,128)(2,1)S(1)}, bf16[128,128]{1,0:T(8,128)(2,1)S(1)}, u32[]{:S(2)}, u32[]{:S(2)}) %collective-permute-start.15) | collective-permute-done | bytes 32800 | tf_op jit(solution)/shard_map/ppermute | solution.py:17
  34.0 0.1 collective-permute-done.16.refs_4_
  34.1 0.4 shard_map.89
  34.5 1.3 %collective-permute-done.18 = f32[256,128]{1,0:T(8,128)S(1)} collective-permute-done((f32[256,128]{1,0:T(8,128)S(1)}, f32[256,128]{1,0:T(8,128)S(1)}, u32[]{:S(2)}, u32[]{:S(2)}) %collective-permute-start.18) | collective-permute-done | bytes 131104 | tf_op jit(solution)/shard_map/ppermute | solution.py:17
  35.9 1.6 %collective-permute-start.19 = (f16[256,128]{1,0:T(8,128)(2,1)S(1)}, f16[256,128]{1,0:T(8,128)(2,1)S(1)}, u32[]{:S(2)}, u32[]{:S(2)}) collective-permute-start(f16[256,128]{1,0:T(8,128)(2,1)S(1)} %multiply_convert_fusion), channel_id=1, source_target_pairs={{0,2},{1,3},{2,0},{3,1},{4,6},{5,7},{6,4},{7,5},{8,10},{9,11},{10,... | collective-permute-start | bytes 196616 | tf_op jit(solution)/shard_map/ppermute | solution.py:17
  37.5 0.3 shard_map.90
  37.9 2.3 %collective-permute-done.19 = f16[256,128]{1,0:T(8,128)(2,1)S(1)} collective-permute-done((f16[256,128]{1,0:T(8,128)(2,1)S(1)}, f16[256,128]{1,0:T(8,128)(2,1)S(1)}, u32[]{:S(2)}, u32[]{:S(2)}) %collective-permute-start.19) | collective-permute-done | bytes 65568 | tf_op jit(solution)/shard_map/ppermute | solution.py:17
  40.3 1.1 %shard_map.91 = (f32[256,128]{1,0:T(8,128)}, f32[256,128]{1,0:T(8,128)}, f32[128,128]{1,0:T(8,128)}) custom-call(f32[256,128]{1,0:T(8,128)S(1)} %get-tuple-element.54.refs_0_, f32[256,128]{1,0:T(8,128)S(1)} %collective-permute-done.17.refs_1_, f32[256,128]{1,0:T(8,128)S(1)} %convert_multiply_fusion.refs_2_, f32[1,256,256]{2,1,0:T(8,128)S(1)} %copy-done.2, ...), custom_call_target="tpu_custom_call" | custom-call | bytes 1310720 | tf_op jit(solution)/shard_map/pallas_call | solution.py:57
  (34 shorter events, 0.5 us)
Async XLA Ops:
  0.6 7.2 %copy-start.4 = (bf16[128,512]{1,0:T(8,128)(2,1)S(1)}, bf16[128,512]{1,0:T(8,128)(2,1)}, u32[]{:S(2)}) copy-start(bf16[128,512]{1,0:T(8,128)(2,1)} %features.1) | copy-start | bytes 393220
  0.6 11.5 %copy-start = (bf16[256,512]{1,0:T(8,128)(2,1)S(1)}, bf16[256,512]{1,0:T(8,128)(2,1)}, u32[]{:S(2)}) copy-start(bf16[256,512]{1,0:T(8,128)(2,1)} %centres.1) | copy-start | bytes 786436
  0.7 8.8 %copy-start.1 = (f32[256,128]{1,0:T(8,128)S(1)}, f32[256,128]{1,0:T(8,128)}, u32[]{:S(2)}) copy-start(f32[256,128]{1,0:T(8,128)} %refs_5_.1) | copy-start | bytes 393220
  0.7 10.7 %collective-permute-start.1 = (bf16[128,512]{1,0:T(8,128)(2,1)}, bf16[128,512]{1,0:T(8,128)(2,1)S(1)}, u32[]{:S(2)}, u32[]{:S(2)}) collective-permute-start(bf16[128,512]{1,0:T(8,128)(2,1)} %features.1), channel_id=1, source_target_pairs={{0,8},{1,9},{2,10},{3,11},{4,12},{5,13},{6,14},{7,15},{8,0},{9,1},... | collective-permute-start | bytes 393224 | tf_op jit(solution)/shard_map/ppermute | solution.py:17
  5.8 6.5 %collective-permute-start.5 = (bf16[128,512]{1,0:T(8,128)(2,1)S(1)}, bf16[128,512]{1,0:T(8,128)(2,1)S(1)}, u32[]{:S(2)}, u32[]{:S(2)}) collective-permute-start(bf16[128,512]{1,0:T(8,128)(2,1)S(1)} %get-tuple-element.64), channel_id=1, source_target_pairs={{0,2},{1,3},{2,0},{3,1},{4,6},{5,7},{6,4},{7,5},{8,10},{9,11},{10,... | collective-permute-start | bytes 393224 | tf_op jit(solution)/shard_map/ppermute | solution.py:17
  7.3 7.7 %collective-permute-start.6 = (bf16[128,512]{1,0:T(8,128)(2,1)S(1)}, bf16[128,512]{1,0:T(8,128)(2,1)S(1)}, u32[]{:S(2)}, u32[]{:S(2)}) collective-permute-start(bf16[128,512]{1,0:T(8,128)(2,1)S(1)} %get-tuple-element.63), channel_id=1, source_target_pairs={{0,2},{1,3},{2,0},{3,1},{4,6},{5,7},{6,4},{7,5},{8,10},{9,11},{10,... | collective-permute-start | bytes 393224 | tf_op jit(solution)/shard_map/ppermute | solution.py:17
  7.8 7.1 %collective-permute-start = (bf16[128,512]{1,0:T(8,128)(2,1)S(1)}, bf16[128,512]{1,0:T(8,128)(2,1)S(1)}, u32[]{:S(2)}, u32[]{:S(2)}) collective-permute-start(bf16[128,512]{1,0:T(8,128)(2,1)S(1)} %copy-done.4), channel_id=1, source_target_pairs={{0,4},{1,5},{2,6},{3,7},{4,0},{5,1},{6,2},{7,3},{8,12},{9,13},{10,... | collective-permute-start | bytes 393224 | tf_op jit(solution)/shard_map/ppermute | solution.py:17
  9.4 7.0 %collective-permute-start.9 = (f32[256,128]{1,0:T(8,128)S(1)}, f32[256,128]{1,0:T(8,128)S(1)}, u32[]{:S(2)}, u32[]{:S(2)}) collective-permute-start(f32[256,128]{1,0:T(8,128)S(1)} %copy-done.1), channel_id=1, source_target_pairs={{0,2},{1,3},{2,0},{3,1},{4,6},{5,7},{6,4},{7,5},{8,10},{9,11},{10,... | collective-permute-start | bytes 393224 | tf_op jit(solution)/shard_map/ppermute | solution.py:17
  11.4 5.3 %collective-permute-start.2 = (bf16[128,512]{1,0:T(8,128)(2,1)S(1)}, bf16[128,512]{1,0:T(8,128)(2,1)S(1)}, u32[]{:S(2)}, u32[]{:S(2)}) collective-permute-start(bf16[128,512]{1,0:T(8,128)(2,1)S(1)} %collective-permute-done.1.refs_2_), channel_id=1, source_target_pairs={{0,4},{1,5},{2,6},{3,7},{4,0},{5,1},{6,2},{7,3},{8,12},{9,13},{10,... | collective-permute-start | bytes 393224 | tf_op jit(solution)/shard_map/ppermute | solution.py:17
  12.2 5.2 %collective-permute-start.3 = (bf16[256,512]{1,0:T(8,128)(2,1)S(1)}, bf16[256,512]{1,0:T(8,128)(2,1)S(1)}, u32[]{:S(2)}, u32[]{:S(2)}) collective-permute-start(bf16[256,512]{1,0:T(8,128)(2,1)S(1)} %copy-done), channel_id=1, source_target_pairs={{0,1},{1,0},{2,3},{3,2},{4,5},{5,4},{6,7},{7,6},{8,9},{9,8},{10,11... | collective-permute-start | bytes 786440 | tf_op jit(solution)/shard_map/ppermute | solution.py:17
  15.0 2.5 %collective-permute-start.4 = (f32[256,128]{1,0:T(8,128)S(1)}, f32[256,128]{1,0:T(8,128)S(1)}, u32[]{:S(2)}, u32[]{:S(2)}) collective-permute-start(f32[256,128]{1,0:T(8,128)S(1)} %copy-done.1), channel_id=1, source_target_pairs={{0,1},{1,0},{2,3},{3,2},{4,5},{5,4},{6,7},{7,6},{8,9},{9,8},{10,11... | collective-permute-start | bytes 393224 | tf_op jit(solution)/shard_map/ppermute | solution.py:17
  15.0 3.0 %collective-permute-start.7 = (bf16[128,512]{1,0:T(8,128)(2,1)S(1)}, bf16[128,512]{1,0:T(8,128)(2,1)S(1)}, u32[]{:S(2)}, u32[]{:S(2)}) collective-permute-start(bf16[128,512]{1,0:T(8,128)(2,1)S(1)} %collective-permute-done.5.refs_4_), channel_id=1, source_target_pairs={{0,1},{1,0},{2,3},{3,2},{4,5},{5,4},{6,7},{7,6},{8,9},{9,8},{10,11... | collective-permute-start | bytes 393224 | tf_op jit(solution)/shard_map/ppermute | solution.py:17
  16.4 1.6 %collective-permute-start.8 = (bf16[128,512]{1,0:T(8,128)(2,1)S(1)}, bf16[128,512]{1,0:T(8,128)(2,1)S(1)}, u32[]{:S(2)}, u32[]{:S(2)}) collective-permute-start(bf16[128,512]{1,0:T(8,128)(2,1)S(1)} %collective-permute-done.6.refs_5_), channel_id=1, source_target_pairs={{0,1},{1,0},{2,3},{3,2},{4,5},{5,4},{6,7},{7,6},{8,9},{9,8},{10,11... | collective-permute-start | bytes 393224 | tf_op jit(solution)/shard_map/ppermute | solution.py:17
  16.7 1.3 %collective-permute-start.10 = (f32[256,128]{1,0:T(8,128)S(1)}, f32[256,128]{1,0:T(8,128)S(1)}, u32[]{:S(2)}, u32[]{:S(2)}) collective-permute-start(f32[256,128]{1,0:T(8,128)S(1)} %collective-permute-done.9.refs_8_), channel_id=1, source_target_pairs={{0,1},{1,0},{2,3},{3,2},{4,5},{5,4},{6,7},{7,6},{8,9},{9,8},{10,11... | collective-permute-start | bytes 393224 | tf_op jit(solution)/shard_map/ppermute | solution.py:17
  18.8 5.8 %collective-permute-start.13 = (f16[128,128]{1,0:T(8,128)(2,1)S(1)}, f16[128,128]{1,0:T(8,128)(2,1)S(1)}, u32[]{:S(2)}, u32[]{:S(2)}) collective-permute-start(f16[128,128]{1,0:T(8,128)(2,1)S(1)} %multiply_convert_fusion.1), channel_id=1, source_target_pairs={{0,12},{1,13},{2,14},{3,15},{4,8},{5,9},{6,10},{7,11},{8,4},{9,5},... | collective-permute-start | bytes 98312 | tf_op jit(solution)/shard_map/ppermute | solution.py:17
  22.5 4.9 %collective-permute-start.12 = (f16[128,128]{1,0:T(8,128)(2,1)S(1)}, f16[128,128]{1,0:T(8,128)(2,1)S(1)}, u32[]{:S(2)}, u32[]{:S(2)}) collective-permute-start(f16[128,128]{1,0:T(8,128)(2,1)S(1)} %multiply_convert_fusion.2), channel_id=1, source_target_pairs={{0,8},{1,9},{2,10},{3,11},{4,12},{5,13},{6,14},{7,15},{8,0},{9,1},... | collective-permute-start | bytes 98312 | tf_op jit(solution)/shard_map/ppermute | solution.py:17
  22.5 4.8 %copy-start.5 = (bf16[128,128]{1,0:T(8,128)(2,1)S(1)}, bf16[128,128]{1,0:T(8,128)(2,1)}, u32[]{:S(2)}) copy-start(bf16[128,128]{1,0:T(8,128)(2,1)} %param.8) | copy-start | bytes 98308
  22.6 4.8 %collective-permute-start.11 = (f16[128,128]{1,0:T(8,128)(2,1)S(1)}, f16[128,128]{1,0:T(8,128)(2,1)S(1)}, u32[]{:S(2)}, u32[]{:S(2)}) collective-permute-start(f16[128,128]{1,0:T(8,128)(2,1)S(1)} %multiply_convert_fusion.3), channel_id=1, source_target_pairs={{0,4},{1,5},{2,6},{3,7},{4,0},{5,1},{6,2},{7,3},{8,12},{9,13},{10,... | collective-permute-start | bytes 98312 | tf_op jit(solution)/shard_map/ppermute | solution.py:17
  27.4 5.9 %collective-permute-start.14 = (bf16[128,128]{1,0:T(8,128)(2,1)S(1)}, bf16[128,128]{1,0:T(8,128)(2,1)S(1)}, u32[]{:S(2)}, u32[]{:S(2)}) collective-permute-start(bf16[128,128]{1,0:T(8,128)(2,1)S(1)} %get-tuple-element.61.refs_1_), channel_id=1, source_target_pairs={{0,12},{1,13},{2,14},{3,15},{4,8},{5,9},{6,10},{7,11},{8,4},{9,5},... | collective-permute-start | bytes 98312 | tf_op jit(solution)/shard_map/ppermute | solution.py:17
  29.1 4.9 %collective-permute-start.15 = (bf16[128,128]{1,0:T(8,128)(2,1)S(1)}, bf16[128,128]{1,0:T(8,128)(2,1)S(1)}, u32[]{:S(2)}, u32[]{:S(2)}) collective-permute-start(bf16[128,128]{1,0:T(8,128)(2,1)S(1)} %get-tuple-element.61.refs_1_), channel_id=1, source_target_pairs={{0,8},{1,9},{2,10},{3,11},{4,12},{5,13},{6,14},{7,15},{8,0},{9,1},... | collective-permute-start | bytes 98312 | tf_op jit(solution)/shard_map/ppermute | solution.py:17
  29.6 4.4 %collective-permute-start.16 = (bf16[128,128]{1,0:T(8,128)(2,1)S(1)}, bf16[128,128]{1,0:T(8,128)(2,1)S(1)}, u32[]{:S(2)}, u32[]{:S(2)}) collective-permute-start(bf16[128,128]{1,0:T(8,128)(2,1)S(1)} %get-tuple-element.61.refs_1_), channel_id=1, source_target_pairs={{0,4},{1,5},{2,6},{3,7},{4,0},{5,1},{6,2},{7,3},{8,12},{9,13},{10,... | collective-permute-start | bytes 98312 | tf_op jit(solution)/shard_map/ppermute | solution.py:17
  34.4 1.4 %collective-permute-start.18 = (f32[256,128]{1,0:T(8,128)S(1)}, f32[256,128]{1,0:T(8,128)S(1)}, u32[]{:S(2)}, u32[]{:S(2)}) collective-permute-start(f32[256,128]{1,0:T(8,128)S(1)} %get-tuple-element.57), channel_id=1, source_target_pairs={{0,1},{1,0},{2,3},{3,2},{4,5},{5,4},{6,7},{7,6},{8,9},{9,8},{10,11... | collective-permute-start | bytes 393224 | tf_op jit(solution)/shard_map/ppermute | solution.py:17
  35.9 4.3 %collective-permute-start.19 = (f16[256,128]{1,0:T(8,128)(2,1)S(1)}, f16[256,128]{1,0:T(8,128)(2,1)S(1)}, u32[]{:S(2)}, u32[]{:S(2)}) collective-permute-start(f16[256,128]{1,0:T(8,128)(2,1)S(1)} %multiply_convert_fusion), channel_id=1, source_target_pairs={{0,2},{1,3},{2,0},{3,1},{4,6},{5,7},{6,4},{7,5},{8,10},{9,11},{10,... | collective-permute-start | bytes 196616 | tf_op jit(solution)/shard_map/ppermute | solution.py:17
  37.5 2.8 %copy-start.2 = (f32[1,256,256]{2,1,0:T(8,128)S(1)}, f32[1,256,256]{2,1,0:T(8,128)}, u32[]{:S(2)}) copy-start(f32[1,256,256]{2,1,0:T(8,128)} %refs_3_.1) | copy-start | bytes 786436
  37.8 2.4 %copy-start.3 = (f32[256,128]{1,0:T(8,128)S(1)}, f32[256,128]{1,0:T(8,128)}, u32[]{:S(2)}) copy-start(f32[256,128]{1,0:T(8,128)} %refs_4_.1) | copy-start | bytes 393220
  37.8 2.4 %collective-permute-start.17 = (f32[256,128]{1,0:T(8,128)S(1)}, f32[256,128]{1,0:T(8,128)S(1)}, u32[]{:S(2)}, u32[]{:S(2)}) collective-permute-start(f32[256,128]{1,0:T(8,128)S(1)} %get-tuple-element.55), channel_id=1, source_target_pairs={{0,1},{1,0},{2,3},{3,2},{4,5},{5,4},{6,7},{7,6},{8,9},{9,8},{10,11... | collective-permute-start | bytes 393224 | tf_op jit(solution)/shard_map/ppermute | solution.py:17

commit v8 on v7

--- a/solution.py
+++ b/solution.py
@@ -177,20 +177,24 @@
     return whole_call(body, [out, out] + joined, [*kernels, pieces[0], *pieces[:0:-1]], flops=4 * total * count * columns)
 
 
-def update_body(batch, npart, *refs):
-    parts, refs = refs[:npart], refs[npart:]
-    inverse, momentum, coefficients, residual, new_momentum, new_coefficients, out = refs
+def product(inverse, gradient, b):
+    order = inverse.shape[1]
+    at = slice(b * order, (b + 1) * order)
+    return at, jnp.dot(inverse[b], gradient[at, :], precision=lax.Precision.HIGHEST, preferred_element_type=F32)
+
+
+def begin_body(batch, keep, got, inverse, momentum, residual, begun, out):
     out[...] = residual[...]
-    gradient = parts[0][...]
-    for part in parts[1:]:
-        gradient += part[...]
-    nblocks, order = inverse.shape[0], inverse.shape[1]
-    for b in range(nblocks):
-        at = slice(b * order, (b + 1) * order)
-        conditioned = jnp.dot(
-            inverse[b], gradient[at], precision=lax.Precision.HIGHEST, preferred_element_type=F32
-        )
-        moved = 0.9 * momentum[at, :] + conditioned / batch
+    gradient = keep[...] + got[...]
+    for b in range(inverse.shape[0]):
+        at, conditioned = product(inverse, gradient, b)
+        begun[at, :] = 0.9 * momentum[at, :] + conditioned / batch
+
+
+def update_body(batch, arrived, inverse, begun, coefficients, new_momentum, new_coefficients):
+    for b in range(inverse.shape[0]):
+        at, conditioned = product(inverse, arrived[...], b)
+        moved = begun[at, :] + conditioned / batch
         new_momentum[at, :] = moved
         new_coefficients[at, :] = coefficients[at, :] - 0.5 * moved
 
@@ -238,12 +242,14 @@
     far_keep, far_give, joined = gradients(far_kernels, far_layout, residuals, count)
     arrived = send((factor * (far_keep + send(far_give, core))).astype(kind), far).astype(F32) / factor
     keep, give = gradients(near_kernels, near_layout, [joined], count)
-    parts = [keep, send(give, core), arrived]
     out = jax.ShapeDtypeStruct(momentum.shape, F32)
-    new_momentum, new_coefficients, residual = whole_call(
-        functools.partial(update_body, batch, len(parts)),
-        [out, out, held],
-        [*parts, block_inverse, momentum, coefficients, residual],
+    begun, residual = whole_call(
+        functools.partial(begin_body, batch),
+        [out, held],
+        [keep, send(give, core), block_inverse, momentum, residual],
+    )
+    new_momentum, new_coefficients = whole_call(
+        functools.partial(update_body, batch), [out, out], [arrived, block_inverse, begun, coefficients]
     )
     return residual, new_momentum, new_coefficients
 

time: 41.5 us -> 41.5 us (level)
  waiting for transfers between devices: 14.2 us -> 12.8 us
  Pallas kernels: 3.63 us -> 4.48 us
    ppermute x20, waiting for transfers between devices: 14.2 us -> 12.8 us  [swap(): return lax.ppermute(x, 'wide', [(i, i ^ mask) for i in range(size)])]
    pallas_call x7 -> x8, Pallas kernels: 3.63 us -> 4.48 us  [whole_call(): pl.pallas_call(body, out_shape=outs, in_specs=[pl.BlockSpec(memory_space=...]
    ppermute x20, starting transfers between devices: 21.6 us -> 22 us  [swap(): return lax.ppermute(x, 'wide', [(i, i ^ mask) for i in range(size)])]
  transfers between devices with their start and end apart: 20 -> 20, of which waited for: 11 -> 11; matrix products, arithmetic and copies ran while one was open for 2% -> 2% of each run, Pallas kernels for 4% -> 6%
where the time goes in v8:
time: 41.5 us; the launch traced here: 41.3 us
  starting transfers between devices  22 us (53%)
  waiting for transfers between devices  12.8 us (31%)
  Pallas kernels  4.48 us (11%)
  local copies, waits for them, and re-layouts  1.02 us (2%)
  between operations  0.82 us (2%)
    ppermute x20, starting transfers between devices, swap(): return lax.ppermute(x, 'wide', [(i, i ^ mask) for i in range(size)])  22 us
    ppermute x20, waiting for transfers between devices, swap(): return lax.ppermute(x, 'wide', [(i, i ^ mask) for i in range(size)])  12.8 us
    pallas_call x8, Pallas kernels, whole_call(): pl.pallas_call(body, out_shape=outs, in_specs=[pl.BlockSpec(memory_space=...  4.48 us
    split x1, local copies, waits for them, and re-layouts, shards(): far_parts = [send(part, far) for part in jnp.split(centres, 2)]  0.98 us
  transfers between devices with their start and end apart: 20, of which 11 were waited for; matrix products, arithmetic and copies ran while one was open for 2% of the time, Pallas kernels for 6%

profile of v8, /device:TPU:0, one launch (start us, length us, event | category | flops | bytes accessed | tf_op | source)
XLA Modules:
  0.0 41.3 jit_solution(6278060990612553297)
XLA Ops:
  0.7 4.1 %collective-permute-start.1 = (bf16[128,512]{1,0:T(8,128)(2,1)}, bf16[128,512]{1,0:T(8,128)(2,1)S(1)}, u32[]{:S(2)}, u32[]{:S(2)}) collective-permute-start(bf16[128,512]{1,0:T(8,128)(2,1)} %features.1), channel_id=1, source_target_pairs={{0,8},{1,9},{2,10},{3,11},{4,12},{5,13},{6,14},{7,15},{8,0},{9,1},... | collective-permute-start | bytes 393224 | tf_op jit(solution)/shard_map/ppermute | solution.py:17
  4.8 1.0 %fusion.1 = (bf16[128,512]{1,0:T(8,128)(2,1)S(1)}, bf16[128,512]{1,0:T(8,128)(2,1)S(1)}) fusion(bf16[256,512]{1,0:T(8,128)(2,1)} %centres.1), kind=kLoop, calls=%fused_computation.7 | loop fusion | bytes 524288 | tf_op jit(solution)/shard_map/split | solution.py:213
  5.8 1.6 %collective-permute-start.5 = (bf16[128,512]{1,0:T(8,128)(2,1)S(1)}, bf16[128,512]{1,0:T(8,128)(2,1)S(1)}, u32[]{:S(2)}, u32[]{:S(2)}) collective-permute-start(bf16[128,512]{1,0:T(8,128)(2,1)S(1)} %get-tuple-element.66), channel_id=1, source_target_pairs={{0,2},{1,3},{2,0},{3,1},{4,6},{5,7},{6,4},{7,5},{8,10},{9,11},{10,... | collective-permute-start | bytes 393224 | tf_op jit(solution)/shard_map/ppermute | solution.py:17
  7.3 0.5 %collective-permute-start.6 = (bf16[128,512]{1,0:T(8,128)(2,1)S(1)}, bf16[128,512]{1,0:T(8,128)(2,1)S(1)}, u32[]{:S(2)}, u32[]{:S(2)}) collective-permute-start(bf16[128,512]{1,0:T(8,128)(2,1)S(1)} %get-tuple-element.65), channel_id=1, source_target_pairs={{0,2},{1,3},{2,0},{3,1},{4,6},{5,7},{6,4},{7,5},{8,10},{9,11},{10,... | collective-permute-start | bytes 393224 | tf_op jit(solution)/shard_map/ppermute | solution.py:17
  7.8 1.6 %collective-permute-start = (bf16[128,512]{1,0:T(8,128)(2,1)S(1)}, bf16[128,512]{1,0:T(8,128)(2,1)S(1)}, u32[]{:S(2)}, u32[]{:S(2)}) collective-permute-start(bf16[128,512]{1,0:T(8,128)(2,1)S(1)} %copy-done.3), channel_id=1, source_target_pairs={{0,4},{1,5},{2,6},{3,7},{4,0},{5,1},{6,2},{7,3},{8,12},{9,13},{10,... | collective-permute-start | bytes 393224 | tf_op jit(solution)/shard_map/ppermute | solution.py:17
  9.4 1.5 %collective-permute-start.9 = (f32[256,128]{1,0:T(8,128)S(1)}, f32[256,128]{1,0:T(8,128)S(1)}, u32[]{:S(2)}, u32[]{:S(2)}) collective-permute-start(f32[256,128]{1,0:T(8,128)S(1)} %copy-done.2), channel_id=1, source_target_pairs={{0,2},{1,3},{2,0},{3,1},{4,6},{5,7},{6,4},{7,5},{8,10},{9,11},{10,... | collective-permute-start | bytes 393224 | tf_op jit(solution)/shard_map/ppermute | solution.py:17
  10.9 0.4 %collective-permute-done.1.refs_2_ = bf16[128,512]{1,0:T(8,128)(2,1)S(1)} collective-permute-done((bf16[128,512]{1,0:T(8,128)(2,1)}, bf16[128,512]{1,0:T(8,128)(2,1)S(1)}, u32[]{:S(2)}, u32[]{:S(2)}) %collective-permute-start.1) | collective-permute-done | bytes 131104 | tf_op jit(solution)/shard_map/ppermute | solution.py:17
  11.4 0.8 %collective-permute-start.2 = (bf16[128,512]{1,0:T(8,128)(2,1)S(1)}, bf16[128,512]{1,0:T(8,128)(2,1)S(1)}, u32[]{:S(2)}, u32[]{:S(2)}) collective-permute-start(bf16[128,512]{1,0:T(8,128)(2,1)S(1)} %collective-permute-done.1.refs_2_), channel_id=1, source_target_pairs={{0,4},{1,5},{2,6},{3,7},{4,0},{5,1},{6,2},{7,3},{8,12},{9,13},{10,... | collective-permute-start | bytes 393224 | tf_op jit(solution)/shard_map/ppermute | solution.py:17
  12.3 2.7 %collective-permute-done.6.refs_5_ = bf16[128,512]{1,0:T(8,128)(2,1)S(1)} collective-permute-done((bf16[128,512]{1,0:T(8,128)(2,1)S(1)}, bf16[128,512]{1,0:T(8,128)(2,1)S(1)}, u32[]{:S(2)}, u32[]{:S(2)}) %collective-permute-start.6) | collective-permute-done | bytes 131104 | tf_op jit(solution)/shard_map/ppermute | solution.py:17
  15.0 0.5 %collective-permute-start.7 = (bf16[128,512]{1,0:T(8,128)(2,1)S(1)}, bf16[128,512]{1,0:T(8,128)(2,1)S(1)}, u32[]{:S(2)}, u32[]{:S(2)}) collective-permute-start(bf16[128,512]{1,0:T(8,128)(2,1)S(1)} %collective-permute-done.5.refs_4_), channel_id=1, source_target_pairs={{0,1},{1,0},{2,3},{3,2},{4,5},{5,4},{6,7},{7,6},{8,9},{9,8},{10,11... | collective-permute-start | bytes 393224 | tf_op jit(solution)/shard_map/ppermute | solution.py:17
  15.5 0.9 %collective-permute-done.9.refs_8_ = f32[256,128]{1,0:T(8,128)S(1)} collective-permute-done((f32[256,128]{1,0:T(8,128)S(1)}, f32[256,128]{1,0:T(8,128)S(1)}, u32[]{:S(2)}, u32[]{:S(2)}) %collective-permute-start.9) | collective-permute-done | bytes 131104 | tf_op jit(solution)/shard_map/ppermute | solution.py:17
  16.4 0.3 collective-permute-done.2.refs_3_
  16.9 0.5 %shard_map.86 = (bf16[512,256]{1,0:T(8,128)(2,1)S(1)}, f32[128,128]{1,0:T(8,128)S(1)}, f32[128,128]{1,0:T(8,128)S(1)}, f32[128,128]{1,0:T(8,128)S(1)}, f32[128,128]{1,0:T(8,128)S(1)}) custom-call(bf16[128,512]{1,0:T(8,128)(2,1)S(1)} %get-tuple-element.33.refs_0_, bf16[128,512]{1,0:T(8,128)(2,1)S(1)} %collective-permute-done.refs_1_, ...), custom_call_target="tpu_custom_call" | custom-call | flops 8000000000 | bytes 1376256 | tf_op jit(solution)/shard_map/pallas_call | solution.py:57
  17.5 0.5 %shard_map.87 = (bf16[512,256]{1,0:T(8,128)(2,1)S(1)}, f32[128,128]{1,0:T(8,128)S(1)}, f32[128,128]{1,0:T(8,128)S(1)}, f32[128,128]{1,0:T(8,128)S(1)}, f32[128,128]{1,0:T(8,128)S(1)}) custom-call(bf16[128,512]{1,0:T(8,128)(2,1)S(1)} %get-tuple-element.33.refs_0_, bf16[128,512]{1,0:T(8,128)(2,1)S(1)} %collective-permute-done.refs_1_, ...), custom_call_target="tpu_custom_call" | custom-call | flops 167772160 | bytes 1703936 | tf_op jit(solution)/shard_map/pallas_call | solution.py:57
  18.0 0.7 %shard_map.88 = (bf16[512,512]{1,0:T(8,128)(2,1)S(1)}, f32[128,128]{1,0:T(8,128)S(1)}, f32[128,128]{1,0:T(8,128)S(1)}, f32[128,128]{1,0:T(8,128)S(1)}, f32[128,128]{1,0:T(8,128)S(1)}) custom-call(bf16[128,512]{1,0:T(8,128)(2,1)S(1)} %get-tuple-element.33.refs_0_, bf16[128,512]{1,0:T(8,128)(2,1)S(1)} %collective-permute-done.refs_1_, ...), custom_call_target="tpu_custom_call" | custom-call | flops 335544320 | bytes 2359296 | tf_op jit(solution)/shard_map/pallas_call | solution.py:57
  18.8 3.7 %collective-permute-start.13 = (f16[128,128]{1,0:T(8,128)(2,1)S(1)}, f16[128,128]{1,0:T(8,128)(2,1)S(1)}, u32[]{:S(2)}, u32[]{:S(2)}) collective-permute-start(f16[128,128]{1,0:T(8,128)(2,1)S(1)} %multiply_convert_fusion.1), channel_id=1, source_target_pairs={{0,12},{1,13},{2,14},{3,15},{4,8},{5,9},{6,10},{7,11},{8,4},{9,5},... | collective-permute-start | bytes 98312 | tf_op jit(solution)/shard_map/ppermute | solution.py:17
  22.6 0.8 %collective-permute-start.11 = (f16[128,128]{1,0:T(8,128)(2,1)S(1)}, f16[128,128]{1,0:T(8,128)(2,1)S(1)}, u32[]{:S(2)}, u32[]{:S(2)}) collective-permute-start(f16[128,128]{1,0:T(8,128)(2,1)S(1)} %multiply_convert_fusion.3), channel_id=1, source_target_pairs={{0,4},{1,5},{2,6},{3,7},{4,0},{5,1},{6,2},{7,3},{8,12},{9,13},{10,... | collective-permute-start | bytes 98312 | tf_op jit(solution)/shard_map/ppermute | solution.py:17
  23.4 1.2 %collective-permute-done.13 = f16[128,128]{1,0:T(8,128)(2,1)S(1)} collective-permute-done((f16[128,128]{1,0:T(8,128)(2,1)S(1)}, f16[128,128]{1,0:T(8,128)(2,1)S(1)}, u32[]{:S(2)}, u32[]{:S(2)}) %collective-permute-start.13) | collective-permute-done | bytes 32800 | tf_op jit(solution)/shard_map/ppermute | solution.py:17
  24.6 2.8 %collective-permute-done.12 = f16[128,128]{1,0:T(8,128)(2,1)S(1)} collective-permute-done((f16[128,128]{1,0:T(8,128)(2,1)S(1)}, f16[128,128]{1,0:T(8,128)(2,1)S(1)}, u32[]{:S(2)}, u32[]{:S(2)}) %collective-permute-start.12) | collective-permute-done | bytes 32800 | tf_op jit(solution)/shard_map/ppermute | solution.py:17
  27.4 1.7 %collective-permute-start.14 = (bf16[128,128]{1,0:T(8,128)(2,1)S(1)}, bf16[128,128]{1,0:T(8,128)(2,1)S(1)}, u32[]{:S(2)}, u32[]{:S(2)}) collective-permute-start(bf16[128,128]{1,0:T(8,128)(2,1)S(1)} %get-tuple-element.63.refs_1_), channel_id=1, source_target_pairs={{0,12},{1,13},{2,14},{3,15},{4,8},{5,9},{6,10},{7,11},{8,4},{9,5},... | collective-permute-start | bytes 98312 | tf_op jit(solution)/shard_map/ppermute | solution.py:17
  29.1 0.6 %collective-permute-start.15 = (bf16[128,128]{1,0:T(8,128)(2,1)S(1)}, bf16[128,128]{1,0:T(8,128)(2,1)S(1)}, u32[]{:S(2)}, u32[]{:S(2)}) collective-permute-start(bf16[128,128]{1,0:T(8,128)(2,1)S(1)} %get-tuple-element.63.refs_1_), channel_id=1, source_target_pairs={{0,8},{1,9},{2,10},{3,11},{4,12},{5,13},{6,14},{7,15},{8,0},{9,1},... | collective-permute-start | bytes 98312 | tf_op jit(solution)/shard_map/ppermute | solution.py:17
  29.6 2.2 %collective-permute-start.16 = (bf16[128,128]{1,0:T(8,128)(2,1)S(1)}, bf16[128,128]{1,0:T(8,128)(2,1)S(1)}, u32[]{:S(2)}, u32[]{:S(2)}) collective-permute-start(bf16[128,128]{1,0:T(8,128)(2,1)S(1)} %get-tuple-element.63.refs_1_), channel_id=1, source_target_pairs={{0,4},{1,5},{2,6},{3,7},{4,0},{5,1},{6,2},{7,3},{8,12},{9,13},{10,... | collective-permute-start | bytes 98312 | tf_op jit(solution)/shard_map/ppermute | solution.py:17
  31.8 1.5 %collective-permute-done.14.refs_2_ = bf16[128,128]{1,0:T(8,128)(2,1)S(1)} collective-permute-done((bf16[128,128]{1,0:T(8,128)(2,1)S(1)}, bf16[128,128]{1,0:T(8,128)(2,1)S(1)}, u32[]{:S(2)}, u32[]{:S(2)}) %collective-permute-start.14) | collective-permute-done | bytes 32800 | tf_op jit(solution)/shard_map/ppermute | solution.py:17
  33.3 0.7 %collective-permute-done.15.refs_3_ = bf16[128,128]{1,0:T(8,128)(2,1)S(1)} collective-permute-done((bf16[128,128]{1,0:T(8,128)(2,1)S(1)}, bf16[128,128]{1,0:T(8,128)(2,1)S(1)}, u32[]{:S(2)}, u32[]{:S(2)}) %collective-permute-start.15) | collective-permute-done | bytes 32800 | tf_op jit(solution)/shard_map/ppermute | solution.py:17
  34.1 0.4 shard_map.89
  34.5 0.3 shard_map.90
  34.9 0.6 %collective-permute-start.17 = (f32[256,128]{1,0:T(8,128)S(1)}, f32[256,128]{1,0:T(8,128)S(1)}, u32[]{:S(2)}, u32[]{:S(2)}) collective-permute-start(f32[256,128]{1,0:T(8,128)S(1)} %get-tuple-element.56), channel_id=1, source_target_pairs={{0,1},{1,0},{2,3},{3,2},{4,5},{5,4},{6,7},{7,6},{8,9},{9,8},{10,11... | collective-permute-start | bytes 393224 | tf_op jit(solution)/shard_map/ppermute | solution.py:17
  35.4 0.4 collective-permute-done.18
  35.9 1.6 %collective-permute-start.19 = (f16[256,128]{1,0:T(8,128)(2,1)S(1)}, f16[256,128]{1,0:T(8,128)(2,1)S(1)}, u32[]{:S(2)}, u32[]{:S(2)}) collective-permute-start(f16[256,128]{1,0:T(8,128)(2,1)S(1)} %multiply_convert_fusion), channel_id=1, source_target_pairs={{0,2},{1,3},{2,0},{3,1},{4,6},{5,7},{6,4},{7,5},{8,10},{9,11},{10,... | collective-permute-start | bytes 196616 | tf_op jit(solution)/shard_map/ppermute | solution.py:17
  37.5 0.9 %shard_map.91 = (f32[256,128]{1,0:T(8,128)S(1)}, f32[128,128]{1,0:T(8,128)}) custom-call(f32[256,128]{1,0:T(8,128)S(1)} %get-tuple-element.55.keep, f32[256,128]{1,0:T(8,128)S(1)} %collective-permute-done.17.got, f32[1,256,256]{2,1,0:T(8,128)S(1)} %copy-done.1, f32[256,128]{1,0:T(8,128)S(1)} %copy-done.4, f32[128,128]{1,0:T(8,128)S(1)} %get-tuple-element.64.residual), custom_call_target="tpu_custom_call" | custom-call | bytes 917504 | tf_op jit(solution)/shard_map/pallas_call | solution.py:57
  38.3 1.9 %collective-permute-done.19 = f16[256,128]{1,0:T(8,128)(2,1)S(1)} collective-permute-done((f16[256,128]{1,0:T(8,128)(2,1)S(1)}, f16[256,128]{1,0:T(8,128)(2,1)S(1)}, u32[]{:S(2)}, u32[]{:S(2)}) %collective-permute-start.19) | collective-permute-done | bytes 65568 | tf_op jit(solution)/shard_map/ppermute | solution.py:17
  40.2 1.1 %shard_map.92 = (f32[256,128]{1,0:T(8,128)}, f32[256,128]{1,0:T(8,128)}) custom-call(f32[256,128]{1,0:T(8,128)S(1)} %convert_multiply_fusion.arrived, f32[1,256,256]{2,1,0:T(8,128)S(1)} %copy-done.1, f32[256,128]{1,0:T(8,128)S(1)} %get-tuple-element.60.begun, f32[256,128]{1,0:T(8,128)S(1)} %copy-done.2), custom_call_target="tpu_custom_call" | custom-call | bytes 917504 | tf_op jit(solution)/shard_map/pallas_call | solution.py:57
  (35 shorter events, 0.7 us)
Async XLA Ops:
  0.6 7.2 %copy-start.3 = (bf16[128,512]{1,0:T(8,128)(2,1)S(1)}, bf16[128,512]{1,0:T(8,128)(2,1)}, u32[]{:S(2)}) copy-start(bf16[128,512]{1,0:T(8,128)(2,1)} %features.1) | copy-start | bytes 393220
  0.6 11.5 %copy-start = (bf16[256,512]{1,0:T(8,128)(2,1)S(1)}, bf16[256,512]{1,0:T(8,128)(2,1)}, u32[]{:S(2)}) copy-start(bf16[256,512]{1,0:T(8,128)(2,1)} %centres.1) | copy-start | bytes 786436
  0.7 8.8 %copy-start.2 = (f32[256,128]{1,0:T(8,128)S(1)}, f32[256,128]{1,0:T(8,128)}, u32[]{:S(2)}) copy-start(f32[256,128]{1,0:T(8,128)} %coefficients.3) | copy-start | bytes 393220
  0.7 10.7 %collective-permute-start.1 = (bf16[128,512]{1,0:T(8,128)(2,1)}, bf16[128,512]{1,0:T(8,128)(2,1)S(1)}, u32[]{:S(2)}, u32[]{:S(2)}) collective-permute-start(bf16[128,512]{1,0:T(8,128)(2,1)} %features.1), channel_id=1, source_target_pairs={{0,8},{1,9},{2,10},{3,11},{4,12},{5,13},{6,14},{7,15},{8,0},{9,1},... | collective-permute-start | bytes 393224 | tf_op jit(solution)/shard_map/ppermute | solution.py:17
  5.8 6.5 %collective-permute-start.5 = (bf16[128,512]{1,0:T(8,128)(2,1)S(1)}, bf16[128,512]{1,0:T(8,128)(2,1)S(1)}, u32[]{:S(2)}, u32[]{:S(2)}) collective-permute-start(bf16[128,512]{1,0:T(8,128)(2,1)S(1)} %get-tuple-element.66), channel_id=1, source_target_pairs={{0,2},{1,3},{2,0},{3,1},{4,6},{5,7},{6,4},{7,5},{8,10},{9,11},{10,... | collective-permute-start | bytes 393224 | tf_op jit(solution)/shard_map/ppermute | solution.py:17
  7.3 7.7 %collective-permute-start.6 = (bf16[128,512]{1,0:T(8,128)(2,1)S(1)}, bf16[128,512]{1,0:T(8,128)(2,1)S(1)}, u32[]{:S(2)}, u32[]{:S(2)}) collective-permute-start(bf16[128,512]{1,0:T(8,128)(2,1)S(1)} %get-tuple-element.65), channel_id=1, source_target_pairs={{0,2},{1,3},{2,0},{3,1},{4,6},{5,7},{6,4},{7,5},{8,10},{9,11},{10,... | collective-permute-start | bytes 393224 | tf_op jit(solution)/shard_map/ppermute | solution.py:17
  7.8 7.1 %collective-permute-start = (bf16[128,512]{1,0:T(8,128)(2,1)S(1)}, bf16[128,512]{1,0:T(8,128)(2,1)S(1)}, u32[]{:S(2)}, u32[]{:S(2)}) collective-permute-start(bf16[128,512]{1,0:T(8,128)(2,1)S(1)} %copy-done.3), channel_id=1, source_target_pairs={{0,4},{1,5},{2,6},{3,7},{4,0},{5,1},{6,2},{7,3},{8,12},{9,13},{10,... | collective-permute-start | bytes 393224 | tf_op jit(solution)/shard_map/ppermute | solution.py:17
  9.4 7.0 %collective-permute-start.9 = (f32[256,128]{1,0:T(8,128)S(1)}, f32[256,128]{1,0:T(8,128)S(1)}, u32[]{:S(2)}, u32[]{:S(2)}) collective-permute-start(f32[256,128]{1,0:T(8,128)S(1)} %copy-done.2), channel_id=1, source_target_pairs={{0,2},{1,3},{2,0},{3,1},{4,6},{5,7},{6,4},{7,5},{8,10},{9,11},{10,... | collective-permute-start | bytes 393224 | tf_op jit(solution)/shard_map/ppermute | solution.py:17
  11.4 5.3 %collective-permute-start.2 = (bf16[128,512]{1,0:T(8,128)(2,1)S(1)}, bf16[128,512]{1,0:T(8,128)(2,1)S(1)}, u32[]{:S(2)}, u32[]{:S(2)}) collective-permute-start(bf16[128,512]{1,0:T(8,128)(2,1)S(1)} %collective-permute-done.1.refs_2_), channel_id=1, source_target_pairs={{0,4},{1,5},{2,6},{3,7},{4,0},{5,1},{6,2},{7,3},{8,12},{9,13},{10,... | collective-permute-start | bytes 393224 | tf_op jit(solution)/shard_map/ppermute | solution.py:17
  12.2 5.2 %collective-permute-start.3 = (bf16[256,512]{1,0:T(8,128)(2,1)S(1)}, bf16[256,512]{1,0:T(8,128)(2,1)S(1)}, u32[]{:S(2)}, u32[]{:S(2)}) collective-permute-start(bf16[256,512]{1,0:T(8,128)(2,1)S(1)} %copy-done), channel_id=1, source_target_pairs={{0,1},{1,0},{2,3},{3,2},{4,5},{5,4},{6,7},{7,6},{8,9},{9,8},{10,11... | collective-permute-start | bytes 786440 | tf_op jit(solution)/shard_map/ppermute | solution.py:17
  15.0 2.5 %collective-permute-start.4 = (f32[256,128]{1,0:T(8,128)S(1)}, f32[256,128]{1,0:T(8,128)S(1)}, u32[]{:S(2)}, u32[]{:S(2)}) collective-permute-start(f32[256,128]{1,0:T(8,128)S(1)} %copy-done.2), channel_id=1, source_target_pairs={{0,1},{1,0},{2,3},{3,2},{4,5},{5,4},{6,7},{7,6},{8,9},{9,8},{10,11... | collective-permute-start | bytes 393224 | tf_op jit(solution)/shard_map/ppermute | solution.py:17
  15.0 3.0 %collective-permute-start.7 = (bf16[128,512]{1,0:T(8,128)(2,1)S(1)}, bf16[128,512]{1,0:T(8,128)(2,1)S(1)}, u32[]{:S(2)}, u32[]{:S(2)}) collective-permute-start(bf16[128,512]{1,0:T(8,128)(2,1)S(1)} %collective-permute-done.5.refs_4_), channel_id=1, source_target_pairs={{0,1},{1,0},{2,3},{3,2},{4,5},{5,4},{6,7},{7,6},{8,9},{9,8},{10,11... | collective-permute-start | bytes 393224 | tf_op jit(solution)/shard_map/ppermute | solution.py:17
  16.4 1.6 %collective-permute-start.8 = (bf16[128,512]{1,0:T(8,128)(2,1)S(1)}, bf16[128,512]{1,0:T(8,128)(2,1)S(1)}, u32[]{:S(2)}, u32[]{:S(2)}) collective-permute-start(bf16[128,512]{1,0:T(8,128)(2,1)S(1)} %collective-permute-done.6.refs_5_), channel_id=1, source_target_pairs={{0,1},{1,0},{2,3},{3,2},{4,5},{5,4},{6,7},{7,6},{8,9},{9,8},{10,11... | collective-permute-start | bytes 393224 | tf_op jit(solution)/shard_map/ppermute | solution.py:17
  16.7 1.3 %collective-permute-start.10 = (f32[256,128]{1,0:T(8,128)S(1)}, f32[256,128]{1,0:T(8,128)S(1)}, u32[]{:S(2)}, u32[]{:S(2)}) collective-permute-start(f32[256,128]{1,0:T(8,128)S(1)} %collective-permute-done.9.refs_8_), channel_id=1, source_target_pairs={{0,1},{1,0},{2,3},{3,2},{4,5},{5,4},{6,7},{7,6},{8,9},{9,8},{10,11... | collective-permute-start | bytes 393224 | tf_op jit(solution)/shard_map/ppermute | solution.py:17
  18.8 5.8 %collective-permute-start.13 = (f16[128,128]{1,0:T(8,128)(2,1)S(1)}, f16[128,128]{1,0:T(8,128)(2,1)S(1)}, u32[]{:S(2)}, u32[]{:S(2)}) collective-permute-start(f16[128,128]{1,0:T(8,128)(2,1)S(1)} %multiply_convert_fusion.1), channel_id=1, source_target_pairs={{0,12},{1,13},{2,14},{3,15},{4,8},{5,9},{6,10},{7,11},{8,4},{9,5},... | collective-permute-start | bytes 98312 | tf_op jit(solution)/shard_map/ppermute | solution.py:17
  22.5 4.9 %collective-permute-start.12 = (f16[128,128]{1,0:T(8,128)(2,1)S(1)}, f16[128,128]{1,0:T(8,128)(2,1)S(1)}, u32[]{:S(2)}, u32[]{:S(2)}) collective-permute-start(f16[128,128]{1,0:T(8,128)(2,1)S(1)} %multiply_convert_fusion.2), channel_id=1, source_target_pairs={{0,8},{1,9},{2,10},{3,11},{4,12},{5,13},{6,14},{7,15},{8,0},{9,1},... | collective-permute-start | bytes 98312 | tf_op jit(solution)/shard_map/ppermute | solution.py:17
  22.5 4.8 %copy-start.5 = (bf16[128,128]{1,0:T(8,128)(2,1)S(1)}, bf16[128,128]{1,0:T(8,128)(2,1)}, u32[]{:S(2)}) copy-start(bf16[128,128]{1,0:T(8,128)(2,1)} %param.8) | copy-start | bytes 98308
  22.6 4.8 %collective-permute-start.11 = (f16[128,128]{1,0:T(8,128)(2,1)S(1)}, f16[128,128]{1,0:T(8,128)(2,1)S(1)}, u32[]{:S(2)}, u32[]{:S(2)}) collective-permute-start(f16[128,128]{1,0:T(8,128)(2,1)S(1)} %multiply_convert_fusion.3), channel_id=1, source_target_pairs={{0,4},{1,5},{2,6},{3,7},{4,0},{5,1},{6,2},{7,3},{8,12},{9,13},{10,... | collective-permute-start | bytes 98312 | tf_op jit(solution)/shard_map/ppermute | solution.py:17
  27.4 5.9 %collective-permute-start.14 = (bf16[128,128]{1,0:T(8,128)(2,1)S(1)}, bf16[128,128]{1,0:T(8,128)(2,1)S(1)}, u32[]{:S(2)}, u32[]{:S(2)}) collective-permute-start(bf16[128,128]{1,0:T(8,128)(2,1)S(1)} %get-tuple-element.63.refs_1_), channel_id=1, source_target_pairs={{0,12},{1,13},{2,14},{3,15},{4,8},{5,9},{6,10},{7,11},{8,4},{9,5},... | collective-permute-start | bytes 98312 | tf_op jit(solution)/shard_map/ppermute | solution.py:17
  29.1 4.9 %collective-permute-start.15 = (bf16[128,128]{1,0:T(8,128)(2,1)S(1)}, bf16[128,128]{1,0:T(8,128)(2,1)S(1)}, u32[]{:S(2)}, u32[]{:S(2)}) collective-permute-start(bf16[128,128]{1,0:T(8,128)(2,1)S(1)} %get-tuple-element.63.refs_1_), channel_id=1, source_target_pairs={{0,8},{1,9},{2,10},{3,11},{4,12},{5,13},{6,14},{7,15},{8,0},{9,1},... | collective-permute-start | bytes 98312 | tf_op jit(solution)/shard_map/ppermute | solution.py:17
  29.6 4.4 %collective-permute-start.16 = (bf16[128,128]{1,0:T(8,128)(2,1)S(1)}, bf16[128,128]{1,0:T(8,128)(2,1)S(1)}, u32[]{:S(2)}, u32[]{:S(2)}) collective-permute-start(bf16[128,128]{1,0:T(8,128)(2,1)S(1)} %get-tuple-element.63.refs_1_), channel_id=1, source_target_pairs={{0,4},{1,5},{2,6},{3,7},{4,0},{5,1},{6,2},{7,3},{8,12},{9,13},{10,... | collective-permute-start | bytes 98312 | tf_op jit(solution)/shard_map/ppermute | solution.py:17
  34.4 1.4 %collective-permute-start.18 = (f32[256,128]{1,0:T(8,128)S(1)}, f32[256,128]{1,0:T(8,128)S(1)}, u32[]{:S(2)}, u32[]{:S(2)}) collective-permute-start(f32[256,128]{1,0:T(8,128)S(1)} %get-tuple-element.59), channel_id=1, source_target_pairs={{0,1},{1,0},{2,3},{3,2},{4,5},{5,4},{6,7},{7,6},{8,9},{9,8},{10,11... | collective-permute-start | bytes 393224 | tf_op jit(solution)/shard_map/ppermute | solution.py:17
  34.5 3.0 %copy-start.4 = (f32[256,128]{1,0:T(8,128)S(1)}, f32[256,128]{1,0:T(8,128)}, u32[]{:S(2)}) copy-start(f32[256,128]{1,0:T(8,128)} %momentum.1) | copy-start | bytes 393220
  34.9 2.6 %copy-start.1 = (f32[1,256,256]{2,1,0:T(8,128)S(1)}, f32[1,256,256]{2,1,0:T(8,128)}, u32[]{:S(2)}) copy-start(f32[1,256,256]{2,1,0:T(8,128)} %inverse.3) | copy-start | bytes 786436
  34.9 2.6 %collective-permute-start.17 = (f32[256,128]{1,0:T(8,128)S(1)}, f32[256,128]{1,0:T(8,128)S(1)}, u32[]{:S(2)}, u32[]{:S(2)}) collective-permute-start(f32[256,128]{1,0:T(8,128)S(1)} %get-tuple-element.56), channel_id=1, source_target_pairs={{0,1},{1,0},{2,3},{3,2},{4,5},{5,4},{6,7},{7,6},{8,9},{9,8},{10,11... | collective-permute-start | bytes 393224 | tf_op jit(solution)/shard_map/ppermute | solution.py:17
  35.9 4.3 %collective-permute-start.19 = (f16[256,128]{1,0:T(8,128)(2,1)S(1)}, f16[256,128]{1,0:T(8,128)(2,1)S(1)}, u32[]{:S(2)}, u32[]{:S(2)}) collective-permute-start(f16[256,128]{1,0:T(8,128)(2,1)S(1)} %multiply_convert_fusion), channel_id=1, source_target_pairs={{0,2},{1,3},{2,0},{3,1},{4,6},{5,7},{6,4},{7,5},{8,10},{9,11},{10,... | collective-permute-start | bytes 196616 | tf_op jit(solution)/shard_map/ppermute | solution.py:17

commit v9 on v7

--- a/solution.py
+++ b/solution.py
@@ -236,7 +236,7 @@
     scale = 2.0 ** math.floor(math.log2(65504 / bound))
     kind, factor = (jnp.float16, scale) if scale >= 2.0**-10 else (F32, 1.0)
     far_keep, far_give, joined = gradients(far_kernels, far_layout, residuals, count)
-    arrived = send((factor * (far_keep + send(far_give, core))).astype(kind), far).astype(F32) / factor
+    arrived = send((factor * (far_keep + send((factor * far_give).astype(kind), core).astype(F32) / factor)).astype(kind), far).astype(F32) / factor
     keep, give = gradients(near_kernels, near_layout, [joined], count)
     parts = [keep, send(give, core), arrived]
     out = jax.ShapeDtypeStruct(momentum.shape, F32)

time: 41.5 us -> 41.4 us (level)
  no operation moved by 1% of the time
where the time goes in v9:
time: 41.4 us; the launch traced here: 41.3 us
  starting transfers between devices  21.6 us (52%)
  waiting for transfers between devices  14.1 us (34%)
  Pallas kernels  3.63 us (9%)
  local copies, waits for them, and re-layouts  1.01 us (2%)
  between operations  0.85 us (2%)
    ppermute x20, starting transfers between devices, swap(): return lax.ppermute(x, 'wide', [(i, i ^ mask) for i in range(size)])  21.6 us
    ppermute x20, waiting for transfers between devices, swap(): return lax.ppermute(x, 'wide', [(i, i ^ mask) for i in range(size)])  14.1 us
    pallas_call x7, Pallas kernels, whole_call(): pl.pallas_call(body, out_shape=outs, in_specs=[pl.BlockSpec(memory_space=...  3.63 us
    split x1, local copies, waits for them, and re-layouts, shards(): far_parts = [send(part, far) for part in jnp.split(centres, 2)]  0.98 us
  transfers between devices with their start and end apart: 20, of which 11 were waited for; matrix products, arithmetic and copies ran while one was open for 2% of the time, Pallas kernels for 4%

profile of v9, /device:TPU:0, one launch (start us, length us, event | category | flops | bytes accessed | tf_op | source)
XLA Modules:
  0.0 41.3 jit_solution(8594212821327657943)
XLA Ops:
  0.7 4.1 %collective-permute-start.1 = (bf16[128,512]{1,0:T(8,128)(2,1)}, bf16[128,512]{1,0:T(8,128)(2,1)S(1)}, u32[]{:S(2)}, u32[]{:S(2)}) collective-permute-start(bf16[128,512]{1,0:T(8,128)(2,1)} %features.1), channel_id=1, source_target_pairs={{0,8},{1,9},{2,10},{3,11},{4,12},{5,13},{6,14},{7,15},{8,0},{9,1},... | collective-permute-start | bytes 393224 | tf_op jit(solution)/shard_map/ppermute | solution.py:17
  4.8 1.0 %fusion.1 = (bf16[128,512]{1,0:T(8,128)(2,1)S(1)}, bf16[128,512]{1,0:T(8,128)(2,1)S(1)}) fusion(bf16[256,512]{1,0:T(8,128)(2,1)} %centres.1), kind=kLoop, calls=%fused_computation.8 | loop fusion | bytes 524288 | tf_op jit(solution)/shard_map/split | solution.py:209
  5.8 1.6 %collective-permute-start.5 = (bf16[128,512]{1,0:T(8,128)(2,1)S(1)}, bf16[128,512]{1,0:T(8,128)(2,1)S(1)}, u32[]{:S(2)}, u32[]{:S(2)}) collective-permute-start(bf16[128,512]{1,0:T(8,128)(2,1)S(1)} %get-tuple-element.64), channel_id=1, source_target_pairs={{0,2},{1,3},{2,0},{3,1},{4,6},{5,7},{6,4},{7,5},{8,10},{9,11},{10,... | collective-permute-start | bytes 393224 | tf_op jit(solution)/shard_map/ppermute | solution.py:17
  7.3 0.5 %collective-permute-start.6 = (bf16[128,512]{1,0:T(8,128)(2,1)S(1)}, bf16[128,512]{1,0:T(8,128)(2,1)S(1)}, u32[]{:S(2)}, u32[]{:S(2)}) collective-permute-start(bf16[128,512]{1,0:T(8,128)(2,1)S(1)} %get-tuple-element.63), channel_id=1, source_target_pairs={{0,2},{1,3},{2,0},{3,1},{4,6},{5,7},{6,4},{7,5},{8,10},{9,11},{10,... | collective-permute-start | bytes 393224 | tf_op jit(solution)/shard_map/ppermute | solution.py:17
  7.8 1.6 %collective-permute-start = (bf16[128,512]{1,0:T(8,128)(2,1)S(1)}, bf16[128,512]{1,0:T(8,128)(2,1)S(1)}, u32[]{:S(2)}, u32[]{:S(2)}) collective-permute-start(bf16[128,512]{1,0:T(8,128)(2,1)S(1)} %copy-done.4), channel_id=1, source_target_pairs={{0,4},{1,5},{2,6},{3,7},{4,0},{5,1},{6,2},{7,3},{8,12},{9,13},{10,... | collective-permute-start | bytes 393224 | tf_op jit(solution)/shard_map/ppermute | solution.py:17
  9.4 1.5 %collective-permute-start.9 = (f32[256,128]{1,0:T(8,128)S(1)}, f32[256,128]{1,0:T(8,128)S(1)}, u32[]{:S(2)}, u32[]{:S(2)}) collective-permute-start(f32[256,128]{1,0:T(8,128)S(1)} %copy-done.1), channel_id=1, source_target_pairs={{0,2},{1,3},{2,0},{3,1},{4,6},{5,7},{6,4},{7,5},{8,10},{9,11},{10,... | collective-permute-start | bytes 393224 | tf_op jit(solution)/shard_map/ppermute | solution.py:17
  10.9 0.4 %collective-permute-done.1.refs_2_ = bf16[128,512]{1,0:T(8,128)(2,1)S(1)} collective-permute-done((bf16[128,512]{1,0:T(8,128)(2,1)}, bf16[128,512]{1,0:T(8,128)(2,1)S(1)}, u32[]{:S(2)}, u32[]{:S(2)}) %collective-permute-start.1) | collective-permute-done | bytes 131104 | tf_op jit(solution)/shard_map/ppermute | solution.py:17
  11.4 0.8 %collective-permute-start.2 = (bf16[128,512]{1,0:T(8,128)(2,1)S(1)}, bf16[128,512]{1,0:T(8,128)(2,1)S(1)}, u32[]{:S(2)}, u32[]{:S(2)}) collective-permute-start(bf16[128,512]{1,0:T(8,128)(2,1)S(1)} %collective-permute-done.1.refs_2_), channel_id=1, source_target_pairs={{0,4},{1,5},{2,6},{3,7},{4,0},{5,1},{6,2},{7,3},{8,12},{9,13},{10,... | collective-permute-start | bytes 393224 | tf_op jit(solution)/shard_map/ppermute | solution.py:17
  12.3 2.7 %collective-permute-done.6.refs_5_ = bf16[128,512]{1,0:T(8,128)(2,1)S(1)} collective-permute-done((bf16[128,512]{1,0:T(8,128)(2,1)S(1)}, bf16[128,512]{1,0:T(8,128)(2,1)S(1)}, u32[]{:S(2)}, u32[]{:S(2)}) %collective-permute-start.6) | collective-permute-done | bytes 131104 | tf_op jit(solution)/shard_map/ppermute | solution.py:17
  15.0 0.5 %collective-permute-start.7 = (bf16[128,512]{1,0:T(8,128)(2,1)S(1)}, bf16[128,512]{1,0:T(8,128)(2,1)S(1)}, u32[]{:S(2)}, u32[]{:S(2)}) collective-permute-start(bf16[128,512]{1,0:T(8,128)(2,1)S(1)} %collective-permute-done.5.refs_4_), channel_id=1, source_target_pairs={{0,1},{1,0},{2,3},{3,2},{4,5},{5,4},{6,7},{7,6},{8,9},{9,8},{10,11... | collective-permute-start | bytes 393224 | tf_op jit(solution)/shard_map/ppermute | solution.py:17
  15.5 0.9 %collective-permute-done.9.refs_8_ = f32[256,128]{1,0:T(8,128)S(1)} collective-permute-done((f32[256,128]{1,0:T(8,128)S(1)}, f32[256,128]{1,0:T(8,128)S(1)}, u32[]{:S(2)}, u32[]{:S(2)}) %collective-permute-start.9) | collective-permute-done | bytes 131104 | tf_op jit(solution)/shard_map/ppermute | solution.py:17
  16.4 0.3 collective-permute-done.2.refs_3_
  16.7 0.2 collective-permute-start.10
  16.9 0.5 %shard_map.86 = (bf16[512,256]{1,0:T(8,128)(2,1)S(1)}, f32[128,128]{1,0:T(8,128)S(1)}, f32[128,128]{1,0:T(8,128)S(1)}, f32[128,128]{1,0:T(8,128)S(1)}, f32[128,128]{1,0:T(8,128)S(1)}) custom-call(bf16[128,512]{1,0:T(8,128)(2,1)S(1)} %get-tuple-element.32.refs_0_, bf16[128,512]{1,0:T(8,128)(2,1)S(1)} %collective-permute-done.refs_1_, ...), custom_call_target="tpu_custom_call" | custom-call | flops 8000000000 | bytes 1376256 | tf_op jit(solution)/shard_map/pallas_call | solution.py:57
  17.5 0.5 %shard_map.87 = (bf16[512,256]{1,0:T(8,128)(2,1)S(1)}, f32[128,128]{1,0:T(8,128)S(1)}, f32[128,128]{1,0:T(8,128)S(1)}, f32[128,128]{1,0:T(8,128)S(1)}, f32[128,128]{1,0:T(8,128)S(1)}) custom-call(bf16[128,512]{1,0:T(8,128)(2,1)S(1)} %get-tuple-element.32.refs_0_, bf16[128,512]{1,0:T(8,128)(2,1)S(1)} %collective-permute-done.refs_1_, ...), custom_call_target="tpu_custom_call" | custom-call | flops 167772160 | bytes 1703936 | tf_op jit(solution)/shard_map/pallas_call | solution.py:57
  18.0 0.7 %shard_map.88 = (bf16[512,512]{1,0:T(8,128)(2,1)S(1)}, f32[128,128]{1,0:T(8,128)S(1)}, f32[128,128]{1,0:T(8,128)S(1)}, f32[128,128]{1,0:T(8,128)S(1)}, f32[128,128]{1,0:T(8,128)S(1)}) custom-call(bf16[128,512]{1,0:T(8,128)(2,1)S(1)} %get-tuple-element.32.refs_0_, bf16[128,512]{1,0:T(8,128)(2,1)S(1)} %collective-permute-done.refs_1_, ...), custom_call_target="tpu_custom_call" | custom-call | flops 335544320 | bytes 2359296 | tf_op jit(solution)/shard_map/pallas_call | solution.py:57
  18.8 3.7 %collective-permute-start.13 = (f16[128,128]{1,0:T(8,128)(2,1)S(1)}, f16[128,128]{1,0:T(8,128)(2,1)S(1)}, u32[]{:S(2)}, u32[]{:S(2)}) collective-permute-start(f16[128,128]{1,0:T(8,128)(2,1)S(1)} %multiply_convert_fusion.2), channel_id=1, source_target_pairs={{0,12},{1,13},{2,14},{3,15},{4,8},{5,9},{6,10},{7,11},{8,4},{9,5},... | collective-permute-start | bytes 98312 | tf_op jit(solution)/shard_map/ppermute | solution.py:17
  22.6 0.8 %collective-permute-start.11 = (f16[128,128]{1,0:T(8,128)(2,1)S(1)}, f16[128,128]{1,0:T(8,128)(2,1)S(1)}, u32[]{:S(2)}, u32[]{:S(2)}) collective-permute-start(f16[128,128]{1,0:T(8,128)(2,1)S(1)} %multiply_convert_fusion.4), channel_id=1, source_target_pairs={{0,4},{1,5},{2,6},{3,7},{4,0},{5,1},{6,2},{7,3},{8,12},{9,13},{10,... | collective-permute-start | bytes 98312 | tf_op jit(solution)/shard_map/ppermute | solution.py:17
  23.4 1.2 %collective-permute-done.13 = f16[128,128]{1,0:T(8,128)(2,1)S(1)} collective-permute-done((f16[128,128]{1,0:T(8,128)(2,1)S(1)}, f16[128,128]{1,0:T(8,128)(2,1)S(1)}, u32[]{:S(2)}, u32[]{:S(2)}) %collective-permute-start.13) | collective-permute-done | bytes 32800 | tf_op jit(solution)/shard_map/ppermute | solution.py:17
  24.6 2.8 %collective-permute-done.12 = f16[128,128]{1,0:T(8,128)(2,1)S(1)} collective-permute-done((f16[128,128]{1,0:T(8,128)(2,1)S(1)}, f16[128,128]{1,0:T(8,128)(2,1)S(1)}, u32[]{:S(2)}, u32[]{:S(2)}) %collective-permute-start.12) | collective-permute-done | bytes 32800 | tf_op jit(solution)/shard_map/ppermute | solution.py:17
  27.4 1.7 %collective-permute-start.14 = (bf16[128,128]{1,0:T(8,128)(2,1)S(1)}, bf16[128,128]{1,0:T(8,128)(2,1)S(1)}, u32[]{:S(2)}, u32[]{:S(2)}) collective-permute-start(bf16[128,128]{1,0:T(8,128)(2,1)S(1)} %get-tuple-element.61.refs_1_), channel_id=1, source_target_pairs={{0,12},{1,13},{2,14},{3,15},{4,8},{5,9},{6,10},{7,11},{8,4},{9,5},... | collective-permute-start | bytes 98312 | tf_op jit(solution)/shard_map/ppermute | solution.py:17
  29.1 0.6 %collective-permute-start.15 = (bf16[128,128]{1,0:T(8,128)(2,1)S(1)}, bf16[128,128]{1,0:T(8,128)(2,1)S(1)}, u32[]{:S(2)}, u32[]{:S(2)}) collective-permute-start(bf16[128,128]{1,0:T(8,128)(2,1)S(1)} %get-tuple-element.61.refs_1_), channel_id=1, source_target_pairs={{0,8},{1,9},{2,10},{3,11},{4,12},{5,13},{6,14},{7,15},{8,0},{9,1},... | collective-permute-start | bytes 98312 | tf_op jit(solution)/shard_map/ppermute | solution.py:17
  29.6 2.2 %collective-permute-start.16 = (bf16[128,128]{1,0:T(8,128)(2,1)S(1)}, bf16[128,128]{1,0:T(8,128)(2,1)S(1)}, u32[]{:S(2)}, u32[]{:S(2)}) collective-permute-start(bf16[128,128]{1,0:T(8,128)(2,1)S(1)} %get-tuple-element.61.refs_1_), channel_id=1, source_target_pairs={{0,4},{1,5},{2,6},{3,7},{4,0},{5,1},{6,2},{7,3},{8,12},{9,13},{10,... | collective-permute-start | bytes 98312 | tf_op jit(solution)/shard_map/ppermute | solution.py:17
  31.8 1.5 %collective-permute-done.14.refs_2_ = bf16[128,128]{1,0:T(8,128)(2,1)S(1)} collective-permute-done((bf16[128,128]{1,0:T(8,128)(2,1)S(1)}, bf16[128,128]{1,0:T(8,128)(2,1)S(1)}, u32[]{:S(2)}, u32[]{:S(2)}) %collective-permute-start.14) | collective-permute-done | bytes 32800 | tf_op jit(solution)/shard_map/ppermute | solution.py:17
  33.3 0.7 %collective-permute-done.15.refs_3_ = bf16[128,128]{1,0:T(8,128)(2,1)S(1)} collective-permute-done((bf16[128,128]{1,0:T(8,128)(2,1)S(1)}, bf16[128,128]{1,0:T(8,128)(2,1)S(1)}, u32[]{:S(2)}, u32[]{:S(2)}) %collective-permute-start.15) | collective-permute-done | bytes 32800 | tf_op jit(solution)/shard_map/ppermute | solution.py:17
  34.0 0.1 collective-permute-done.16.refs_4_
  34.1 0.4 shard_map.89
  34.5 1.2 %collective-permute-done.18 = f16[256,128]{1,0:T(8,128)(2,1)S(1)} collective-permute-done((f16[256,128]{1,0:T(8,128)(2,1)S(1)}, f16[256,128]{1,0:T(8,128)(2,1)S(1)}, u32[]{:S(2)}, u32[]{:S(2)}) %collective-permute-start.18) | collective-permute-done | bytes 65568 | tf_op jit(solution)/shard_map/ppermute | solution.py:17
  35.8 1.6 %collective-permute-start.19 = (f16[256,128]{1,0:T(8,128)(2,1)S(1)}, f16[256,128]{1,0:T(8,128)(2,1)S(1)}, u32[]{:S(2)}, u32[]{:S(2)}) collective-permute-start(f16[256,128]{1,0:T(8,128)(2,1)S(1)} %multiply_convert_fusion), channel_id=1, source_target_pairs={{0,2},{1,3},{2,0},{3,1},{4,6},{5,7},{6,4},{7,5},{8,10},{9,11},{10,... | collective-permute-start | bytes 196616 | tf_op jit(solution)/shard_map/ppermute | solution.py:17
  37.4 0.3 shard_map.90
  37.8 2.3 %collective-permute-done.19 = f16[256,128]{1,0:T(8,128)(2,1)S(1)} collective-permute-done((f16[256,128]{1,0:T(8,128)(2,1)S(1)}, f16[256,128]{1,0:T(8,128)(2,1)S(1)}, u32[]{:S(2)}, u32[]{:S(2)}) %collective-permute-start.19) | collective-permute-done | bytes 65568 | tf_op jit(solution)/shard_map/ppermute | solution.py:17
  40.2 1.1 %shard_map.91 = (f32[256,128]{1,0:T(8,128)}, f32[256,128]{1,0:T(8,128)}, f32[128,128]{1,0:T(8,128)}) custom-call(f32[256,128]{1,0:T(8,128)S(1)} %get-tuple-element.54.refs_0_, f32[256,128]{1,0:T(8,128)S(1)} %collective-permute-done.17.refs_1_, f32[256,128]{1,0:T(8,128)S(1)} %convert_multiply_fusion.refs_2_, f32[1,256,256]{2,1,0:T(8,128)S(1)} %copy-done.2, ...), custom_call_target="tpu_custom_call" | custom-call | bytes 1310720 | tf_op jit(solution)/shard_map/pallas_call | solution.py:57
  (35 shorter events, 0.5 us)
Async XLA Ops:
  0.6 7.2 %copy-start.4 = (bf16[128,512]{1,0:T(8,128)(2,1)S(1)}, bf16[128,512]{1,0:T(8,128)(2,1)}, u32[]{:S(2)}) copy-start(bf16[128,512]{1,0:T(8,128)(2,1)} %features.1) | copy-start | bytes 393220
  0.6 11.5 %copy-start = (bf16[256,512]{1,0:T(8,128)(2,1)S(1)}, bf16[256,512]{1,0:T(8,128)(2,1)}, u32[]{:S(2)}) copy-start(bf16[256,512]{1,0:T(8,128)(2,1)} %centres.1) | copy-start | bytes 786436
  0.7 8.8 %copy-start.1 = (f32[256,128]{1,0:T(8,128)S(1)}, f32[256,128]{1,0:T(8,128)}, u32[]{:S(2)}) copy-start(f32[256,128]{1,0:T(8,128)} %refs_5_.1) | copy-start | bytes 393220
  0.7 10.7 %collective-permute-start.1 = (bf16[128,512]{1,0:T(8,128)(2,1)}, bf16[128,512]{1,0:T(8,128)(2,1)S(1)}, u32[]{:S(2)}, u32[]{:S(2)}) collective-permute-start(bf16[128,512]{1,0:T(8,128)(2,1)} %features.1), channel_id=1, source_target_pairs={{0,8},{1,9},{2,10},{3,11},{4,12},{5,13},{6,14},{7,15},{8,0},{9,1},... | collective-permute-start | bytes 393224 | tf_op jit(solution)/shard_map/ppermute | solution.py:17
  5.8 6.5 %collective-permute-start.5 = (bf16[128,512]{1,0:T(8,128)(2,1)S(1)}, bf16[128,512]{1,0:T(8,128)(2,1)S(1)}, u32[]{:S(2)}, u32[]{:S(2)}) collective-permute-start(bf16[128,512]{1,0:T(8,128)(2,1)S(1)} %get-tuple-element.64), channel_id=1, source_target_pairs={{0,2},{1,3},{2,0},{3,1},{4,6},{5,7},{6,4},{7,5},{8,10},{9,11},{10,... | collective-permute-start | bytes 393224 | tf_op jit(solution)/shard_map/ppermute | solution.py:17
  7.3 7.7 %collective-permute-start.6 = (bf16[128,512]{1,0:T(8,128)(2,1)S(1)}, bf16[128,512]{1,0:T(8,128)(2,1)S(1)}, u32[]{:S(2)}, u32[]{:S(2)}) collective-permute-start(bf16[128,512]{1,0:T(8,128)(2,1)S(1)} %get-tuple-element.63), channel_id=1, source_target_pairs={{0,2},{1,3},{2,0},{3,1},{4,6},{5,7},{6,4},{7,5},{8,10},{9,11},{10,... | collective-permute-start | bytes 393224 | tf_op jit(solution)/shard_map/ppermute | solution.py:17
  7.8 7.1 %collective-permute-start = (bf16[128,512]{1,0:T(8,128)(2,1)S(1)}, bf16[128,512]{1,0:T(8,128)(2,1)S(1)}, u32[]{:S(2)}, u32[]{:S(2)}) collective-permute-start(bf16[128,512]{1,0:T(8,128)(2,1)S(1)} %copy-done.4), channel_id=1, source_target_pairs={{0,4},{1,5},{2,6},{3,7},{4,0},{5,1},{6,2},{7,3},{8,12},{9,13},{10,... | collective-permute-start | bytes 393224 | tf_op jit(solution)/shard_map/ppermute | solution.py:17
  9.4 7.0 %collective-permute-start.9 = (f32[256,128]{1,0:T(8,128)S(1)}, f32[256,128]{1,0:T(8,128)S(1)}, u32[]{:S(2)}, u32[]{:S(2)}) collective-permute-start(f32[256,128]{1,0:T(8,128)S(1)} %copy-done.1), channel_id=1, source_target_pairs={{0,2},{1,3},{2,0},{3,1},{4,6},{5,7},{6,4},{7,5},{8,10},{9,11},{10,... | collective-permute-start | bytes 393224 | tf_op jit(solution)/shard_map/ppermute | solution.py:17
  11.4 5.3 %collective-permute-start.2 = (bf16[128,512]{1,0:T(8,128)(2,1)S(1)}, bf16[128,512]{1,0:T(8,128)(2,1)S(1)}, u32[]{:S(2)}, u32[]{:S(2)}) collective-permute-start(bf16[128,512]{1,0:T(8,128)(2,1)S(1)} %collective-permute-done.1.refs_2_), channel_id=1, source_target_pairs={{0,4},{1,5},{2,6},{3,7},{4,0},{5,1},{6,2},{7,3},{8,12},{9,13},{10,... | collective-permute-start | bytes 393224 | tf_op jit(solution)/shard_map/ppermute | solution.py:17
  12.2 5.2 %collective-permute-start.3 = (bf16[256,512]{1,0:T(8,128)(2,1)S(1)}, bf16[256,512]{1,0:T(8,128)(2,1)S(1)}, u32[]{:S(2)}, u32[]{:S(2)}) collective-permute-start(bf16[256,512]{1,0:T(8,128)(2,1)S(1)} %copy-done), channel_id=1, source_target_pairs={{0,1},{1,0},{2,3},{3,2},{4,5},{5,4},{6,7},{7,6},{8,9},{9,8},{10,11... | collective-permute-start | bytes 786440 | tf_op jit(solution)/shard_map/ppermute | solution.py:17
  15.0 2.5 %collective-permute-start.4 = (f32[256,128]{1,0:T(8,128)S(1)}, f32[256,128]{1,0:T(8,128)S(1)}, u32[]{:S(2)}, u32[]{:S(2)}) collective-permute-start(f32[256,128]{1,0:T(8,128)S(1)} %copy-done.1), channel_id=1, source_target_pairs={{0,1},{1,0},{2,3},{3,2},{4,5},{5,4},{6,7},{7,6},{8,9},{9,8},{10,11... | collective-permute-start | bytes 393224 | tf_op jit(solution)/shard_map/ppermute | solution.py:17
  15.0 3.0 %collective-permute-start.7 = (bf16[128,512]{1,0:T(8,128)(2,1)S(1)}, bf16[128,512]{1,0:T(8,128)(2,1)S(1)}, u32[]{:S(2)}, u32[]{:S(2)}) collective-permute-start(bf16[128,512]{1,0:T(8,128)(2,1)S(1)} %collective-permute-done.5.refs_4_), channel_id=1, source_target_pairs={{0,1},{1,0},{2,3},{3,2},{4,5},{5,4},{6,7},{7,6},{8,9},{9,8},{10,11... | collective-permute-start | bytes 393224 | tf_op jit(solution)/shard_map/ppermute | solution.py:17
  16.4 1.6 %collective-permute-start.8 = (bf16[128,512]{1,0:T(8,128)(2,1)S(1)}, bf16[128,512]{1,0:T(8,128)(2,1)S(1)}, u32[]{:S(2)}, u32[]{:S(2)}) collective-permute-start(bf16[128,512]{1,0:T(8,128)(2,1)S(1)} %collective-permute-done.6.refs_5_), channel_id=1, source_target_pairs={{0,1},{1,0},{2,3},{3,2},{4,5},{5,4},{6,7},{7,6},{8,9},{9,8},{10,11... | collective-permute-start | bytes 393224 | tf_op jit(solution)/shard_map/ppermute | solution.py:17
  16.7 1.3 %collective-permute-start.10 = (f32[256,128]{1,0:T(8,128)S(1)}, f32[256,128]{1,0:T(8,128)S(1)}, u32[]{:S(2)}, u32[]{:S(2)}) collective-permute-start(f32[256,128]{1,0:T(8,128)S(1)} %collective-permute-done.9.refs_8_), channel_id=1, source_target_pairs={{0,1},{1,0},{2,3},{3,2},{4,5},{5,4},{6,7},{7,6},{8,9},{9,8},{10,11... | collective-permute-start | bytes 393224 | tf_op jit(solution)/shard_map/ppermute | solution.py:17
  18.8 5.8 %collective-permute-start.13 = (f16[128,128]{1,0:T(8,128)(2,1)S(1)}, f16[128,128]{1,0:T(8,128)(2,1)S(1)}, u32[]{:S(2)}, u32[]{:S(2)}) collective-permute-start(f16[128,128]{1,0:T(8,128)(2,1)S(1)} %multiply_convert_fusion.2), channel_id=1, source_target_pairs={{0,12},{1,13},{2,14},{3,15},{4,8},{5,9},{6,10},{7,11},{8,4},{9,5},... | collective-permute-start | bytes 98312 | tf_op jit(solution)/shard_map/ppermute | solution.py:17
  22.5 4.9 %collective-permute-start.12 = (f16[128,128]{1,0:T(8,128)(2,1)S(1)}, f16[128,128]{1,0:T(8,128)(2,1)S(1)}, u32[]{:S(2)}, u32[]{:S(2)}) collective-permute-start(f16[128,128]{1,0:T(8,128)(2,1)S(1)} %multiply_convert_fusion.3), channel_id=1, source_target_pairs={{0,8},{1,9},{2,10},{3,11},{4,12},{5,13},{6,14},{7,15},{8,0},{9,1},... | collective-permute-start | bytes 98312 | tf_op jit(solution)/shard_map/ppermute | solution.py:17
  22.5 4.8 %copy-start.5 = (bf16[128,128]{1,0:T(8,128)(2,1)S(1)}, bf16[128,128]{1,0:T(8,128)(2,1)}, u32[]{:S(2)}) copy-start(bf16[128,128]{1,0:T(8,128)(2,1)} %param.8) | copy-start | bytes 98308
  22.6 4.8 %collective-permute-start.11 = (f16[128,128]{1,0:T(8,128)(2,1)S(1)}, f16[128,128]{1,0:T(8,128)(2,1)S(1)}, u32[]{:S(2)}, u32[]{:S(2)}) collective-permute-start(f16[128,128]{1,0:T(8,128)(2,1)S(1)} %multiply_convert_fusion.4), channel_id=1, source_target_pairs={{0,4},{1,5},{2,6},{3,7},{4,0},{5,1},{6,2},{7,3},{8,12},{9,13},{10,... | collective-permute-start | bytes 98312 | tf_op jit(solution)/shard_map/ppermute | solution.py:17
  27.4 5.9 %collective-permute-start.14 = (bf16[128,128]{1,0:T(8,128)(2,1)S(1)}, bf16[128,128]{1,0:T(8,128)(2,1)S(1)}, u32[]{:S(2)}, u32[]{:S(2)}) collective-permute-start(bf16[128,128]{1,0:T(8,128)(2,1)S(1)} %get-tuple-element.61.refs_1_), channel_id=1, source_target_pairs={{0,12},{1,13},{2,14},{3,15},{4,8},{5,9},{6,10},{7,11},{8,4},{9,5},... | collective-permute-start | bytes 98312 | tf_op jit(solution)/shard_map/ppermute | solution.py:17
  29.1 4.9 %collective-permute-start.15 = (bf16[128,128]{1,0:T(8,128)(2,1)S(1)}, bf16[128,128]{1,0:T(8,128)(2,1)S(1)}, u32[]{:S(2)}, u32[]{:S(2)}) collective-permute-start(bf16[128,128]{1,0:T(8,128)(2,1)S(1)} %get-tuple-element.61.refs_1_), channel_id=1, source_target_pairs={{0,8},{1,9},{2,10},{3,11},{4,12},{5,13},{6,14},{7,15},{8,0},{9,1},... | collective-permute-start | bytes 98312 | tf_op jit(solution)/shard_map/ppermute | solution.py:17
  29.6 4.4 %collective-permute-start.16 = (bf16[128,128]{1,0:T(8,128)(2,1)S(1)}, bf16[128,128]{1,0:T(8,128)(2,1)S(1)}, u32[]{:S(2)}, u32[]{:S(2)}) collective-permute-start(bf16[128,128]{1,0:T(8,128)(2,1)S(1)} %get-tuple-element.61.refs_1_), channel_id=1, source_target_pairs={{0,4},{1,5},{2,6},{3,7},{4,0},{5,1},{6,2},{7,3},{8,12},{9,13},{10,... | collective-permute-start | bytes 98312 | tf_op jit(solution)/shard_map/ppermute | solution.py:17
  34.5 1.3 %collective-permute-start.18 = (f16[256,128]{1,0:T(8,128)(2,1)S(1)}, f16[256,128]{1,0:T(8,128)(2,1)S(1)}, u32[]{:S(2)}, u32[]{:S(2)}) collective-permute-start(f16[256,128]{1,0:T(8,128)(2,1)S(1)} %multiply_convert_fusion.1), channel_id=1, source_target_pairs={{0,1},{1,0},{2,3},{3,2},{4,5},{5,4},{6,7},{7,6},{8,9},{9,8},{10,11... | collective-permute-start | bytes 196616 | tf_op jit(solution)/shard_map/ppermute | solution.py:17
  35.8 4.3 %collective-permute-start.19 = (f16[256,128]{1,0:T(8,128)(2,1)S(1)}, f16[256,128]{1,0:T(8,128)(2,1)S(1)}, u32[]{:S(2)}, u32[]{:S(2)}) collective-permute-start(f16[256,128]{1,0:T(8,128)(2,1)S(1)} %multiply_convert_fusion), channel_id=1, source_target_pairs={{0,2},{1,3},{2,0},{3,1},{4,6},{5,7},{6,4},{7,5},{8,10},{9,11},{10,... | collective-permute-start | bytes 196616 | tf_op jit(solution)/shard_map/ppermute | solution.py:17
  37.4 2.8 %copy-start.2 = (f32[1,256,256]{2,1,0:T(8,128)S(1)}, f32[1,256,256]{2,1,0:T(8,128)}, u32[]{:S(2)}) copy-start(f32[1,256,256]{2,1,0:T(8,128)} %refs_3_.1) | copy-start | bytes 786436
  37.8 2.4 %copy-start.3 = (f32[256,128]{1,0:T(8,128)S(1)}, f32[256,128]{1,0:T(8,128)}, u32[]{:S(2)}) copy-start(f32[256,128]{1,0:T(8,128)} %refs_4_.1) | copy-start | bytes 393220
  37.8 2.4 %collective-permute-start.17 = (f32[256,128]{1,0:T(8,128)S(1)}, f32[256,128]{1,0:T(8,128)S(1)}, u32[]{:S(2)}, u32[]{:S(2)}) collective-permute-start(f32[256,128]{1,0:T(8,128)S(1)} %get-tuple-element.55), channel_id=1, source_target_pairs={{0,1},{1,0},{2,3},{3,2},{4,5},{5,4},{6,7},{7,6},{8,9},{9,8},{10,11... | collective-permute-start | bytes 393224 | tf_op jit(solution)/shard_map/ppermute | solution.py:17
